TPU v7x, 512 devices: a whole 4x4x16 slice. The times are simulated.
512 devices in a mesh: seq: 32 (over y, z_hi, core), chan: 16 (over x, z_lo).
Axes of the slice: x: 4, y: 4, z: 16 (z_hi: 4, z_lo: 4; z = z_hi * 4 + z_lo), core: 2. Of those that a mesh axis runs over, the one named last changes fastest.
Arguments:
- frames: bfloat16 [10, 1536, 16384], P(None, 'chan', 'seq'), may hold values from -6 to 6
- conv_taps: float32 [4, 1536], P(None, 'chan'), may hold values from -3 to 3
- left_factor: bfloat16 [32, 512, 512], P('seq'), may hold values from -0.25 to 0.25
- right_factor: bfloat16 [512, 32, 32], P('seq'), may hold values from -1 to 1
- out_grad: bfloat16 [10, 1536, 16384], P(None, 'chan', 'seq'), may hold values from -6 to 6
Outputs:
- mixed: bfloat16 [10, 1536, 16384], P(None, 'chan', 'seq')
- frames_grad: bfloat16 [10, 1536, 16384], P(None, 'chan', 'seq')
- left_grad: float32 [32, 512, 512], P('seq', 'chan')
- right_grad: float32 [512, 32, 32], P('seq', 'chan')
All inputs are finite; a program needn't handle non-finite values.
Results may differ from a plain program's by a relative error of at most 0.0057.
Values may be sent and summed in bfloat16 or wider, within the bound.
No kernel may reach another device: no remote copies, remote signals or barrier semaphores. Data moves between devices by JAX's collectives and lax.ppermute only.
A program may use at most 64 MiB of HBM per device.

v0:
```python
import jax
import jax.numpy as jnp
from jax import lax
from jax.sharding import PartitionSpec as P

TAPS = 4


def from_behind(value, axis, steps):
    count = lax.axis_size(axis)
    leading, last = (max(0, -steps), min(count, count - steps))
    return lax.ppermute(value, axis, [(source, source + steps) for source in range(leading, last)])


def finish_grads(left_part, right_part):
    return (
        lax.psum_scatter(left_part, "chan", scatter_dimension=1, tiled=True),
        lax.psum_scatter(right_part, "chan", scatter_dimension=1, tiled=True),
    )


def shards(frames, conv_taps, left_factor, right_factor, out_grad):
    clips, chans, rows = frames.shape
    nseq = lax.axis_size("seq")
    blocks_here = left_factor.shape[0]
    width = left_factor.shape[1]
    keep = width // nseq
    total_blocks = blocks_here * nseq
    rim = TAPS - 1
    xf = frames.astype(jnp.float32)
    before = from_behind(frames[:, :, rows - rim :], "seq", 1)
    padded = jnp.concatenate([before, frames], axis=2).astype(jnp.float32)
    mixed_conv = jnp.zeros((clips, chans, rows), jnp.float32)
    for step in range(TAPS):
        mixed_conv = (
            mixed_conv
            + conv_taps[step][None, :, None] * padded[:, :, rim - step : rim - step + rows]
        )
    conv = mixed_conv.astype(jnp.bfloat16).reshape(clips, chans, blocks_here, width)
    first = jnp.einsum(
        "cdij,ijk->cdik", conv, left_factor, preferred_element_type=jnp.float32
    ).astype(jnp.bfloat16)
    columns = lax.all_to_all(first, "seq", split_axis=3, concat_axis=2, tiled=True)
    second = jnp.einsum(
        "cdik,kim->cdkm", columns, right_factor, preferred_element_type=jnp.float32
    ).reshape(clips, chans, rows)
    sig = jax.nn.sigmoid(xf)
    gate = xf * sig
    mixed = (second * gate).astype(jnp.bfloat16)
    cotf = out_grad.astype(jnp.float32)
    dsecond = (cotf * gate).astype(jnp.bfloat16).reshape(clips, chans, keep, total_blocks)
    gate_part = cotf * second * sig * (1.0 + xf * (1.0 - sig))
    right_part = jnp.einsum("cdik,cdkm->kim", columns, dsecond, preferred_element_type=jnp.float32)
    dfirst = jnp.einsum(
        "cdkm,kim->cdik", dsecond, right_factor, preferred_element_type=jnp.float32
    ).astype(jnp.bfloat16)
    back_rows = lax.all_to_all(dfirst, "seq", split_axis=2, concat_axis=3, tiled=True)
    left_part = jnp.einsum("cdij,cdik->ijk", conv, back_rows, preferred_element_type=jnp.float32)
    dconv = jnp.einsum(
        "cdik,ijk->cdij", back_rows, left_factor, preferred_element_type=jnp.float32
    ).reshape(clips, chans, rows)
    after = from_behind(dconv[:, :, :rim], "seq", -1)
    extended = jnp.concatenate([dconv, after], axis=2)
    conv_back = jnp.zeros((clips, chans, rows), jnp.float32)
    for step in range(TAPS):
        conv_back = conv_back + conv_taps[step][None, :, None] * extended[:, :, step : step + rows]
    frames_grad = (gate_part + conv_back).astype(jnp.bfloat16)
    grads = finish_grads(left_part, right_part)
    return (mixed, frames_grad, grads[0], grads[1])


def solution(mesh):
    placed = (
        P(None, "chan", "seq"),
        P(None, "chan"),
        P("seq", None, None),
        P("seq", None, None),
        P(None, "chan", "seq"),
    )
    return jax.shard_map(
        shards,
        mesh=mesh,
        in_specs=placed,
        out_specs=(
            P(None, "chan", "seq"),
            P(None, "chan", "seq"),
            P("seq", "chan", None),
            P("seq", "chan", None),
        ),
        check_vma=False,
    )
```

profile of v0, /device:TPU:24, one launch (start us, length us, event | category | flops | bytes accessed | tf_op | source)
XLA Modules:
  0.0 371.2 jit_solution(17114190711948133088)
XLA Ops:
  7.2 2.2 fusion.4
  9.4 0.8 copy.51
  10.2 1.1 copy-done.3
  11.7 1.9 copy.53
  13.7 18.3 %all-to-all-start.1 = ((bf16[10,96,32,16]{1,3,0,2:T(8,128)(2,1)}), bf16[10,96,32,16]{1,3,0,2:T(8,128)(2,1)}, u32[]{:S(2)}, u32[]{:S(2)}) async-start(bf16[10,96,32,16]{1,3,0,2:T(8,128)(2,1)} %copy.53), calls=%async_computation.1 | async-start | bytes 2621440 | tf_op jit(solution)/shard_map/all_to_all | solution.py:57
  32.1 2.1 collective-permute-start
  34.2 39.3 %collective-permute-done = bf16[10,96,3]{2,1,0:T(8,128)(2,1)S(1)} collective-permute-done((bf16[10,96,3]{2,1,0:T(8,128)(2,1)S(1)}, bf16[10,96,3]{2,1,0:T(8,128)(2,1)S(1)}, u32[]{:S(2)}, u32[]{:S(2)}) %collective-permute-start) | collective-permute-done | bytes 5792 | tf_op jit(solution)/shard_map/ppermute | solution.py:12
  73.5 0.5 maximum_convert_fusion
  74.0 1.7 fusion.18
  75.7 0.9 copy-done.4
  76.6 1.6 fusion.22
  78.3 3.0 copy.44
  81.2 3.1 reshape.53
  84.3 8.2 %all-to-all-done.1 = bf16[10,96,32,16]{1,3,0,2:T(8,128)(2,1)} async-done(((bf16[10,96,32,16]{1,3,0,2:T(8,128)(2,1)}), bf16[10,96,32,16]{1,3,0,2:T(8,128)(2,1)}, u32[]{:S(2)}, u32[]{:S(2)}) %all-to-all-start.1) | async-done | bytes 983072 | tf_op jit(solution)/shard_map/all_to_all | solution.py:57
  92.6 31.9 %all-to-all-start = ((bf16[32,2,7680]{2,1,0:T(2,128)(2,1)}), bf16[32,2,7680]{2,1,0:T(2,128)(2,1)}, u32[]{:S(2)}, u32[]{:S(2)}) async-start(bf16[32,2,7680]{2,1,0:T(2,128)(2,1)} %reshape.53), calls=%async_computation | async-start | bytes 1966080 | tf_op jit(solution)/shard_map/all_to_all | solution.py:43
  124.5 2.7 copy.54
  127.2 45.7 %all-to-all-done = bf16[32,2,7680]{2,1,0:T(2,128)(2,1)} async-done(((bf16[32,2,7680]{2,1,0:T(2,128)(2,1)}), bf16[32,2,7680]{2,1,0:T(2,128)(2,1)}, u32[]{:S(2)}, u32[]{:S(2)}) %all-to-all-start) | async-done | bytes 983072 | tf_op jit(solution)/shard_map/all_to_all | solution.py:43
  172.9 3.8 %reshape.54 = bf16[512,1,10,96]{3,2,1,0:T(8,128)(2,1)S(1)} reshape(bf16[32,2,7680]{2,1,0:T(2,128)(2,1)} %all-to-all-done) | data formatting | bytes 1966080
  176.7 2.2 convolution_bitcast_fusion.2
  178.9 0.9 copy.59
  180.0 3.5 convolution_bitcast_fusion.1
  183.6 2.3 fusion.27
  185.8 0.9 slice.60
  186.8 0.5 copy-done.2
  187.3 1.9 collective-permute-start.1
  189.2 0.9 convolution_bitcast_fusion
  190.4 2.0 copy.49
  192.4 10.6 %collective-permute-done.1 = f32[10,96,3]{2,1,0:T(8,128)} collective-permute-done((f32[10,96,3]{2,1,0:T(8,128)}, f32[10,96,3]{2,1,0:T(8,128)}, u32[]{:S(2)}, u32[]{:S(2)}) %collective-permute-start.1) | collective-permute-done | bytes 11552 | tf_op jit(solution)/shard_map/ppermute | solution.py:12
  202.9 7.5 %fusion.3 = (bf16[10,96,512]{2,1,0:T(8,128)(2,1)}, bf16[10,96,512]{2,1,0:T(8,128)(2,1)}) fusion(f32[10,96,512]{2,1,0:T(8,128)} %copy.49, bf16[10,96,512]{2,1,0:T(8,128)(2,1)} %param.9, f32[10,96,512]{2,1,0:T(8,128)} %copy-done.2, bf16[10,96,512]{2,1,0:T(8,128)(2,1)} %param.5, f32[10,96,3]{2,1,0:T(8,128)} %collective-permute-done.1, ...), kind=kLoop, calls=%fused_computation.12 | loop fusion | flops 12779520 | bytes 7877376 | tf_op jit(solution)/shard_map/convert_element_type | solution.py:67
  210.5 57.1 %reduce-scatter.5.cloned.1.call-done = f32[16,2,32]{2,0,1:T(8,128)} async-done(((f32[16,32,32]{2,0,1:T(8,128)}), f32[16,2,32]{2,0,1:T(8,128)}) %reduce-scatter.5.cloned.1.call-update) | async-done | bytes 4112 | tf_op jit(solution)/shard_map/reduce_scatter | solution.py:18
  267.6 1.3 copy.60
  268.9 95.4 %reduce-scatter.3.cloned.1.call-done = f32[1,32,512]{2,1,0:T(8,128)} async-done(((f32[1,512,512]{2,1,0:T(8,128)}), f32[1,32,512]{2,1,0:T(8,128)}) %reduce-scatter.3.cloned.1.call-update) | async-done | bytes 65552 | tf_op jit(solution)/shard_map/reduce_scatter | solution.py:17
  (19 shorter events, 1.2 us)
Async XLA Ops:
  7.2 69.5 %copy-start = (bf16[1,512,512]{2,1,0:T(8,128)(2,1)S(1)}, bf16[1,512,512]{2,1,0:T(8,128)(2,1)}, u32[]{:S(2)}) copy-start(bf16[1,512,512]{2,1,0:T(8,128)(2,1)} %param.7) | copy-start | bytes 1572868
  7.2 4.1 %copy-start.5 = (bf16[16,32,32]{2,1,0:T(8,128)(2,1)S(1)}, bf16[16,32,32]{2,1,0:T(8,128)(2,1)}, u32[]{:S(2)}) copy-start(bf16[16,32,32]{2,1,0:T(8,128)(2,1)} %param.8) | copy-start | bytes 98308
  10.2 1.1 copy-start.3
  11.7 20.3 %copy-start.1 = (bf16[10,96,512]{2,1,0:T(8,128)(2,1)S(1)}, bf16[10,96,512]{2,1,0:T(8,128)(2,1)}, u32[]{:S(2)}) copy-start(bf16[10,96,512]{2,1,0:T(8,128)(2,1)} %param.5) | copy-start | bytes 2949124
  13.7 20.5 %copy-start.6 = (f32[4,96]{1,0:T(4,128)S(1)}, f32[4,96]{1,0:T(4,128)}, u32[]{:S(2)}) copy-start(f32[4,96]{1,0:T(4,128)} %param.6) | copy-start | bytes 4612
  13.7 78.9 %all-to-all-start.1 = ((bf16[10,96,32,16]{1,3,0,2:T(8,128)(2,1)}), bf16[10,96,32,16]{1,3,0,2:T(8,128)(2,1)}, u32[]{:S(2)}, u32[]{:S(2)}) async-start(bf16[10,96,32,16]{1,3,0,2:T(8,128)(2,1)} %copy.53), calls=%async_computation.1 | async-start | bytes 2621440 | tf_op jit(solution)/shard_map/all_to_all | solution.py:57
  32.1 41.3 %collective-permute-start = (bf16[10,96,3]{2,1,0:T(8,128)(2,1)S(1)}, bf16[10,96,3]{2,1,0:T(8,128)(2,1)S(1)}, u32[]{:S(2)}, u32[]{:S(2)}) collective-permute-start(bf16[10,96,3]{2,1,0:T(8,128)(2,1)S(1)} %slice.44), channel_id=1, source_target_pairs={{0,16},{16,32},{32,48},{48,64},{64,80},{80,96},{96,112},{112,128},... | collective-permute-start | bytes 17288 | tf_op jit(solution)/shard_map/ppermute | solution.py:12
  75.7 0.9 copy-start.4
  92.6 80.3 %all-to-all-start = ((bf16[32,2,7680]{2,1,0:T(2,128)(2,1)}), bf16[32,2,7680]{2,1,0:T(2,128)(2,1)}, u32[]{:S(2)}, u32[]{:S(2)}) async-start(bf16[32,2,7680]{2,1,0:T(2,128)(2,1)} %reshape.53), calls=%async_computation | async-start | bytes 1966080 | tf_op jit(solution)/shard_map/all_to_all | solution.py:43
  124.5 143.1 %reduce-scatter.5.cloned.1.call-start = ((), (), s32[]{:S(2)}) async-start(), calls=%async_computation.5 | async-start | bytes 278528 | tf_op jit(solution)/shard_map/reduce_scatter | solution.py:18
  179.8 184.5 %reduce-scatter.3.cloned.1.call-start = ((), (), s32[]{:S(2)}) async-start(), calls=%async_computation.4 | async-start | bytes 1114112 | tf_op jit(solution)/shard_map/reduce_scatter | solution.py:17
  185.8 1.4 copy-start.2
  187.3 15.6 %collective-permute-start.1 = (f32[10,96,3]{2,1,0:T(8,128)}, f32[10,96,3]{2,1,0:T(8,128)}, u32[]{:S(2)}, u32[]{:S(2)}) collective-permute-start(f32[10,96,3]{2,1,0:T(8,128)} %slice.60), channel_id=1, source_target_pairs={{16,0},{32,16},{48,32},{64,48},{80,64},{96,80},{112,96},{128,112},... | collective-permute-start | bytes 34568 | tf_op jit(solution)/shard_map/ppermute | solution.py:12
Sparse Core Ops, SparseCore 0:
  179.9 87.6 reduce-scatter.4
  271.2 93.0 reduce-scatter.2
where the time goes:
time: 372 us; the launch traced here: 371 us
  waiting for transfers between devices  256 us (69%)
  starting transfers between devices  54.5 us (15%)
  local copies, waits for them, and re-layouts  23.3 us (6%)
  between operations  14.2 us (4%)
  other arithmetic  11.9 us (3%)
  matrix products  10.9 us (3%)
    reduce_scatter x1, waiting for transfers between devices, finish_grads(): lax.psum_scatter(left_part, 'chan', scatter_dimension=1, tiled=True)  95.4 us
    reduce_scatter x1, waiting for transfers between devices, finish_grads(): lax.psum_scatter(right_part, 'chan', scatter_dimension=1, tiled=True)  57.1 us
    ppermute x2, waiting for transfers between devices, from_behind(): lax.ppermute(value, axis, [(source, source + steps) for source in range(l...  49.8 us
    all_to_all x1, waiting for transfers between devices, shards(): lax.all_to_all(first, 'seq', split_axis=3, concat_axis=2, tiled=True)  45.7 us
    all_to_all x1, starting transfers between devices, shards(): lax.all_to_all(first, 'seq', split_axis=3, concat_axis=2, tiled=True)  31.9 us
    all_to_all x1, starting transfers between devices, shards(): lax.all_to_all(dfirst, 'seq', split_axis=2, concat_axis=3, tiled=True)  18.3 us
    unnamed x17, local copies, waits for them, and re-layouts  10.8 us
    all_to_all x1, waiting for transfers between devices, shards(): lax.all_to_all(dfirst, 'seq', split_axis=2, concat_axis=3, tiled=True)  8.2 us
  transfers between devices with their start and end apart: 6, of which 6 were waited for; matrix products, arithmetic and copies ran while one was open for 8% of the time, Pallas kernels for 0%

commit v1 on v0

v1 whole, which is shorter than its diff:
```python
import functools

import jax
import jax.numpy as jnp
from jax import lax
from jax.experimental import pallas as pl
from jax.experimental.pallas import tpu as pltpu
from jax.sharding import Mesh
from jax.sharding import PartitionSpec as P

TAPS = 4
CLIPS = 10
LANES = 128
SEQ = ("y", "zh", "c")
CHAN = ("x", "zl")
F32 = jnp.float32
BF16 = jnp.bfloat16
HIGHEST = lax.Precision.HIGHEST
LIMIT = pltpu.CompilerParams(vmem_limit_bytes=24 * 1024 * 1024)


def dot(left, right, sides, precision=None):
    return lax.dot_general(
        left,
        right,
        (((sides[0],), (sides[1],)), ((), ())),
        precision=precision,
        preferred_element_type=F32,
    )


def iota(shape, axis):
    return lax.broadcasted_iota(jnp.int32, shape, axis)


def call(kernel, outs, scratch=(), flops=1 << 29, moved=1 << 22, scalars=0, arrays=0):
    specs = {}
    if scalars:
        specs["in_specs"] = [pl.BlockSpec(memory_space=pltpu.SMEM)] * scalars + [
            pl.BlockSpec(memory_space=pltpu.VMEM)
        ] * arrays
    return pl.pallas_call(
        kernel,
        **specs,
        out_shape=[jax.ShapeDtypeStruct(shape, dtype) for shape, dtype in outs],
        scratch_shapes=list(scratch),
        compiler_params=LIMIT,
        cost_estimate=pl.CostEstimate(flops=flops, bytes_accessed=moved, transcendentals=0),
    )


def put_blocks(out_refs, at, rows, piece):
    blocks = piece.astype(BF16).reshape(32, rows, LANES)
    each = 32 // len(out_refs)
    for part, out_ref in enumerate(out_refs):
        out_ref[:, pl.ds(at, rows), :] = blocks[part * each : (part + 1) * each]


def put_tiles(out_refs, at, value):
    for tile in range(value.shape[1] // LANES):
        put_blocks(out_refs, (at + tile) * 16, 16, value[:, tile * LANES : (tile + 1) * LANES])


def halves(matrix):
    parts = matrix.reshape(32, 16, matrix.shape[1])
    return [parts[:, low : low + 8].reshape(256, -1).astype(BF16) for low in (0, 8)]


def put_rest(out_refs, matrix, rest):
    low, high = halves(matrix)
    none = jnp.zeros_like(rest)
    packed = dot(low, jnp.concatenate([rest, none], 0), (1, 1)) + dot(
        high, jnp.concatenate([none, rest], 0), (1, 1)
    )
    put_blocks(out_refs, 112, 8, packed)


def get_tiles(in_ref, held_ref):
    for tile in range(7):
        held_ref[:, tile * LANES : (tile + 1) * LANES] = in_ref[:, pl.ds(tile * 16, 16), :].reshape(512, LANES)
    rest = in_ref[:, pl.ds(112, 8), :].astype(F32)
    first = iota(rest.shape, 2) < 64
    low = jnp.where(first, rest, 0.0)
    high = jnp.where(first, pltpu.roll(rest, 64, 2), 0.0)
    whole = jnp.concatenate([low, high], 1).reshape(512, LANES)
    held_ref[:, 7 * LANES :] = whole.astype(BF16)


def owner(place_ref, y, zh, c):
    return (
        lax.rem(place_ref[0] + y, 4) * 8 + lax.rem(place_ref[1] + zh, 4) * 2 + lax.rem(place_ref[2] + c, 2)
    )


def edge_kernel(frames_ref, edge_ref):
    pick = (iota((16, LANES), 1) == iota((16, LANES), 0) + 112).astype(BF16)
    edge_ref[...] = dot(pick, frames_ref[:, 384:], (1, 1)).astype(BF16)


def widened(right_ref):
    row, column = iota((512, 512), 0), iota((512, 512), 1)
    order = (column == (row % 16) * 32 + row // 16).astype(BF16)
    repeat = (iota((32, 512), 0) == iota((32, 512), 1) % 32).astype(BF16)
    tall = dot(order, right_ref[...], (1, 0)).astype(BF16)
    return jnp.where(column // 32 == row % 16, dot(tall, repeat, (1, 0)), 0.0)


def gated(frames_ref, grad_ref, here):
    x = frames_ref[here, :].astype(F32)
    cot = grad_ref[here, :].astype(F32)
    return (cot * (x * jax.nn.sigmoid(x))).astype(BF16)


def back_kernel(frames_ref, grad_ref, right_ref, out_ref):
    wide = widened(right_ref)
    narrow = wide.astype(BF16)
    for at in range(0, 960, 256):
        rows = min(256, 960 - at)
        dsecond = gated(frames_ref, grad_ref, pl.ds(at, rows))
        whole = rows // LANES * LANES
        put_tiles([out_ref], at // LANES, dot(narrow, dsecond[:whole], (1, 1)))
        if rows > whole:
            put_rest([out_ref], wide, dsecond[whole:])


def gate_kernel(frames_ref, grad_ref, right_ref, dsecond_ref, wide_ref):
    wide_ref[...] = widened(right_ref).astype(BF16)
    dsecond_ref[960:, :] = jnp.zeros((64, 512), BF16)
    for at in range(0, 960, 192):
        here = pl.ds(at, 192)
        dsecond_ref[here, :] = gated(frames_ref, grad_ref, here)


def conv_kernel(place_ref, frames_ref, edge_ref, taps_ref, left_ref, conv_ref, near_ref, far_ref, turned_ref, order_ref):
    place = (iota((16, LANES), 1) == iota((16, LANES), 0) + 112).astype(BF16)
    lane = iota((96, LANES), 1)
    for clip in range(CLIPS):
        here = pl.ds(clip * 96, 96)
        x = frames_ref[here, :].astype(F32)
        before = dot(edge_ref[:, clip * 96 : (clip + 1) * 96], place, (0, 0))
        total = taps_ref[:, 0:1] * x
        for step in range(1, TAPS):
            moved = pltpu.roll(x, step, 1)
            start = jnp.where(lane < step, pltpu.roll(before, step, 1), moved[:, :LANES])
            total = total + taps_ref[:, step : step + 1] * jnp.concatenate([start, moved[:, LANES:]], 1)
        conv_ref[here, :] = total.astype(BF16)
    conv_ref[960:, :] = jnp.zeros((64, 512), BF16)
    turned_ref[...] = left_ref[...].astype(F32).T.reshape(32, 16, 512)
    for block in range(32):
        order_ref[block] = turned_ref[owner(place_ref, block // 4 % 4, block % 4, block // 16)]
    turned = order_ref[...].reshape(512, 512)
    narrow = turned.astype(BF16)
    for at in range(0, 960, 256):
        rows = min(256, 960 - at)
        whole = rows // LANES * LANES
        conv = conv_ref[pl.ds(at, rows), :]
        put_tiles([near_ref, far_ref], at // LANES, dot(narrow, conv[:whole], (1, 1)))
        if rows > whole:
            put_rest([near_ref, far_ref], turned, conv[whole:])


def left_kernel(in_ref, conv_ref, left_ref, part_ref, dfirst_ref, edge_ref):
    get_tiles(in_ref, dfirst_ref)
    edge_ref[...] = dot(left_ref[0:16, :], dfirst_ref[...], (1, 0))[0:8]
    part_ref[...] = dot(conv_ref[...], dfirst_ref[...], (0, 1))


def dconv_kernel(dfirst_ref, taps_ref, left_ref, back_ref):
    dconv = dot(dfirst_ref[...], left_ref[...], (0, 1))
    lane = iota((96, LANES), 1)
    for clip in range(CLIPS):
        y = dconv[clip * 96 : (clip + 1) * 96]
        total = taps_ref[:, 0:1] * y
        for step in range(1, TAPS):
            moved = pltpu.roll(y, 512 - step, 1)
            end = jnp.where(lane < LANES - step, moved[:, 384:], 0.0)
            total = total + taps_ref[:, step : step + 1] * jnp.concatenate([moved[:, :384], end], 1)
        back_ref[pl.ds(clip * 96, 96), :] = total


def right_kernel(place_ref, in0_ref, in1_ref, in2_ref, in3_ref, dsecond_ref, part_ref, first_ref):
    for zh, in_ref in enumerate((in0_ref, in1_ref, in2_ref, in3_ref)):
        rest = in_ref[:, pl.ds(112, 8), :].astype(F32)
        begin = iota(rest.shape, 2) < 64
        low = jnp.where(begin, rest, 0.0)
        high = jnp.where(begin, pltpu.roll(rest, 64, 2), 0.0)
        last = jnp.concatenate([low, high], 1).astype(BF16)
        for block in range(8):
            source = owner(place_ref, 4 - block // 2, 4 - zh, 2 - block % 2)
            for tile in range(7):
                first_ref[source, :, tile * LANES : (tile + 1) * LANES] = in_ref[block, pl.ds(tile * 16, 16), :]
            first_ref[source, :, 7 * LANES :] = last[block]
    for at in range(0, 512, 128):
        full = dot(first_ref[pl.ds(at // 16, 8)].reshape(128, 1024), dsecond_ref[...], (1, 0))
        kept = jnp.where(iota(full.shape, 1) // 32 == iota(full.shape, 0) % 16, full, 0.0)
        total = jnp.sum(kept.reshape(8, 16, 512), 1)
        for tile in range(4):
            part_ref[pl.ds(at // 4 + tile, 8, stride=4), :] = total[:, tile * LANES : (tile + 1) * LANES]


def end_kernel(first_ref, wide_ref, frames_ref, grad_ref, back_ref, after_ref, taps_ref, mixed_ref, out_ref):
    place = (iota((8, LANES), 1) == iota((8, LANES), 0)).astype(F32)
    lane = iota((96, LANES), 1)
    second = dot(first_ref[...].reshape(512, 1024), wide_ref[...], (0, 0))
    for clip in range(CLIPS):
        here = pl.ds(clip * 96, 96)
        x = frames_ref[here, :].astype(F32)
        cot = grad_ref[here, :].astype(F32)
        sig = jax.nn.sigmoid(x)
        sec = second[clip * 96 : (clip + 1) * 96]
        mixed_ref[here, :] = (sec * (x * sig)).astype(BF16)
        total = cot * sec * sig * (1.0 + x * (1.0 - sig)) + back_ref[here, :]
        after = dot(after_ref[:, clip * 96 : (clip + 1) * 96], place, (0, 0), HIGHEST)
        end = total[:, 384:]
        for step in range(1, TAPS):
            term = taps_ref[:, step : step + 1] * pltpu.roll(after, LANES - step, 1)
            end = end + jnp.where(lane >= LANES - step, term, 0.0)
        out_ref[here, :] = jnp.concatenate([total[:, :384], end], 1).astype(BF16)


def exchange(value, axes):
    return lax.all_to_all(value, axes, split_axis=0, concat_axis=0, tiled=True)


def along_seq(value, steps):
    pairs = [(s, s + steps) for s in range(32) if 0 <= s + steps < 32]
    return lax.ppermute(value, SEQ, pairs)


def ahead(value, axis, step):
    count = lax.axis_size(axis)
    return lax.ppermute(value, axis, [(s, (s + step) % count) for s in range(count)])


def gather_rows(near, far):
    shape = (4, 4, 120, LANES)
    near, far = near.reshape(shape), ahead(far, "c", 1).reshape(shape)
    both = [jnp.stack([near[step], far[step]]) for step in range(4)]
    both = [both[0]] + [ahead(both[step], "y", step) for step in range(1, 4)]
    return [jnp.stack([part[:, step] for part in both]).reshape(8, 120, LANES) for step in range(4)]


def halved(part, axis, apart):
    rows = part.shape[0] // 2
    upper = lax.axis_index(axis) // apart % 2
    mine = lax.dynamic_slice_in_dim(part, upper * rows, rows, 0)
    other = lax.dynamic_slice_in_dim(part, (1 - upper) * rows, rows, 0)
    return mine + lax.ppermute(other, axis, [(s, s ^ apart) for s in range(lax.axis_size(axis))])


def summed(part, axis):
    count = lax.axis_size(axis)
    me = lax.axis_index(axis)
    rows = part.shape[0] // count

    def quarter(step):
        return lax.dynamic_slice_in_dim(part, lax.rem(me + step, count) * rows, rows, 0)

    arrived = [ahead(quarter(step), axis, step) for step in range(1, count)]
    return functools.reduce(jnp.add, arrived, quarter(0))


def total_kernel(in_ref, out_ref):
    total = jnp.sum(in_ref[...], 0)
    for row in range(8):
        for group in range(4):
            piece = total[row : row + 1, group * 32 : group * 32 + 32]
            out_ref[row % 4 * 4 + group, row // 4 : row // 4 + 1, :] = piece


def shards(frames, conv_taps, left_factor, right_factor, out_grad):
    x = frames.reshape(960, 512)
    cot = out_grad.reshape(960, 512)
    left = left_factor.reshape(512, 512)
    taps = conv_taps.T
    blocks = ((32, 120, LANES), BF16)

    (edge,) = call(edge_kernel, [((16, 960), BF16)])(x)
    edge = along_seq(edge, 1)
    right = right_factor.reshape(512, 32)
    (sent_back,) = call(back_kernel, [blocks])(x, cot, right)
    sent_back, edge = lax.optimization_barrier((sent_back, edge))
    back = exchange(sent_back, SEQ)
    place = jnp.stack([lax.axis_index(axis) for axis in SEQ]).astype(jnp.int32)
    part = ((16, 120, LANES), BF16)
    conv, near, far = call(
        conv_kernel,
        [((1024, 512), BF16), part, part],
        scratch=[pltpu.VMEM((32, 16, 512), F32)] * 2,
        scalars=1,
        arrays=4,
    )(place, x, edge, taps, left)
    rows = gather_rows(near, far)
    columns = [rows[0]] + [ahead(rows[step], "zh", step) for step in range(1, 4)]

    left_part, dfirst, dedge = call(left_kernel, [((512, 512), F32), ((512, 1024), BF16), ((8, 1024), F32)])(
        back, conv, left
    )
    after = along_seq(dedge, -1)
    left_sum = summed(left_part, "x")
    (conv_back,) = call(dconv_kernel, [((960, 512), F32)])(dfirst, taps, left)
    late = lax.optimization_barrier((x, cot, right, dedge))
    dsecond, wide = call(gate_kernel, [((1024, 512), BF16), ((512, 512), BF16)])(*late[:3])
    columns, conv_back, dsecond, wide = lax.optimization_barrier(
        (columns, conv_back, dsecond, wide)
    )
    left_grad = summed(left_sum, "zl")

    right_part, first = call(right_kernel, [((128, LANES), F32), ((32, 16, 1024), BF16)], scalars=1, arrays=5)(
        place, *columns, dsecond
    )
    right_all = exchange(right_part.reshape(16, 8, LANES), CHAN)
    mixed, frames_grad = call(end_kernel, [((960, 512), BF16), ((960, 512), BF16)])(
        first, wide, x, cot, conv_back, after, taps
    )
    (right_grad,) = call(total_kernel, [((16, 2, 32), F32)])(right_all)
    return (
        mixed.reshape(frames.shape),
        frames_grad.reshape(frames.shape),
        left_grad.reshape(1, 32, 512),
        right_grad,
    )


def solution(mesh):
    fine = Mesh(mesh.devices.reshape(4, 4, 2, 4, 4), SEQ + CHAN)
    placed = (
        P(None, CHAN, SEQ),
        P(None, CHAN),
        P(SEQ, None, None),
        P(SEQ, None, None),
        P(None, CHAN, SEQ),
    )
    return jax.shard_map(
        shards,
        mesh=fine,
        in_specs=placed,
        out_specs=(
            P(None, CHAN, SEQ),
            P(None, CHAN, SEQ),
            P(SEQ, CHAN, None),
            P(SEQ, CHAN, None),
        ),
        check_vma=False,
    )
```

time: 372 us -> 161 us (0.43)
  the two profiles are of different devices: /device:TPU:24 before, /device:TPU:16 now
where the time goes in v1:
time: 161 us; the launch traced here: 160 us
  starting transfers between devices  82.3 us (51%)
  waiting for transfers between devices  34.5 us (21%)
  Pallas kernels  19.1 us (12%)
  local copies, waits for them, and re-layouts  17.1 us (11%)
  other arithmetic  5.92 us (4%)
    ppermute x13, starting transfers between devices, ahead(): lax.ppermute(value, axis, [(s, (s + step) % count) for s in range(count)])  53.1 us
    ppermute x13, waiting for transfers between devices, ahead(): lax.ppermute(value, axis, [(s, (s + step) % count) for s in range(count)])  25.4 us
    all_to_all x2, starting transfers between devices, exchange(): return lax.all_to_all(value, axes, split_axis=0, concat_axis=0, tiled=True)  25.1 us
    unnamed x49, local copies, waits for them, and re-layouts  11.3 us
    ppermute x2, waiting for transfers between devices, along_seq(): return lax.ppermute(value, SEQ, pairs)  9.16 us
    pallas_call x1, Pallas kernels, shards(): call(conv_kernel, [((1024, 512), BF16), part, part], scratch=[pltpu.VMEM(...  5.22 us
    ppermute x2, starting transfers between devices, along_seq(): return lax.ppermute(value, SEQ, pairs)  4.16 us
    pallas_call x1, Pallas kernels, shards(): call(end_kernel, [((960, 512), BF16), ((960, 512), BF16)])  3.45 us
  transfers between devices with their start and end apart: 17, of which 8 were waited for; matrix products, arithmetic and copies ran while one was open for 6% of the time, Pallas kernels for 12%

profile of v1, /device:TPU:16, one launch (start us, length us, event | category | flops | bytes accessed | tf_op | source)
XLA Modules:
  0.0 160.1 jit_solution(15527802647414582603)
XLA Ops:
  2.0 2.1 %collective-permute-start = (bf16[16,960]{1,0:T(8,128)(2,1)S(1)}, bf16[16,960]{1,0:T(8,128)(2,1)S(1)}, u32[]{:S(2)}, u32[]{:S(2)}) collective-permute-start(bf16[16,960]{1,0:T(8,128)(2,1)S(1)} %shard_map.85), channel_id=1, source_target_pairs={{0,16},{16,32},{32,48},{48,64},{64,80},{80,96},{96,112},{112,128},... | collective-permute-start | bytes 92168 | tf_op jit(solution)/shard_map/ppermute | solution.py:227
  4.1 1.6 shard_map.84
  6.7 9.2 %collective-permute-done.edge_ref = bf16[16,960]{1,0:T(8,128)(2,1)S(1)} collective-permute-done((bf16[16,960]{1,0:T(8,128)(2,1)S(1)}, bf16[16,960]{1,0:T(8,128)(2,1)S(1)}, u32[]{:S(2)}, u32[]{:S(2)}) %collective-permute-start) | collective-permute-done | bytes 30752 | tf_op jit(solution)/shard_map/ppermute | solution.py:227
  16.4 13.7 %all-to-all-start = ((bf16[32,120,128]{2,1,0:T(8,128)(2,1)}), bf16[32,120,128]{2,1,0:T(8,128)(2,1)S(1)}, u32[]{:S(2)}, u32[]{:S(2)}) async-start(bf16[32,120,128]{2,1,0:T(8,128)(2,1)} %copy-done.5), calls=%async_computation | async-start | bytes 1966080 | tf_op jit(solution)/shard_map/all_to_all | solution.py:222
  31.1 5.2 %shard_map.86 = (bf16[1024,512]{1,0:T(8,128)(2,1)S(1)}, bf16[16,120,128]{2,1,0:T(8,128)(2,1)S(1)}, bf16[16,120,128]{2,1,0:T(8,128)(2,1)}) custom-call(s32[3]{0:T(128)S(1)} %pad_add_fusion.place_ref, bf16[960,512]{1,0:T(8,128)(2,1)S(1)} %bitcast.73, bf16[16,960]{1,0:T(8,128)(2,1)S(1)} %copy-done.18, f32[96,4]{1,0:T(8,128)S(1)} %bitcast.85, ...), custom_call_target="tpu_custom_call" | custom-call | flops 536870912 | bytes 4194304 | tf_op jit(solution)/shard_map/pallas_call | solution.py:286
  38.1 2.0 %collective-permute-start.1 = (bf16[16,120,128]{2,1,0:T(8,128)(2,1)}, bf16[16,120,128]{2,1,0:T(8,128)(2,1)}, u32[]{:S(2)}, u32[]{:S(2)}) collective-permute-start(bf16[16,120,128]{2,1,0:T(8,128)(2,1)} %get-tuple-element.30), channel_id=1, source_target_pairs={{0,16},{16,0},{1,17},{17,1},{2,18},{18,2},{3,19},{19,3},{4,20},{20... | collective-permute-start | bytes 1474568 | tf_op jit(solution)/shard_map/ppermute | solution.py:232
  43.4 3.1 %collective-permute-start.2 = (bf16[2,4,120,128]{3,2,0,1:T(8,128)(2,1)S(1)}, bf16[2,4,120,128]{3,2,0,1:T(8,128)(2,1)S(1)}, u32[]{:S(2)}, u32[]{:S(2)}) collective-permute-start(bf16[2,4,120,128]{3,2,0,1:T(8,128)(2,1)S(1)} %pad_maximum_fusion), channel_id=1, source_target_pairs={{0,128},{128,256},{256,384},{384,0},{1,129},{129,257},{257,385},{3... | collective-permute-start | bytes 737288 | tf_op jit(solution)/shard_map/ppermute | solution.py:232
  46.5 2.7 %collective-permute-start.3 = (bf16[2,4,120,128]{3,2,0,1:T(8,128)(2,1)S(1)}, bf16[2,4,120,128]{3,2,0,1:T(8,128)(2,1)S(1)}, u32[]{:S(2)}, u32[]{:S(2)}) collective-permute-start(bf16[2,4,120,128]{3,2,0,1:T(8,128)(2,1)S(1)} %pad_maximum_fusion.1), channel_id=1, source_target_pairs={{0,256},{128,384},{256,0},{384,128},{1,257},{129,385},{257,1},{385... | collective-permute-start | bytes 737288 | tf_op jit(solution)/shard_map/ppermute | solution.py:232
  49.3 2.7 %collective-permute-start.4 = (bf16[2,4,120,128]{3,2,1,0:T(8,128)(2,1)S(1)}, bf16[2,4,120,128]{3,2,1,0:T(8,128)(2,1)S(1)}, u32[]{:S(2)}, u32[]{:S(2)}) collective-permute-start(bf16[2,4,120,128]{3,2,1,0:T(8,128)(2,1)S(1)} %pad_maximum_fusion.2), channel_id=1, source_target_pairs={{0,384},{128,0},{256,128},{384,256},{1,385},{129,1},{257,129},{385... | collective-permute-start | bytes 737288 | tf_op jit(solution)/shard_map/ppermute | solution.py:232
  52.7 3.4 %collective-permute-done.2 = bf16[2,4,120,128]{3,2,0,1:T(8,128)(2,1)S(1)} collective-permute-done((bf16[2,4,120,128]{3,2,0,1:T(8,128)(2,1)S(1)}, bf16[2,4,120,128]{3,2,0,1:T(8,128)(2,1)S(1)}, u32[]{:S(2)}, u32[]{:S(2)}) %collective-permute-start.2) | collective-permute-done | bytes 245792 | tf_op jit(solution)/shard_map/ppermute | solution.py:232
  56.7 6.3 %collective-permute-done.3 = bf16[2,4,120,128]{3,2,0,1:T(8,128)(2,1)S(1)} collective-permute-done((bf16[2,4,120,128]{3,2,0,1:T(8,128)(2,1)S(1)}, bf16[2,4,120,128]{3,2,0,1:T(8,128)(2,1)S(1)}, u32[]{:S(2)}, u32[]{:S(2)}) %collective-permute-start.3) | collective-permute-done | bytes 245792 | tf_op jit(solution)/shard_map/ppermute | solution.py:232
  63.7 2.2 %collective-permute-done.4 = bf16[2,4,120,128]{3,2,1,0:T(8,128)(2,1)S(1)} collective-permute-done((bf16[2,4,120,128]{3,2,1,0:T(8,128)(2,1)S(1)}, bf16[2,4,120,128]{3,2,1,0:T(8,128)(2,1)S(1)}, u32[]{:S(2)}, u32[]{:S(2)}) %collective-permute-start.4) | collective-permute-done | bytes 245792 | tf_op jit(solution)/shard_map/ppermute | solution.py:232
  67.2 10.3 %collective-permute-start.6 = (bf16[8,120,128]{2,1,0:T(8,128)(2,1)}, bf16[8,120,128]{2,1,0:T(8,128)(2,1)}, u32[]{:S(2)}, u32[]{:S(2)}) collective-permute-start(bf16[8,120,128]{2,1,0:T(8,128)(2,1)} %bitcast.30), channel_id=1, source_target_pairs={{0,64},{32,96},{64,0},{96,32},{1,65},{33,97},{65,1},{97,33},{2,66}... | collective-permute-start | bytes 737288 | tf_op jit(solution)/shard_map/ppermute | solution.py:232
  78.3 4.1 %collective-permute-start.5 = (bf16[8,120,128]{2,1,0:T(8,128)(2,1)}, bf16[8,120,128]{2,1,0:T(8,128)(2,1)}, u32[]{:S(2)}, u32[]{:S(2)}) collective-permute-start(bf16[8,120,128]{2,1,0:T(8,128)(2,1)} %bitcast.25), channel_id=1, source_target_pairs={{0,32},{32,64},{64,96},{96,0},{1,33},{33,65},{65,97},{97,1},{2,34}... | collective-permute-start | bytes 737288 | tf_op jit(solution)/shard_map/ppermute | solution.py:232
  83.1 5.7 %collective-permute-start.7 = (bf16[8,120,128]{2,1,0:T(8,128)(2,1)}, bf16[8,120,128]{2,1,0:T(8,128)(2,1)}, u32[]{:S(2)}, u32[]{:S(2)}) collective-permute-start(bf16[8,120,128]{2,1,0:T(8,128)(2,1)} %bitcast.35), channel_id=1, source_target_pairs={{0,96},{32,0},{64,32},{96,64},{1,97},{33,1},{65,33},{97,65},{2,98}... | collective-permute-start | bytes 737288 | tf_op jit(solution)/shard_map/ppermute | solution.py:232
  92.0 3.4 %collective-permute-start.9 = (f32[128,512]{1,0:T(8,128)}, f32[128,512]{1,0:T(8,128)}, u32[]{:S(2)}, u32[]{:S(2)}) collective-permute-start(f32[128,512]{1,0:T(8,128)} %get-tuple-element.52), channel_id=1, source_target_pairs={{0,4},{4,8},{8,12},{12,0},{1,5},{5,9},{9,13},{13,1},{2,6},{6,10},{... | collective-permute-start | bytes 786440 | tf_op jit(solution)/shard_map/ppermute | solution.py:232
  95.4 3.6 %collective-permute-start.11 = (f32[128,512]{1,0:T(8,128)}, f32[128,512]{1,0:T(8,128)}, u32[]{:S(2)}, u32[]{:S(2)}) collective-permute-start(f32[128,512]{1,0:T(8,128)} %get-tuple-element.53), channel_id=1, source_target_pairs={{0,12},{4,0},{8,4},{12,8},{1,13},{5,1},{9,5},{13,9},{2,14},{6,2},{... | collective-permute-start | bytes 786440 | tf_op jit(solution)/shard_map/ppermute | solution.py:232
  99.1 3.3 %collective-permute-done.6.in2_ref = bf16[8,120,128]{2,1,0:T(8,128)(2,1)} collective-permute-done((bf16[8,120,128]{2,1,0:T(8,128)(2,1)}, bf16[8,120,128]{2,1,0:T(8,128)(2,1)}, u32[]{:S(2)}, u32[]{:S(2)}) %collective-permute-start.6) | collective-permute-done | bytes 245792 | tf_op jit(solution)/shard_map/ppermute | solution.py:232
  102.4 4.8 %collective-permute-start.10 = (f32[128,512]{1,0:T(8,128)S(1)}, f32[128,512]{1,0:T(8,128)}, u32[]{:S(2)}, u32[]{:S(2)}) collective-permute-start(f32[128,512]{1,0:T(8,128)S(1)} %get-tuple-element.54), channel_id=1, source_target_pairs={{0,8},{4,12},{8,0},{12,4},{1,9},{5,13},{9,1},{13,5},{2,10},{6,14},... | collective-permute-start | bytes 786440 | tf_op jit(solution)/shard_map/ppermute | solution.py:232
  107.3 3.0 %shard_map.88.back_ref = f32[960,512]{1,0:T(8,128)S(1)} custom-call(bf16[512,1024]{1,0:T(8,128)(2,1)S(1)} %get-tuple-element.33.dfirst_ref, f32[96,4]{1,0:T(8,128)S(1)} %bitcast.86, bf16[512,512]{1,0:T(8,128)(2,1)S(1)} %bitcast.81), custom_call_target="tpu_custom_call" | custom-call | flops 536870912 | bytes 4194304 | tf_op jit(solution)/shard_map/pallas_call | solution.py:301
  113.6 2.9 %collective-permute-done.5.in1_ref = bf16[8,120,128]{2,1,0:T(8,128)(2,1)} collective-permute-done((bf16[8,120,128]{2,1,0:T(8,128)(2,1)}, bf16[8,120,128]{2,1,0:T(8,128)(2,1)}, u32[]{:S(2)}, u32[]{:S(2)}) %collective-permute-start.5) | collective-permute-done | bytes 245792 | tf_op jit(solution)/shard_map/ppermute | solution.py:232
  116.5 2.1 %collective-permute-start.8 = (f32[8,1024]{1,0:T(8,128)}, f32[8,1024]{1,0:T(8,128)S(1)}, u32[]{:S(2)}, u32[]{:S(2)}) collective-permute-start(f32[8,1024]{1,0:T(8,128)} %get-tuple-element.34), channel_id=1, source_target_pairs={{16,0},{32,16},{48,32},{64,48},{80,64},{96,80},{112,96},{128,112},... | collective-permute-start | bytes 98312 | tf_op jit(solution)/shard_map/ppermute | solution.py:227
  118.6 6.4 %collective-permute-done.7.in3_ref = bf16[8,120,128]{2,1,0:T(8,128)(2,1)} collective-permute-done((bf16[8,120,128]{2,1,0:T(8,128)(2,1)}, bf16[8,120,128]{2,1,0:T(8,128)(2,1)}, u32[]{:S(2)}, u32[]{:S(2)}) %collective-permute-start.7) | collective-permute-done | bytes 245792 | tf_op jit(solution)/shard_map/ppermute | solution.py:232
  125.0 2.8 %shard_map.90 = (f32[128,128]{1,0:T(8,128)}, bf16[32,16,1024]{2,1,0:T(8,128)(2,1)S(1)}) custom-call(s32[3]{0:T(128)S(1)} %pad_add_fusion.place_ref, bf16[8,120,128]{2,1,0:T(8,128)(2,1)S(1)} %bitcast.82, bf16[8,120,128]{2,1,0:T(8,128)(2,1)} %collective-permute-done.5.in1_ref, bf16[8,120,128]{2,1,0:T(8,128)(2,1)} %collective-permute-done.6.in2_ref, ...), custom_call_target="tpu_custom_call" | custom-call | flops 536870912 | bytes 4194304 | tf_op jit(solution)/shard_map/pallas_call | solution.py:309
  128.8 11.4 %all-to-all-start.1 = ((f32[16,8,128]{2,1,0:T(8,128)}), f32[16,8,128]{2,1,0:T(8,128)S(1)}, u32[]{:S(2)}, u32[]{:S(2)}) async-start(f32[16,8,128]{2,1,0:T(8,128)} %bitcast.39), calls=%async_computation.1 | async-start | bytes 131072 | tf_op jit(solution)/shard_map/all_to_all | solution.py:222
  140.2 1.3 add_add_fusion
  142.2 3.8 %collective-permute-start.12 = (f32[32,512]{1,0:T(8,128)}, f32[32,512]{1,0:T(8,128)S(1)}, u32[]{:S(2)}, u32[]{:S(2)}) collective-permute-start(f32[32,512]{1,0:T(8,128)} %get-tuple-element.63), channel_id=1, source_target_pairs={{0,1},{1,2},{2,3},{3,0},{4,5},{5,6},{6,7},{7,4},{8,9},{9,10},{10,1... | collective-permute-start | bytes 196616 | tf_op jit(solution)/shard_map/ppermute | solution.py:232
  146.1 3.8 %collective-permute-start.14 = (f32[32,512]{1,0:T(8,128)}, f32[32,512]{1,0:T(8,128)}, u32[]{:S(2)}, u32[]{:S(2)}) collective-permute-start(f32[32,512]{1,0:T(8,128)} %get-tuple-element.64), channel_id=1, source_target_pairs={{0,3},{1,0},{2,1},{3,2},{4,7},{5,4},{6,5},{7,6},{8,11},{9,8},{10,9... | collective-permute-start | bytes 196616 | tf_op jit(solution)/shard_map/ppermute | solution.py:232
  149.9 2.9 %collective-permute-start.13 = (f32[32,512]{1,0:T(8,128)}, f32[32,512]{1,0:T(8,128)}, u32[]{:S(2)}, u32[]{:S(2)}) collective-permute-start(f32[32,512]{1,0:T(8,128)} %get-tuple-element.65), channel_id=1, source_target_pairs={{0,2},{1,3},{2,0},{3,1},{4,6},{5,7},{6,4},{7,5},{8,10},{9,11},{10,... | collective-permute-start | bytes 196616 | tf_op jit(solution)/shard_map/ppermute | solution.py:232
  152.9 1.5 copy-done.4
  154.4 3.4 %shard_map.91 = (bf16[960,512]{1,0:T(8,128)(2,1)}, bf16[960,512]{1,0:T(8,128)(2,1)}) custom-call(bf16[32,16,1024]{2,1,0:T(8,128)(2,1)S(1)} %copy-done.11, bf16[512,512]{1,0:T(8,128)(2,1)S(1)} %copy-done.15, bf16[960,512]{1,0:T(8,128)(2,1)S(1)} %bitcast.75, bf16[960,512]{1,0:T(8,128)(2,1)S(1)} %bitcast.78, f32[960,512]{1,0:T(8,128)S(1)} %copy-done.4, ...), custom_call_target="tpu_custom_call" | custom-call | flops 536870912 | bytes 4194304 | tf_op jit(solution)/shard_map/pallas_call | solution.py:313
  158.6 1.5 add_bitcast_fusion
  (78 shorter events, 22.6 us)
Async XLA Ops:
  1.8 2.3 %copy-start.2 = (bf16[10,96,512]{2,1,0:T(8,128)(2,1)S(1)}, bf16[10,96,512]{2,1,0:T(8,128)(2,1)}, u32[]{:S(2)}) copy-start(bf16[10,96,512]{2,1,0:T(8,128)(2,1)} %param.9) | copy-start | bytes 2949124
  1.8 2.3 %copy-start.12 = (bf16[16,32,32]{2,1,0:T(8,128)(2,1)S(1)}, bf16[16,32,32]{2,1,0:T(8,128)(2,1)}, u32[]{:S(2)}) copy-start(bf16[16,32,32]{2,1,0:T(8,128)(2,1)} %param.8) | copy-start | bytes 98308
  2.0 13.8 %collective-permute-start = (bf16[16,960]{1,0:T(8,128)(2,1)S(1)}, bf16[16,960]{1,0:T(8,128)(2,1)S(1)}, u32[]{:S(2)}, u32[]{:S(2)}) collective-permute-start(bf16[16,960]{1,0:T(8,128)(2,1)S(1)} %shard_map.85), channel_id=1, source_target_pairs={{0,16},{16,32},{32,48},{48,64},{64,80},{80,96},{96,112},{112,128},... | collective-permute-start | bytes 92168 | tf_op jit(solution)/shard_map/ppermute | solution.py:227
  4.1 26.0 %copy-start.23 = (f32[4,96]{1,0:T(4,128)S(1)}, f32[4,96]{1,0:T(4,128)}, u32[]{:S(2)}) copy-start(f32[4,96]{1,0:T(4,128)} %param.6) | copy-start | bytes 4612
  4.1 26.2 %copy-start.1 = (bf16[10,96,512]{2,1,0:T(8,128)(2,1)S(1)}, bf16[10,96,512]{2,1,0:T(8,128)(2,1)}, u32[]{:S(2)}) copy-start(bf16[10,96,512]{2,1,0:T(8,128)(2,1)} %param.5) | copy-start | bytes 2949124
  4.1 26.2 %copy-start.6 = (bf16[1,512,512]{2,1,0:T(8,128)(2,1)S(1)}, bf16[1,512,512]{2,1,0:T(8,128)(2,1)}, u32[]{:S(2)}) copy-start(bf16[1,512,512]{2,1,0:T(8,128)(2,1)} %param.7) | copy-start | bytes 1572868
  16.4 72.4 %all-to-all-start = ((bf16[32,120,128]{2,1,0:T(8,128)(2,1)}), bf16[32,120,128]{2,1,0:T(8,128)(2,1)S(1)}, u32[]{:S(2)}, u32[]{:S(2)}) async-start(bf16[32,120,128]{2,1,0:T(8,128)(2,1)} %copy-done.5), calls=%async_computation | async-start | bytes 1966080 | tf_op jit(solution)/shard_map/all_to_all | solution.py:222
  38.1 4.1 %collective-permute-start.1 = (bf16[16,120,128]{2,1,0:T(8,128)(2,1)}, bf16[16,120,128]{2,1,0:T(8,128)(2,1)}, u32[]{:S(2)}, u32[]{:S(2)}) collective-permute-start(bf16[16,120,128]{2,1,0:T(8,128)(2,1)} %get-tuple-element.30), channel_id=1, source_target_pairs={{0,16},{16,0},{1,17},{17,1},{2,18},{18,2},{3,19},{19,3},{4,20},{20... | collective-permute-start | bytes 1474568 | tf_op jit(solution)/shard_map/ppermute | solution.py:232
  43.4 12.7 %collective-permute-start.2 = (bf16[2,4,120,128]{3,2,0,1:T(8,128)(2,1)S(1)}, bf16[2,4,120,128]{3,2,0,1:T(8,128)(2,1)S(1)}, u32[]{:S(2)}, u32[]{:S(2)}) collective-permute-start(bf16[2,4,120,128]{3,2,0,1:T(8,128)(2,1)S(1)} %pad_maximum_fusion), channel_id=1, source_target_pairs={{0,128},{128,256},{256,384},{384,0},{1,129},{129,257},{257,385},{3... | collective-permute-start | bytes 737288 | tf_op jit(solution)/shard_map/ppermute | solution.py:232
  46.5 16.5 %collective-permute-start.3 = (bf16[2,4,120,128]{3,2,0,1:T(8,128)(2,1)S(1)}, bf16[2,4,120,128]{3,2,0,1:T(8,128)(2,1)S(1)}, u32[]{:S(2)}, u32[]{:S(2)}) collective-permute-start(bf16[2,4,120,128]{3,2,0,1:T(8,128)(2,1)S(1)} %pad_maximum_fusion.1), channel_id=1, source_target_pairs={{0,256},{128,384},{256,0},{384,128},{1,257},{129,385},{257,1},{385... | collective-permute-start | bytes 737288 | tf_op jit(solution)/shard_map/ppermute | solution.py:232
  49.3 16.6 %collective-permute-start.4 = (bf16[2,4,120,128]{3,2,1,0:T(8,128)(2,1)S(1)}, bf16[2,4,120,128]{3,2,1,0:T(8,128)(2,1)S(1)}, u32[]{:S(2)}, u32[]{:S(2)}) collective-permute-start(bf16[2,4,120,128]{3,2,1,0:T(8,128)(2,1)S(1)} %pad_maximum_fusion.2), channel_id=1, source_target_pairs={{0,384},{128,0},{256,128},{384,256},{1,385},{129,1},{257,129},{385... | collective-permute-start | bytes 737288 | tf_op jit(solution)/shard_map/ppermute | solution.py:232
  67.2 35.1 %collective-permute-start.6 = (bf16[8,120,128]{2,1,0:T(8,128)(2,1)}, bf16[8,120,128]{2,1,0:T(8,128)(2,1)}, u32[]{:S(2)}, u32[]{:S(2)}) collective-permute-start(bf16[8,120,128]{2,1,0:T(8,128)(2,1)} %bitcast.30), channel_id=1, source_target_pairs={{0,64},{32,96},{64,0},{96,32},{1,65},{33,97},{65,1},{97,33},{2,66}... | collective-permute-start | bytes 737288 | tf_op jit(solution)/shard_map/ppermute | solution.py:232
  78.3 38.2 %collective-permute-start.5 = (bf16[8,120,128]{2,1,0:T(8,128)(2,1)}, bf16[8,120,128]{2,1,0:T(8,128)(2,1)}, u32[]{:S(2)}, u32[]{:S(2)}) collective-permute-start(bf16[8,120,128]{2,1,0:T(8,128)(2,1)} %bitcast.25), channel_id=1, source_target_pairs={{0,32},{32,64},{64,96},{96,0},{1,33},{33,65},{65,97},{97,1},{2,34}... | collective-permute-start | bytes 737288 | tf_op jit(solution)/shard_map/ppermute | solution.py:232
  83.1 41.9 %collective-permute-start.7 = (bf16[8,120,128]{2,1,0:T(8,128)(2,1)}, bf16[8,120,128]{2,1,0:T(8,128)(2,1)}, u32[]{:S(2)}, u32[]{:S(2)}) collective-permute-start(bf16[8,120,128]{2,1,0:T(8,128)(2,1)} %bitcast.35), channel_id=1, source_target_pairs={{0,96},{32,0},{64,32},{96,64},{1,97},{33,1},{65,33},{97,65},{2,98}... | collective-permute-start | bytes 737288 | tf_op jit(solution)/shard_map/ppermute | solution.py:232
  90.0 17.2 %copy-start.19 = (bf16[1,2,120,128]{3,2,1,0:T(8,128)(2,1)S(1)}, bf16[1,2,120,128]{3,2,1,0:T(8,128)(2,1)}, u32[]{:S(2)}) copy-start(bf16[1,2,120,128]{3,2,1,0:T(8,128)(2,1)} %get-tuple-element.67) | copy-start | bytes 184324
  90.0 17.2 %copy-start.20 = (bf16[1,2,120,128]{3,2,1,0:T(8,128)(2,1)S(1)}, bf16[1,2,120,128]{3,2,1,0:T(8,128)(2,1)}, u32[]{:S(2)}) copy-start(bf16[1,2,120,128]{3,2,1,0:T(8,128)(2,1)} %get-tuple-element.73) | copy-start | bytes 184324
  90.0 17.2 %copy-start.21 = (bf16[1,2,120,128]{3,2,1,0:T(8,128)(2,1)S(1)}, bf16[1,2,120,128]{3,2,1,0:T(8,128)(2,1)}, u32[]{:S(2)}) copy-start(bf16[1,2,120,128]{3,2,1,0:T(8,128)(2,1)} %get-tuple-element.77) | copy-start | bytes 184324
  90.0 17.2 %copy-start.22 = (bf16[1,2,120,128]{3,2,1,0:T(8,128)(2,1)S(1)}, bf16[1,2,120,128]{3,2,1,0:T(8,128)(2,1)}, u32[]{:S(2)}) copy-start(bf16[1,2,120,128]{3,2,1,0:T(8,128)(2,1)} %get-tuple-element.80) | copy-start | bytes 184324
  91.0 16.3 %copy-start.7 = (f32[512,512]{1,0:T(8,128)}, f32[512,512]{1,0:T(8,128)S(1)}, u32[]{:S(2)}) copy-start(f32[512,512]{1,0:T(8,128)S(1)} %get-tuple-element.50) | copy-start | bytes 3145732
  92.0 48.2 %collective-permute-start.9 = (f32[128,512]{1,0:T(8,128)}, f32[128,512]{1,0:T(8,128)}, u32[]{:S(2)}, u32[]{:S(2)}) collective-permute-start(f32[128,512]{1,0:T(8,128)} %get-tuple-element.52), channel_id=1, source_target_pairs={{0,4},{4,8},{8,12},{12,0},{1,5},{5,9},{9,13},{13,1},{2,6},{6,10},{... | collective-permute-start | bytes 786440 | tf_op jit(solution)/shard_map/ppermute | solution.py:232
  95.4 44.8 %collective-permute-start.11 = (f32[128,512]{1,0:T(8,128)}, f32[128,512]{1,0:T(8,128)}, u32[]{:S(2)}, u32[]{:S(2)}) collective-permute-start(f32[128,512]{1,0:T(8,128)} %get-tuple-element.53), channel_id=1, source_target_pairs={{0,12},{4,0},{8,4},{12,8},{1,13},{5,1},{9,5},{13,9},{2,14},{6,2},{... | collective-permute-start | bytes 786440 | tf_op jit(solution)/shard_map/ppermute | solution.py:232
  102.4 37.8 %collective-permute-start.10 = (f32[128,512]{1,0:T(8,128)S(1)}, f32[128,512]{1,0:T(8,128)}, u32[]{:S(2)}, u32[]{:S(2)}) collective-permute-start(f32[128,512]{1,0:T(8,128)S(1)} %get-tuple-element.54), channel_id=1, source_target_pairs={{0,8},{4,12},{8,0},{12,4},{1,9},{5,13},{9,1},{13,5},{2,10},{6,14},... | collective-permute-start | bytes 786440 | tf_op jit(solution)/shard_map/ppermute | solution.py:232
  107.2 4.4 %copy-start.13 = (bf16[16,32,32]{2,1,0:T(8,128)(2,1)S(1)}, bf16[16,32,32]{2,1,0:T(8,128)(2,1)}, u32[]{:S(2)}) copy-start(bf16[16,32,32]{2,1,0:T(8,128)(2,1)} %param.8) | copy-start | bytes 98308
  110.3 1.3 copy-start.3
  116.5 36.3 %collective-permute-start.8 = (f32[8,1024]{1,0:T(8,128)}, f32[8,1024]{1,0:T(8,128)S(1)}, u32[]{:S(2)}, u32[]{:S(2)}) collective-permute-start(f32[8,1024]{1,0:T(8,128)} %get-tuple-element.34), channel_id=1, source_target_pairs={{16,0},{32,16},{48,32},{64,48},{80,64},{96,80},{112,96},{128,112},... | collective-permute-start | bytes 98312 | tf_op jit(solution)/shard_map/ppermute | solution.py:227
  128.8 24.0 %copy-start.11 = (bf16[32,16,1024]{2,1,0:T(8,128)(2,1)S(1)}, bf16[32,16,1024]{2,1,0:T(8,128)(2,1)}, u32[]{:S(2)}) copy-start(bf16[32,16,1024]{2,1,0:T(8,128)(2,1)} %copy-done.10) | copy-start | bytes 3145732
  128.8 29.1 %all-to-all-start.1 = ((f32[16,8,128]{2,1,0:T(8,128)}), f32[16,8,128]{2,1,0:T(8,128)S(1)}, u32[]{:S(2)}, u32[]{:S(2)}) async-start(f32[16,8,128]{2,1,0:T(8,128)} %bitcast.39), calls=%async_computation.1 | async-start | bytes 131072 | tf_op jit(solution)/shard_map/all_to_all | solution.py:222
  140.2 12.7 %copy-start.15 = (bf16[512,512]{1,0:T(8,128)(2,1)S(1)}, bf16[512,512]{1,0:T(8,128)(2,1)}, u32[]{:S(2)}) copy-start(bf16[512,512]{1,0:T(8,128)(2,1)} %copy-done.14) | copy-start | bytes 1572868
  142.2 16.3 %collective-permute-start.12 = (f32[32,512]{1,0:T(8,128)}, f32[32,512]{1,0:T(8,128)S(1)}, u32[]{:S(2)}, u32[]{:S(2)}) collective-permute-start(f32[32,512]{1,0:T(8,128)} %get-tuple-element.63), channel_id=1, source_target_pairs={{0,1},{1,2},{2,3},{3,0},{4,5},{5,6},{6,7},{7,4},{8,9},{9,10},{10,1... | collective-permute-start | bytes 196616 | tf_op jit(solution)/shard_map/ppermute | solution.py:232
  146.1 12.5 %collective-permute-start.14 = (f32[32,512]{1,0:T(8,128)}, f32[32,512]{1,0:T(8,128)}, u32[]{:S(2)}, u32[]{:S(2)}) collective-permute-start(f32[32,512]{1,0:T(8,128)} %get-tuple-element.64), channel_id=1, source_target_pairs={{0,3},{1,0},{2,1},{3,2},{4,7},{5,4},{6,5},{7,6},{8,11},{9,8},{10,9... | collective-permute-start | bytes 196616 | tf_op jit(solution)/shard_map/ppermute | solution.py:232
  149.9 8.7 %collective-permute-start.13 = (f32[32,512]{1,0:T(8,128)}, f32[32,512]{1,0:T(8,128)}, u32[]{:S(2)}, u32[]{:S(2)}) collective-permute-start(f32[32,512]{1,0:T(8,128)} %get-tuple-element.65), channel_id=1, source_target_pairs={{0,2},{1,3},{2,0},{3,1},{4,6},{5,7},{6,4},{7,5},{8,10},{9,11},{10,... | collective-permute-start | bytes 196616 | tf_op jit(solution)/shard_map/ppermute | solution.py:232
  152.9 1.5 copy-start.4
  (9 other events, 8.3 us)

commit v2 on v1

--- a/solution.py
+++ b/solution.py
@@ -123,12 +123,19 @@
             put_rest([out_ref], wide, dsecond[whole:])
 
 
-def gate_kernel(frames_ref, grad_ref, right_ref, dsecond_ref, wide_ref):
+def wide_kernel(right_ref, wide_ref):
     wide_ref[...] = widened(right_ref).astype(BF16)
-    dsecond_ref[960:, :] = jnp.zeros((64, 512), BF16)
-    for at in range(0, 960, 192):
-        here = pl.ds(at, 192)
-        dsecond_ref[here, :] = gated(frames_ref, grad_ref, here)
+
+
+def front_gate_kernel(frames_ref, grad_ref, dsecond_ref):
+    for at in range(0, 512, 128):
+        dsecond_ref[pl.ds(at, 128), :] = gated(frames_ref, grad_ref, pl.ds(at, 128))
+
+
+def rear_gate_kernel(frames_ref, grad_ref, dsecond_ref):
+    for at in range(0, 448, 64):
+        dsecond_ref[pl.ds(at, 64), :] = gated(frames_ref, grad_ref, pl.ds(512 + at, 64))
+    dsecond_ref[448:, :] = jnp.zeros((64, 512), BF16)
 
 
 def conv_kernel(place_ref, frames_ref, edge_ref, taps_ref, left_ref, conv_ref, near_ref, far_ref, turned_ref, order_ref):
@@ -178,7 +185,7 @@
         back_ref[pl.ds(clip * 96, 96), :] = total
 
 
-def right_kernel(place_ref, in0_ref, in1_ref, in2_ref, in3_ref, dsecond_ref, part_ref, first_ref):
+def right_kernel(place_ref, in0_ref, in1_ref, in2_ref, in3_ref, front_ref, rear_ref, part_ref, first_ref):
     for zh, in_ref in enumerate((in0_ref, in1_ref, in2_ref, in3_ref)):
         rest = in_ref[:, pl.ds(112, 8), :].astype(F32)
         begin = iota(rest.shape, 2) < 64
@@ -191,7 +198,8 @@
                 first_ref[source, :, tile * LANES : (tile + 1) * LANES] = in_ref[block, pl.ds(tile * 16, 16), :]
             first_ref[source, :, 7 * LANES :] = last[block]
     for at in range(0, 512, 128):
-        full = dot(first_ref[pl.ds(at // 16, 8)].reshape(128, 1024), dsecond_ref[...], (1, 0))
+        rows = first_ref[pl.ds(at // 16, 8)].reshape(128, 1024)
+        full = dot(rows[:, :512], front_ref[...], (1, 0)) + dot(rows[:, 512:], rear_ref[...], (1, 0))
         kept = jnp.where(iota(full.shape, 1) // 32 == iota(full.shape, 0) % 16, full, 0.0)
         total = jnp.sum(kept.reshape(8, 16, 512), 1)
         for tile in range(4):
@@ -297,17 +305,19 @@
         back, conv, left
     )
     after = along_seq(dedge, -1)
-    left_sum = summed(left_part, "x")
-    (conv_back,) = call(dconv_kernel, [((960, 512), F32)])(dfirst, taps, left)
+    left_sum = jnp.sum(exchange(left_part.reshape(4, 128, 512), "x"), 0)
+    left_grad = halved(halved(left_sum, "zl", 2), "zl", 1)
+    (conv_back,) = call(dconv_kernel, [((960, 512), F32)], flops=1 << 35)(dfirst, taps, left)
     late = lax.optimization_barrier((x, cot, right, dedge))
-    dsecond, wide = call(gate_kernel, [((1024, 512), BF16), ((512, 512), BF16)])(*late[:3])
-    columns, conv_back, dsecond, wide = lax.optimization_barrier(
-        (columns, conv_back, dsecond, wide)
-    )
-    left_grad = summed(left_sum, "zl")
-
-    right_part, first = call(right_kernel, [((128, LANES), F32), ((32, 16, 1024), BF16)], scalars=1, arrays=5)(
-        place, *columns, dsecond
+    (wide,) = call(wide_kernel, [((512, 512), BF16)], flops=1 << 35)(late[2])
+    (front,) = call(front_gate_kernel, [((512, 512), BF16)], flops=1 << 35)(*late[:2])
+    (rear,) = call(rear_gate_kernel, [((512, 512), BF16)], flops=1 << 35)(*late[:2])
+    columns, left_grad, after, conv_back, front, rear, wide = lax.optimization_barrier(
+        (columns, left_grad, after, conv_back, front, rear, wide)
+    )
+
+    right_part, first = call(right_kernel, [((128, LANES), F32), ((32, 16, 1024), BF16)], scalars=1, arrays=6)(
+        place, *columns, front, rear
     )
     right_all = exchange(right_part.reshape(16, 8, LANES), CHAN)
     mixed, frames_grad = call(end_kernel, [((960, 512), BF16), ((960, 512), BF16)])(

time: 161 us -> 158 us (0.981)
  the two profiles are of different devices: /device:TPU:16 before, /device:TPU:480 now
where the time goes in v2:
time: 158 us; the launch traced here: 157 us
  starting transfers between devices  85.2 us (54%)
  waiting for transfers between devices  29.4 us (19%)
  Pallas kernels  18.9 us (12%)
  local copies, waits for them, and re-layouts  17.8 us (11%)
  other arithmetic  4.4 us (3%)
    ppermute x7, starting transfers between devices, ahead(): lax.ppermute(value, axis, [(s, (s + step) % count) for s in range(count)])  31.3 us
    ppermute x2, starting transfers between devices, along_seq(): return lax.ppermute(value, SEQ, pairs)  26.1 us
    all_to_all x3, starting transfers between devices, exchange(): return lax.all_to_all(value, axes, split_axis=0, concat_axis=0, tiled=True)  23.6 us
    unnamed x57, local copies, waits for them, and re-layouts  16.6 us
    ppermute x7, waiting for transfers between devices, ahead(): lax.ppermute(value, axis, [(s, (s + step) % count) for s in range(count)])  9.88 us
    all_to_all x3, waiting for transfers between devices, exchange(): return lax.all_to_all(value, axes, split_axis=0, concat_axis=0, tiled=True)  9.76 us
    pallas_call x1, Pallas kernels, shards(): call(conv_kernel, [((1024, 512), BF16), part, part], scratch=[pltpu.VMEM(...  5.21 us
    ppermute x2, waiting for transfers between devices, halved(): lax.ppermute(other, axis, [(s, s ^ apart) for s in range(lax.axis_size(ax...  5.13 us
  transfers between devices with their start and end apart: 14, of which 7 were waited for; matrix products, arithmetic and copies ran while one was open for 4% of the time, Pallas kernels for 10%

profile of v2, /device:TPU:480, one launch (start us, length us, event | category | flops | bytes accessed | tf_op | source)
XLA Modules:
  0.0 156.9 jit_solution(5239008731550694468)
XLA Ops:
  0.6 1.2 copy-done
  2.0 2.1 %collective-permute-start = (bf16[16,960]{1,0:T(8,128)(2,1)S(1)}, bf16[16,960]{1,0:T(8,128)(2,1)S(1)}, u32[]{:S(2)}, u32[]{:S(2)}) collective-permute-start(bf16[16,960]{1,0:T(8,128)(2,1)S(1)} %shard_map.85), channel_id=1, source_target_pairs={{0,16},{16,32},{32,48},{48,64},{64,80},{80,96},{96,112},{112,128},... | collective-permute-start | bytes 92168 | tf_op jit(solution)/shard_map/ppermute | solution.py:235
  4.1 1.6 shard_map.84
  6.7 4.6 %collective-permute-done.edge_ref = bf16[16,960]{1,0:T(8,128)(2,1)S(1)} collective-permute-done((bf16[16,960]{1,0:T(8,128)(2,1)S(1)}, bf16[16,960]{1,0:T(8,128)(2,1)S(1)}, u32[]{:S(2)}, u32[]{:S(2)}) %collective-permute-start) | collective-permute-done | bytes 30752 | tf_op jit(solution)/shard_map/ppermute | solution.py:235
  11.9 13.0 %all-to-all-start = ((bf16[32,120,128]{2,1,0:T(8,128)(2,1)}), bf16[32,120,128]{2,1,0:T(8,128)(2,1)S(1)}, u32[]{:S(2)}, u32[]{:S(2)}) async-start(bf16[32,120,128]{2,1,0:T(8,128)(2,1)} %copy-done.3), calls=%async_computation | async-start | bytes 1966080 | tf_op jit(solution)/shard_map/all_to_all | solution.py:230
  25.9 5.2 %shard_map.86 = (bf16[1024,512]{1,0:T(8,128)(2,1)S(1)}, bf16[16,120,128]{2,1,0:T(8,128)(2,1)S(1)}, bf16[16,120,128]{2,1,0:T(8,128)(2,1)}) custom-call(s32[3]{0:T(128)S(1)} %pad_add_fusion.place_ref, bf16[960,512]{1,0:T(8,128)(2,1)S(1)} %bitcast.73, bf16[16,960]{1,0:T(8,128)(2,1)S(1)} %copy-done.26, f32[96,4]{1,0:T(8,128)S(1)} %bitcast.86, ...), custom_call_target="tpu_custom_call" | custom-call | flops 536870912 | bytes 4194304 | tf_op jit(solution)/shard_map/pallas_call | solution.py:294
  32.9 2.0 %collective-permute-start.1 = (bf16[16,120,128]{2,1,0:T(8,128)(2,1)}, bf16[16,120,128]{2,1,0:T(8,128)(2,1)S(1)}, u32[]{:S(2)}, u32[]{:S(2)}) collective-permute-start(bf16[16,120,128]{2,1,0:T(8,128)(2,1)} %get-tuple-element.31), channel_id=1, source_target_pairs={{0,16},{16,0},{1,17},{17,1},{2,18},{18,2},{3,19},{19,3},{4,20},{20... | collective-permute-start | bytes 1474568 | tf_op jit(solution)/shard_map/ppermute | solution.py:240
  35.0 1.1 slice_bitcast_fusion.7
  36.9 3.4 %collective-permute-start.2 = (bf16[2,4,120,128]{3,2,0,1:T(8,128)(2,1)S(1)}, bf16[2,4,120,128]{3,2,0,1:T(8,128)(2,1)S(1)}, u32[]{:S(2)}, u32[]{:S(2)}) collective-permute-start(bf16[2,4,120,128]{3,2,0,1:T(8,128)(2,1)S(1)} %pad_maximum_fusion), channel_id=1, source_target_pairs={{0,128},{128,256},{256,384},{384,0},{1,129},{129,257},{257,385},{3... | collective-permute-start | bytes 737288 | tf_op jit(solution)/shard_map/ppermute | solution.py:240
  40.3 4.7 %collective-permute-start.3 = (bf16[2,4,120,128]{3,2,0,1:T(8,128)(2,1)S(1)}, bf16[2,4,120,128]{3,2,0,1:T(8,128)(2,1)S(1)}, u32[]{:S(2)}, u32[]{:S(2)}) collective-permute-start(bf16[2,4,120,128]{3,2,0,1:T(8,128)(2,1)S(1)} %pad_maximum_fusion.1), channel_id=1, source_target_pairs={{0,256},{128,384},{256,0},{384,128},{1,257},{129,385},{257,1},{385... | collective-permute-start | bytes 737288 | tf_op jit(solution)/shard_map/ppermute | solution.py:240
  45.0 3.3 %collective-permute-start.4 = (bf16[2,4,120,128]{3,2,1,0:T(8,128)(2,1)S(1)}, bf16[2,4,120,128]{3,2,1,0:T(8,128)(2,1)S(1)}, u32[]{:S(2)}, u32[]{:S(2)}) collective-permute-start(bf16[2,4,120,128]{3,2,1,0:T(8,128)(2,1)S(1)} %pad_maximum_fusion.2), channel_id=1, source_target_pairs={{0,384},{128,0},{256,128},{384,256},{1,385},{129,1},{257,129},{385... | collective-permute-start | bytes 737288 | tf_op jit(solution)/shard_map/ppermute | solution.py:240
  48.4 1.9 %collective-permute-done.2 = bf16[2,4,120,128]{3,2,0,1:T(8,128)(2,1)S(1)} collective-permute-done((bf16[2,4,120,128]{3,2,0,1:T(8,128)(2,1)S(1)}, bf16[2,4,120,128]{3,2,0,1:T(8,128)(2,1)S(1)}, u32[]{:S(2)}, u32[]{:S(2)}) %collective-permute-start.2) | collective-permute-done | bytes 245792 | tf_op jit(solution)/shard_map/ppermute | solution.py:240
  50.3 6.9 %collective-permute-done.3 = bf16[2,4,120,128]{3,2,0,1:T(8,128)(2,1)S(1)} collective-permute-done((bf16[2,4,120,128]{3,2,0,1:T(8,128)(2,1)S(1)}, bf16[2,4,120,128]{3,2,0,1:T(8,128)(2,1)S(1)}, u32[]{:S(2)}, u32[]{:S(2)}) %collective-permute-start.3) | collective-permute-done | bytes 245792 | tf_op jit(solution)/shard_map/ppermute | solution.py:240
  58.4 8.2 %collective-permute-start.6 = (bf16[8,120,128]{2,1,0:T(8,128)(2,1)}, bf16[8,120,128]{2,1,0:T(8,128)(2,1)S(1)}, u32[]{:S(2)}, u32[]{:S(2)}) collective-permute-start(bf16[8,120,128]{2,1,0:T(8,128)(2,1)} %bitcast.30), channel_id=1, source_target_pairs={{0,64},{32,96},{64,0},{96,32},{1,65},{33,97},{65,1},{97,33},{2,66}... | collective-permute-start | bytes 737288 | tf_op jit(solution)/shard_map/ppermute | solution.py:240
  67.3 5.9 %collective-permute-start.5 = (bf16[8,120,128]{2,1,0:T(8,128)(2,1)}, bf16[8,120,128]{2,1,0:T(8,128)(2,1)}, u32[]{:S(2)}, u32[]{:S(2)}) collective-permute-start(bf16[8,120,128]{2,1,0:T(8,128)(2,1)} %bitcast.25), channel_id=1, source_target_pairs={{0,32},{32,64},{64,96},{96,0},{1,33},{33,65},{65,97},{97,1},{2,34}... | collective-permute-start | bytes 737288 | tf_op jit(solution)/shard_map/ppermute | solution.py:240
  73.9 3.9 %collective-permute-start.7 = (bf16[8,120,128]{2,1,0:T(8,128)(2,1)}, bf16[8,120,128]{2,1,0:T(8,128)(2,1)}, u32[]{:S(2)}, u32[]{:S(2)}) collective-permute-start(bf16[8,120,128]{2,1,0:T(8,128)(2,1)} %bitcast.35), channel_id=1, source_target_pairs={{0,96},{32,0},{64,32},{96,64},{1,97},{33,1},{65,33},{97,65},{2,98}... | collective-permute-start | bytes 737288 | tf_op jit(solution)/shard_map/ppermute | solution.py:240
  77.9 1.2 copy-done.7
  79.1 1.0 copy-done.12
  83.1 24.1 %collective-permute-start.10 = (f32[8,1024]{1,0:T(8,128)}, f32[8,1024]{1,0:T(8,128)S(1)}, u32[]{:S(2)}, u32[]{:S(2)}) collective-permute-start(f32[8,1024]{1,0:T(8,128)} %get-tuple-element.35), channel_id=1, source_target_pairs={{16,0},{32,16},{48,32},{64,48},{80,64},{96,80},{112,96},{128,112},... | collective-permute-start | bytes 98312 | tf_op jit(solution)/shard_map/ppermute | solution.py:235
  107.2 4.3 %all-to-all-start.1 = ((f32[4,128,512]{2,1,0:T(8,128)}), f32[4,128,512]{2,1,0:T(8,128)}, u32[]{:S(2)}, u32[]{:S(2)}) async-start(f32[4,128,512]{2,1,0:T(8,128)} %bitcast.81), calls=%async_computation.1 | async-start | bytes 2097152 | tf_op jit(solution)/shard_map/all_to_all | solution.py:230
  112.7 9.8 %all-to-all-done.1 = f32[4,128,512]{2,1,0:T(8,128)} async-done(((f32[4,128,512]{2,1,0:T(8,128)}), f32[4,128,512]{2,1,0:T(8,128)}, u32[]{:S(2)}, u32[]{:S(2)}) %all-to-all-start.1) | async-done | bytes 1048608 | tf_op jit(solution)/shard_map/all_to_all | solution.py:230
  122.5 1.3 reduce_sum.9
  123.9 2.1 %collective-permute-start.8 = (f32[64,512]{1,0:T(8,128)S(1)}, f32[64,512]{1,0:T(8,128)S(1)}, u32[]{:S(2)}, u32[]{:S(2)}) collective-permute-start(f32[64,512]{1,0:T(8,128)S(1)} %constant_dynamic-slice_fusion.1), channel_id=1, source_target_pairs={{0,2},{1,3},{2,0},{3,1},{4,6},{5,7},{6,4},{7,5},{8,10},{9,11},{10,... | collective-permute-start | bytes 393224 | tf_op jit(solution)/shard_map/ppermute | solution.py:256
  126.6 5.1 %collective-permute-done.8 = f32[64,512]{1,0:T(8,128)S(1)} collective-permute-done((f32[64,512]{1,0:T(8,128)S(1)}, f32[64,512]{1,0:T(8,128)S(1)}, u32[]{:S(2)}, u32[]{:S(2)}) %collective-permute-start.8) | collective-permute-done | bytes 131104 | tf_op jit(solution)/shard_map/ppermute | solution.py:256
  131.8 2.1 %collective-permute-start.9 = (f32[32,512]{1,0:T(8,128)S(1)}, f32[32,512]{1,0:T(8,128)S(1)}, u32[]{:S(2)}, u32[]{:S(2)}) collective-permute-start(f32[32,512]{1,0:T(8,128)S(1)} %constant_dynamic-slice_fusion), channel_id=1, source_target_pairs={{0,1},{1,0},{2,3},{3,2},{4,5},{5,4},{6,7},{7,6},{8,9},{9,8},{10,11... | collective-permute-start | bytes 196616 | tf_op jit(solution)/shard_map/ppermute | solution.py:256
  134.0 3.0 %shard_map.88.back_ref = f32[960,512]{1,0:T(8,128)S(1)} custom-call(bf16[512,1024]{1,0:T(8,128)(2,1)S(1)} %copy-done.24, f32[96,4]{1,0:T(8,128)S(1)} %bitcast.87, bf16[512,512]{1,0:T(8,128)(2,1)S(1)} %bitcast.85), custom_call_target="tpu_custom_call" | custom-call | flops 34359738368 | bytes 4194304 | tf_op jit(solution)/shard_map/pallas_call | solution.py:310
  137.0 1.3 copy-done.4
  139.0 2.7 %shard_map.92 = (f32[128,128]{1,0:T(8,128)}, bf16[32,16,1024]{2,1,0:T(8,128)(2,1)S(1)}) custom-call(s32[3]{0:T(128)S(1)} %pad_add_fusion.place_ref, bf16[8,120,128]{2,1,0:T(8,128)(2,1)S(1)} %bitcast.82, bf16[8,120,128]{2,1,0:T(8,128)(2,1)} %collective-permute-done.5.in1_ref, bf16[8,120,128]{2,1,0:T(8,128)(2,1)S(1)} %collective-permute-done.6.in2_ref, ...), custom_call_target="tpu_custom_call" | custom-call | flops 536870912 | bytes 4194304 | tf_op jit(solution)/shard_map/pallas_call | solution.py:319
  142.6 6.3 %all-to-all-start.2 = ((f32[16,8,128]{2,1,0:T(8,128)}), f32[16,8,128]{2,1,0:T(8,128)S(1)}, u32[]{:S(2)}, u32[]{:S(2)}) async-start(f32[16,8,128]{2,1,0:T(8,128)} %bitcast.40), calls=%async_computation.2 | async-start | bytes 131072 | tf_op jit(solution)/shard_map/all_to_all | solution.py:230
  148.9 1.5 copy-done.5
  150.4 1.2 copy-done.10
  152.7 3.4 %shard_map.93 = (bf16[960,512]{1,0:T(8,128)(2,1)}, bf16[960,512]{1,0:T(8,128)(2,1)}) custom-call(bf16[32,16,1024]{2,1,0:T(8,128)(2,1)S(1)} %copy-done.10, bf16[512,512]{1,0:T(8,128)(2,1)S(1)} %copy-done.19, bf16[960,512]{1,0:T(8,128)(2,1)S(1)} %bitcast.76, bf16[960,512]{1,0:T(8,128)(2,1)S(1)} %bitcast.80, f32[960,512]{1,0:T(8,128)S(1)} %copy-done.5, ...), custom_call_target="tpu_custom_call" | custom-call | flops 536870912 | bytes 4194304 | tf_op jit(solution)/shard_map/pallas_call | solution.py:323
  (83 shorter events, 16.4 us)
Async XLA Ops:
  0.6 1.2 copy-start
  1.8 2.3 %copy-start.2 = (bf16[10,96,512]{2,1,0:T(8,128)(2,1)S(1)}, bf16[10,96,512]{2,1,0:T(8,128)(2,1)}, u32[]{:S(2)}) copy-start(bf16[10,96,512]{2,1,0:T(8,128)(2,1)} %param.9) | copy-start | bytes 2949124
  1.8 2.3 %copy-start.21 = (bf16[16,32,32]{2,1,0:T(8,128)(2,1)S(1)}, bf16[16,32,32]{2,1,0:T(8,128)(2,1)}, u32[]{:S(2)}) copy-start(bf16[16,32,32]{2,1,0:T(8,128)(2,1)} %param.8) | copy-start | bytes 98308
  2.0 9.3 %collective-permute-start = (bf16[16,960]{1,0:T(8,128)(2,1)S(1)}, bf16[16,960]{1,0:T(8,128)(2,1)S(1)}, u32[]{:S(2)}, u32[]{:S(2)}) collective-permute-start(bf16[16,960]{1,0:T(8,128)(2,1)S(1)} %shard_map.85), channel_id=1, source_target_pairs={{0,16},{16,32},{32,48},{48,64},{64,80},{80,96},{96,112},{112,128},... | collective-permute-start | bytes 92168 | tf_op jit(solution)/shard_map/ppermute | solution.py:235
  4.1 20.8 %copy-start.27 = (f32[4,96]{1,0:T(4,128)S(1)}, f32[4,96]{1,0:T(4,128)}, u32[]{:S(2)}) copy-start(f32[4,96]{1,0:T(4,128)} %param.6) | copy-start | bytes 4612
  4.1 21.0 %copy-start.1 = (bf16[10,96,512]{2,1,0:T(8,128)(2,1)S(1)}, bf16[10,96,512]{2,1,0:T(8,128)(2,1)}, u32[]{:S(2)}) copy-start(bf16[10,96,512]{2,1,0:T(8,128)(2,1)} %param.5) | copy-start | bytes 2949124
  4.1 21.0 %copy-start.11 = (bf16[1,512,512]{2,1,0:T(8,128)(2,1)S(1)}, bf16[1,512,512]{2,1,0:T(8,128)(2,1)}, u32[]{:S(2)}) copy-start(bf16[1,512,512]{2,1,0:T(8,128)(2,1)} %param.7) | copy-start | bytes 1572868
  11.9 65.9 %all-to-all-start = ((bf16[32,120,128]{2,1,0:T(8,128)(2,1)}), bf16[32,120,128]{2,1,0:T(8,128)(2,1)S(1)}, u32[]{:S(2)}, u32[]{:S(2)}) async-start(bf16[32,120,128]{2,1,0:T(8,128)(2,1)} %copy-done.3), calls=%async_computation | async-start | bytes 1966080 | tf_op jit(solution)/shard_map/all_to_all | solution.py:230
  32.9 4.0 %collective-permute-start.1 = (bf16[16,120,128]{2,1,0:T(8,128)(2,1)}, bf16[16,120,128]{2,1,0:T(8,128)(2,1)S(1)}, u32[]{:S(2)}, u32[]{:S(2)}) collective-permute-start(bf16[16,120,128]{2,1,0:T(8,128)(2,1)} %get-tuple-element.31), channel_id=1, source_target_pairs={{0,16},{16,0},{1,17},{17,1},{2,18},{18,2},{3,19},{19,3},{4,20},{20... | collective-permute-start | bytes 1474568 | tf_op jit(solution)/shard_map/ppermute | solution.py:240
  36.9 13.4 %collective-permute-start.2 = (bf16[2,4,120,128]{3,2,0,1:T(8,128)(2,1)S(1)}, bf16[2,4,120,128]{3,2,0,1:T(8,128)(2,1)S(1)}, u32[]{:S(2)}, u32[]{:S(2)}) collective-permute-start(bf16[2,4,120,128]{3,2,0,1:T(8,128)(2,1)S(1)} %pad_maximum_fusion), channel_id=1, source_target_pairs={{0,128},{128,256},{256,384},{384,0},{1,129},{129,257},{257,385},{3... | collective-permute-start | bytes 737288 | tf_op jit(solution)/shard_map/ppermute | solution.py:240
  40.3 16.8 %collective-permute-start.3 = (bf16[2,4,120,128]{3,2,0,1:T(8,128)(2,1)S(1)}, bf16[2,4,120,128]{3,2,0,1:T(8,128)(2,1)S(1)}, u32[]{:S(2)}, u32[]{:S(2)}) collective-permute-start(bf16[2,4,120,128]{3,2,0,1:T(8,128)(2,1)S(1)} %pad_maximum_fusion.1), channel_id=1, source_target_pairs={{0,256},{128,384},{256,0},{384,128},{1,257},{129,385},{257,1},{385... | collective-permute-start | bytes 737288 | tf_op jit(solution)/shard_map/ppermute | solution.py:240
  45.0 12.6 %collective-permute-start.4 = (bf16[2,4,120,128]{3,2,1,0:T(8,128)(2,1)S(1)}, bf16[2,4,120,128]{3,2,1,0:T(8,128)(2,1)S(1)}, u32[]{:S(2)}, u32[]{:S(2)}) collective-permute-start(bf16[2,4,120,128]{3,2,1,0:T(8,128)(2,1)S(1)} %pad_maximum_fusion.2), channel_id=1, source_target_pairs={{0,384},{128,0},{256,128},{384,256},{1,385},{129,1},{257,129},{385... | collective-permute-start | bytes 737288 | tf_op jit(solution)/shard_map/ppermute | solution.py:240
  58.4 80.6 %collective-permute-start.6 = (bf16[8,120,128]{2,1,0:T(8,128)(2,1)}, bf16[8,120,128]{2,1,0:T(8,128)(2,1)S(1)}, u32[]{:S(2)}, u32[]{:S(2)}) collective-permute-start(bf16[8,120,128]{2,1,0:T(8,128)(2,1)} %bitcast.30), channel_id=1, source_target_pairs={{0,64},{32,96},{64,0},{96,32},{1,65},{33,97},{65,1},{97,33},{2,66}... | collective-permute-start | bytes 737288 | tf_op jit(solution)/shard_map/ppermute | solution.py:240
  67.3 71.6 %collective-permute-start.5 = (bf16[8,120,128]{2,1,0:T(8,128)(2,1)}, bf16[8,120,128]{2,1,0:T(8,128)(2,1)}, u32[]{:S(2)}, u32[]{:S(2)}) collective-permute-start(bf16[8,120,128]{2,1,0:T(8,128)(2,1)} %bitcast.25), channel_id=1, source_target_pairs={{0,32},{32,64},{64,96},{96,0},{1,33},{33,65},{65,97},{97,1},{2,34}... | collective-permute-start | bytes 737288 | tf_op jit(solution)/shard_map/ppermute | solution.py:240
  73.9 65.0 %collective-permute-start.7 = (bf16[8,120,128]{2,1,0:T(8,128)(2,1)}, bf16[8,120,128]{2,1,0:T(8,128)(2,1)}, u32[]{:S(2)}, u32[]{:S(2)}) collective-permute-start(bf16[8,120,128]{2,1,0:T(8,128)(2,1)} %bitcast.35), channel_id=1, source_target_pairs={{0,96},{32,0},{64,32},{96,64},{1,97},{33,1},{65,33},{97,65},{2,98}... | collective-permute-start | bytes 737288 | tf_op jit(solution)/shard_map/ppermute | solution.py:240
  77.8 1.2 copy-start.7
  79.1 1.0 copy-start.12
  83.1 55.9 %collective-permute-start.10 = (f32[8,1024]{1,0:T(8,128)}, f32[8,1024]{1,0:T(8,128)S(1)}, u32[]{:S(2)}, u32[]{:S(2)}) collective-permute-start(f32[8,1024]{1,0:T(8,128)} %get-tuple-element.35), channel_id=1, source_target_pairs={{16,0},{32,16},{48,32},{64,48},{80,64},{96,80},{112,96},{128,112},... | collective-permute-start | bytes 98312 | tf_op jit(solution)/shard_map/ppermute | solution.py:235
  107.2 15.3 %all-to-all-start.1 = ((f32[4,128,512]{2,1,0:T(8,128)}), f32[4,128,512]{2,1,0:T(8,128)}, u32[]{:S(2)}, u32[]{:S(2)}) async-start(f32[4,128,512]{2,1,0:T(8,128)} %bitcast.81), calls=%async_computation.1 | async-start | bytes 2097152 | tf_op jit(solution)/shard_map/all_to_all | solution.py:230
  112.5 13.4 %copy-start.22 = (bf16[16,32,32]{2,1,0:T(8,128)(2,1)S(1)}, bf16[16,32,32]{2,1,0:T(8,128)(2,1)}, u32[]{:S(2)}) copy-start(bf16[16,32,32]{2,1,0:T(8,128)(2,1)} %param.8) | copy-start | bytes 98308
  112.7 11.1 %copy-start.16 = (bf16[512,512]{1,0:T(8,128)(2,1)}, bf16[512,512]{1,0:T(8,128)(2,1)S(1)}, u32[]{:S(2)}) copy-start(bf16[512,512]{1,0:T(8,128)(2,1)S(1)} %shard_map.89.front_ref) | copy-start | bytes 1572868
  123.8 10.1 %copy-start.13 = (bf16[1,512,512]{2,1,0:T(8,128)(2,1)S(1)}, bf16[1,512,512]{2,1,0:T(8,128)(2,1)}, u32[]{:S(2)}) copy-start(bf16[1,512,512]{2,1,0:T(8,128)(2,1)} %param.7) | copy-start | bytes 1572868
  123.9 10.1 %copy-start.24 = (bf16[512,1024]{1,0:T(8,128)(2,1)S(1)}, bf16[512,1024]{1,0:T(8,128)(2,1)}, u32[]{:S(2)}) copy-start(bf16[512,1024]{1,0:T(8,128)(2,1)} %copy-done.23) | copy-start | bytes 3145732
  123.9 7.9 %collective-permute-start.8 = (f32[64,512]{1,0:T(8,128)S(1)}, f32[64,512]{1,0:T(8,128)S(1)}, u32[]{:S(2)}, u32[]{:S(2)}) collective-permute-start(f32[64,512]{1,0:T(8,128)S(1)} %constant_dynamic-slice_fusion.1), channel_id=1, source_target_pairs={{0,2},{1,3},{2,0},{3,1},{4,6},{5,7},{6,4},{7,5},{8,10},{9,11},{10,... | collective-permute-start | bytes 393224 | tf_op jit(solution)/shard_map/ppermute | solution.py:256
  126.6 7.3 %copy-start.18 = (bf16[512,512]{1,0:T(8,128)(2,1)}, bf16[512,512]{1,0:T(8,128)(2,1)S(1)}, u32[]{:S(2)}) copy-start(bf16[512,512]{1,0:T(8,128)(2,1)S(1)} %shard_map.91.wide_ref) | copy-start | bytes 1572868
  131.8 6.5 %collective-permute-start.9 = (f32[32,512]{1,0:T(8,128)S(1)}, f32[32,512]{1,0:T(8,128)S(1)}, u32[]{:S(2)}, u32[]{:S(2)}) collective-permute-start(f32[32,512]{1,0:T(8,128)S(1)} %constant_dynamic-slice_fusion), channel_id=1, source_target_pairs={{0,1},{1,0},{2,3},{3,2},{4,5},{5,4},{6,7},{7,6},{8,9},{9,8},{10,11... | collective-permute-start | bytes 196616 | tf_op jit(solution)/shard_map/ppermute | solution.py:256
  133.9 5.0 %copy-start.15 = (bf16[512,512]{1,0:T(8,128)(2,1)S(1)}, bf16[512,512]{1,0:T(8,128)(2,1)}, u32[]{:S(2)}) copy-start(bf16[512,512]{1,0:T(8,128)(2,1)} %copy-done.14) | copy-start | bytes 1572868
  133.9 5.0 %copy-start.17 = (bf16[512,512]{1,0:T(8,128)(2,1)S(1)}, bf16[512,512]{1,0:T(8,128)(2,1)}, u32[]{:S(2)}) copy-start(bf16[512,512]{1,0:T(8,128)(2,1)} %copy-done.16) | copy-start | bytes 1572868
  137.0 1.3 copy-start.4
  142.6 13.5 %all-to-all-start.2 = ((f32[16,8,128]{2,1,0:T(8,128)}), f32[16,8,128]{2,1,0:T(8,128)S(1)}, u32[]{:S(2)}, u32[]{:S(2)}) async-start(f32[16,8,128]{2,1,0:T(8,128)} %bitcast.40), calls=%async_computation.2 | async-start | bytes 131072 | tf_op jit(solution)/shard_map/all_to_all | solution.py:230
  148.9 1.5 copy-start.5
  150.4 1.2 copy-start.10
  (10 other events, 8.9 us)

commit v3 on v2

--- a/solution.py
+++ b/solution.py
@@ -1,5 +1,3 @@
-import functools
-
 import jax
 import jax.numpy as jnp
 from jax import lax
@@ -248,24 +246,12 @@
     return [jnp.stack([part[:, step] for part in both]).reshape(8, 120, LANES) for step in range(4)]
 
 
-def halved(part, axis, apart):
+def halves_met(part, axis, apart):
     rows = part.shape[0] // 2
     upper = lax.axis_index(axis) // apart % 2
     mine = lax.dynamic_slice_in_dim(part, upper * rows, rows, 0)
     other = lax.dynamic_slice_in_dim(part, (1 - upper) * rows, rows, 0)
-    return mine + lax.ppermute(other, axis, [(s, s ^ apart) for s in range(lax.axis_size(axis))])
-
-
-def summed(part, axis):
-    count = lax.axis_size(axis)
-    me = lax.axis_index(axis)
-    rows = part.shape[0] // count
-
-    def quarter(step):
-        return lax.dynamic_slice_in_dim(part, lax.rem(me + step, count) * rows, rows, 0)
-
-    arrived = [ahead(quarter(step), axis, step) for step in range(1, count)]
-    return functools.reduce(jnp.add, arrived, quarter(0))
+    return mine, lax.ppermute(other, axis, [(s, s ^ apart) for s in range(lax.axis_size(axis))])
 
 
 def total_kernel(in_ref, out_ref):
@@ -305,21 +291,24 @@
         back, conv, left
     )
     after = along_seq(dedge, -1)
+    (conv_back,) = call(dconv_kernel, [((960, 512), F32)], flops=1 << 35)(dfirst, taps, left)
     left_sum = jnp.sum(exchange(left_part.reshape(4, 128, 512), "x"), 0)
-    left_grad = halved(halved(left_sum, "zl", 2), "zl", 1)
-    (conv_back,) = call(dconv_kernel, [((960, 512), F32)], flops=1 << 35)(dfirst, taps, left)
+    left_sum = lax.optimization_barrier((left_sum, conv_back))[0]
+    kept, met = halves_met(left_sum, "zl", 2)
     late = lax.optimization_barrier((x, cot, right, dedge))
-    (wide,) = call(wide_kernel, [((512, 512), BF16)], flops=1 << 35)(late[2])
-    (front,) = call(front_gate_kernel, [((512, 512), BF16)], flops=1 << 35)(*late[:2])
-    (rear,) = call(rear_gate_kernel, [((512, 512), BF16)], flops=1 << 35)(*late[:2])
-    columns, left_grad, after, conv_back, front, rear, wide = lax.optimization_barrier(
-        (columns, left_grad, after, conv_back, front, rear, wide)
+    (wide,) = call(wide_kernel, [((512, 512), BF16)], flops=1 << 31)(late[2])
+    (front,) = call(front_gate_kernel, [((512, 512), BF16)], flops=1 << 31)(*late[:2])
+    (rear,) = call(rear_gate_kernel, [((512, 512), BF16)], flops=1 << 31)(*late[:2])
+    columns, after, conv_back, front, rear, wide = lax.optimization_barrier(
+        (columns, after, conv_back, front, rear, wide)
     )
 
     right_part, first = call(right_kernel, [((128, LANES), F32), ((32, 16, 1024), BF16)], scalars=1, arrays=6)(
         place, *columns, front, rear
     )
     right_all = exchange(right_part.reshape(16, 8, LANES), CHAN)
+    met = lax.optimization_barrier((met, right_part))[0]
+    left_grad = sum(halves_met(kept + met, "zl", 1))
     mixed, frames_grad = call(end_kernel, [((960, 512), BF16), ((960, 512), BF16)])(
         first, wide, x, cot, conv_back, after, taps
     )

time: 158 us -> 157 us (level)
  the two profiles are of different devices: /device:TPU:480 before, /device:TPU:8 now
where the time goes in v3:
time: 157 us; the launch traced here: 156 us
  starting transfers between devices  77.1 us (49%)
  waiting for transfers between devices  35.3 us (22%)
  Pallas kernels  19 us (12%)
  local copies, waits for them, and re-layouts  18.5 us (12%)
  other arithmetic  5.39 us (3%)
    all_to_all x3, starting transfers between devices, exchange(): return lax.all_to_all(value, axes, split_axis=0, concat_axis=0, tiled=True)  33.4 us
    ppermute x7, starting transfers between devices, ahead(): lax.ppermute(value, axis, [(s, (s + step) % count) for s in range(count)])  33 us
    ppermute x7, waiting for transfers between devices, ahead(): lax.ppermute(value, axis, [(s, (s + step) % count) for s in range(count)])  19.9 us
    unnamed x55, local copies, waits for them, and re-layouts  16.6 us
    ppermute x2, waiting for transfers between devices, along_seq(): return lax.ppermute(value, SEQ, pairs)  9.16 us
    ppermute x2, starting transfers between devices, halves_met(): lax.ppermute(other, axis, [(s, s ^ apart) for s in range(lax.axis_size(ax...  6.74 us
    all_to_all x3, waiting for transfers between devices, exchange(): return lax.all_to_all(value, axes, split_axis=0, concat_axis=0, tiled=True)  6.21 us
    pallas_call x1, Pallas kernels, shards(): call(conv_kernel, [((1024, 512), BF16), part, part], scratch=[pltpu.VMEM(...  5.28 us
  transfers between devices with their start and end apart: 14, of which 8 were waited for; matrix products, arithmetic and copies ran while one was open for 4% of the time, Pallas kernels for 12%

profile of v3, /device:TPU:8, one launch (start us, length us, event | category | flops | bytes accessed | tf_op | source)
XLA Modules:
  0.0 156.4 jit_solution(13219901683353364769)
XLA Ops:
  0.6 1.2 copy-done
  2.0 2.1 %collective-permute-start = (bf16[16,960]{1,0:T(8,128)(2,1)S(1)}, bf16[16,960]{1,0:T(8,128)(2,1)S(1)}, u32[]{:S(2)}, u32[]{:S(2)}) collective-permute-start(bf16[16,960]{1,0:T(8,128)(2,1)S(1)} %shard_map.85), channel_id=1, source_target_pairs={{0,16},{16,32},{32,48},{48,64},{64,80},{80,96},{96,112},{112,128},... | collective-permute-start | bytes 92168 | tf_op jit(solution)/shard_map/ppermute | solution.py:233
  4.1 1.6 shard_map.84
  6.7 9.2 %collective-permute-done.edge_ref = bf16[16,960]{1,0:T(8,128)(2,1)S(1)} collective-permute-done((bf16[16,960]{1,0:T(8,128)(2,1)S(1)}, bf16[16,960]{1,0:T(8,128)(2,1)S(1)}, u32[]{:S(2)}, u32[]{:S(2)}) %collective-permute-start) | collective-permute-done | bytes 30752 | tf_op jit(solution)/shard_map/ppermute | solution.py:233
  16.4 13.8 %all-to-all-start = ((bf16[32,120,128]{2,1,0:T(8,128)(2,1)}), bf16[32,120,128]{2,1,0:T(8,128)(2,1)S(1)}, u32[]{:S(2)}, u32[]{:S(2)}) async-start(bf16[32,120,128]{2,1,0:T(8,128)(2,1)} %copy-done.3), calls=%async_computation | async-start | bytes 1966080 | tf_op jit(solution)/shard_map/all_to_all | solution.py:228
  31.2 5.3 %shard_map.86 = (bf16[1024,512]{1,0:T(8,128)(2,1)S(1)}, bf16[16,120,128]{2,1,0:T(8,128)(2,1)S(1)}, bf16[16,120,128]{2,1,0:T(8,128)(2,1)}) custom-call(s32[3]{0:T(128)S(1)} %pad_add_fusion.place_ref, bf16[960,512]{1,0:T(8,128)(2,1)S(1)} %bitcast.74, bf16[16,960]{1,0:T(8,128)(2,1)S(1)} %copy-done.24, f32[96,4]{1,0:T(8,128)S(1)} %bitcast.87, ...), custom_call_target="tpu_custom_call" | custom-call | flops 536870912 | bytes 4194304 | tf_op jit(solution)/shard_map/pallas_call | solution.py:280
  38.3 2.0 %collective-permute-start.1 = (bf16[16,120,128]{2,1,0:T(8,128)(2,1)}, bf16[16,120,128]{2,1,0:T(8,128)(2,1)S(1)}, u32[]{:S(2)}, u32[]{:S(2)}) collective-permute-start(bf16[16,120,128]{2,1,0:T(8,128)(2,1)} %get-tuple-element.32), channel_id=1, source_target_pairs={{0,16},{16,0},{1,17},{17,1},{2,18},{18,2},{3,19},{19,3},{4,20},{20... | collective-permute-start | bytes 1474568 | tf_op jit(solution)/shard_map/ppermute | solution.py:238
  40.4 1.1 slice_bitcast_fusion.7
  42.3 3.4 %collective-permute-start.2 = (bf16[2,4,120,128]{3,2,0,1:T(8,128)(2,1)S(1)}, bf16[2,4,120,128]{3,2,0,1:T(8,128)(2,1)S(1)}, u32[]{:S(2)}, u32[]{:S(2)}) collective-permute-start(bf16[2,4,120,128]{3,2,0,1:T(8,128)(2,1)S(1)} %pad_maximum_fusion), channel_id=1, source_target_pairs={{0,128},{128,256},{256,384},{384,0},{1,129},{129,257},{257,385},{3... | collective-permute-start | bytes 737288 | tf_op jit(solution)/shard_map/ppermute | solution.py:238
  45.8 2.7 %collective-permute-start.3 = (bf16[2,4,120,128]{3,2,0,1:T(8,128)(2,1)S(1)}, bf16[2,4,120,128]{3,2,0,1:T(8,128)(2,1)S(1)}, u32[]{:S(2)}, u32[]{:S(2)}) collective-permute-start(bf16[2,4,120,128]{3,2,0,1:T(8,128)(2,1)S(1)} %pad_maximum_fusion.1), channel_id=1, source_target_pairs={{0,256},{128,384},{256,0},{384,128},{1,257},{129,385},{257,1},{385... | collective-permute-start | bytes 737288 | tf_op jit(solution)/shard_map/ppermute | solution.py:238
  48.5 4.4 %collective-permute-start.4 = (bf16[2,4,120,128]{3,2,1,0:T(8,128)(2,1)S(1)}, bf16[2,4,120,128]{3,2,1,0:T(8,128)(2,1)S(1)}, u32[]{:S(2)}, u32[]{:S(2)}) collective-permute-start(bf16[2,4,120,128]{3,2,1,0:T(8,128)(2,1)S(1)} %pad_maximum_fusion.2), channel_id=1, source_target_pairs={{0,384},{128,0},{256,128},{384,256},{1,385},{129,1},{257,129},{385... | collective-permute-start | bytes 737288 | tf_op jit(solution)/shard_map/ppermute | solution.py:238
  52.9 3.2 %collective-permute-done.2 = bf16[2,4,120,128]{3,2,0,1:T(8,128)(2,1)S(1)} collective-permute-done((bf16[2,4,120,128]{3,2,0,1:T(8,128)(2,1)S(1)}, bf16[2,4,120,128]{3,2,0,1:T(8,128)(2,1)S(1)}, u32[]{:S(2)}, u32[]{:S(2)}) %collective-permute-start.2) | collective-permute-done | bytes 245792 | tf_op jit(solution)/shard_map/ppermute | solution.py:238
  56.2 4.9 %collective-permute-done.3 = bf16[2,4,120,128]{3,2,0,1:T(8,128)(2,1)S(1)} collective-permute-done((bf16[2,4,120,128]{3,2,0,1:T(8,128)(2,1)S(1)}, bf16[2,4,120,128]{3,2,0,1:T(8,128)(2,1)S(1)}, u32[]{:S(2)}, u32[]{:S(2)}) %collective-permute-start.3) | collective-permute-done | bytes 245792 | tf_op jit(solution)/shard_map/ppermute | solution.py:238
  61.1 4.7 %collective-permute-done.4 = bf16[2,4,120,128]{3,2,1,0:T(8,128)(2,1)S(1)} collective-permute-done((bf16[2,4,120,128]{3,2,1,0:T(8,128)(2,1)S(1)}, bf16[2,4,120,128]{3,2,1,0:T(8,128)(2,1)S(1)}, u32[]{:S(2)}, u32[]{:S(2)}) %collective-permute-start.4) | collective-permute-done | bytes 245792 | tf_op jit(solution)/shard_map/ppermute | solution.py:238
  66.5 10.8 %collective-permute-start.6 = (bf16[8,120,128]{2,1,0:T(8,128)(2,1)}, bf16[8,120,128]{2,1,0:T(8,128)(2,1)S(1)}, u32[]{:S(2)}, u32[]{:S(2)}) collective-permute-start(bf16[8,120,128]{2,1,0:T(8,128)(2,1)} %bitcast.30), channel_id=1, source_target_pairs={{0,64},{32,96},{64,0},{96,32},{1,65},{33,97},{65,1},{97,33},{2,66}... | collective-permute-start | bytes 737288 | tf_op jit(solution)/shard_map/ppermute | solution.py:238
  78.0 3.3 %collective-permute-start.5 = (bf16[8,120,128]{2,1,0:T(8,128)(2,1)}, bf16[8,120,128]{2,1,0:T(8,128)(2,1)}, u32[]{:S(2)}, u32[]{:S(2)}) collective-permute-start(bf16[8,120,128]{2,1,0:T(8,128)(2,1)} %bitcast.25), channel_id=1, source_target_pairs={{0,32},{32,64},{64,96},{96,0},{1,33},{33,65},{65,97},{97,1},{2,34}... | collective-permute-start | bytes 737288 | tf_op jit(solution)/shard_map/ppermute | solution.py:238
  82.1 6.4 %collective-permute-start.7 = (bf16[8,120,128]{2,1,0:T(8,128)(2,1)}, bf16[8,120,128]{2,1,0:T(8,128)(2,1)}, u32[]{:S(2)}, u32[]{:S(2)}) collective-permute-start(bf16[8,120,128]{2,1,0:T(8,128)(2,1)} %bitcast.35), channel_id=1, source_target_pairs={{0,96},{32,0},{64,32},{96,64},{1,97},{33,1},{65,33},{97,65},{2,98}... | collective-permute-start | bytes 737288 | tf_op jit(solution)/shard_map/ppermute | solution.py:238
  88.5 1.2 copy-done.7
  93.8 4.4 %all-to-all-start.1 = ((f32[4,128,512]{2,1,0:T(8,128)}), f32[4,128,512]{2,1,0:T(8,128)}, u32[]{:S(2)}, u32[]{:S(2)}) async-start(f32[4,128,512]{2,1,0:T(8,128)} %bitcast.82), calls=%async_computation.1 | async-start | bytes 2097152 | tf_op jit(solution)/shard_map/all_to_all | solution.py:228
  98.2 1.9 %collective-permute-start.8 = (f32[8,1024]{1,0:T(8,128)S(1)}, f32[8,1024]{1,0:T(8,128)S(1)}, u32[]{:S(2)}, u32[]{:S(2)}) collective-permute-start(f32[8,1024]{1,0:T(8,128)S(1)} %get-tuple-element.35), channel_id=1, source_target_pairs={{16,0},{32,16},{48,32},{64,48},{80,64},{96,80},{112,96},{128,112},... | collective-permute-start | bytes 98312 | tf_op jit(solution)/shard_map/ppermute | solution.py:233
  100.2 1.2 copy-done.22
  101.4 3.0 %shard_map.88.back_ref = f32[960,512]{1,0:T(8,128)S(1)} custom-call(bf16[512,1024]{1,0:T(8,128)(2,1)S(1)} %copy-done.22, f32[96,4]{1,0:T(8,128)S(1)} %bitcast.88, bf16[512,512]{1,0:T(8,128)(2,1)S(1)} %bitcast.86), custom_call_target="tpu_custom_call" | custom-call | flops 34359738368 | bytes 4194304 | tf_op jit(solution)/shard_map/pallas_call | solution.py:294
  106.7 6.2 %all-to-all-done.1 = f32[4,128,512]{2,1,0:T(8,128)} async-done(((f32[4,128,512]{2,1,0:T(8,128)}), f32[4,128,512]{2,1,0:T(8,128)}, u32[]{:S(2)}, u32[]{:S(2)}) %all-to-all-start.1) | async-done | bytes 1048608 | tf_op jit(solution)/shard_map/all_to_all | solution.py:228
  113.0 1.3 reduce_sum.9
  115.0 2.9 %collective-permute-start.9 = (f32[64,512]{1,0:T(8,128)}, f32[64,512]{1,0:T(8,128)}, u32[]{:S(2)}, u32[]{:S(2)}) collective-permute-start(f32[64,512]{1,0:T(8,128)} %constant_dynamic-slice_fusion.1), channel_id=1, source_target_pairs={{0,2},{1,3},{2,0},{3,1},{4,6},{5,7},{6,4},{7,5},{8,10},{9,11},{10,... | collective-permute-start | bytes 393224 | tf_op jit(solution)/shard_map/ppermute | solution.py:254
  119.5 5.5 %collective-permute-done.7.in3_ref = bf16[8,120,128]{2,1,0:T(8,128)(2,1)} collective-permute-done((bf16[8,120,128]{2,1,0:T(8,128)(2,1)}, bf16[8,120,128]{2,1,0:T(8,128)(2,1)}, u32[]{:S(2)}, u32[]{:S(2)}) %collective-permute-start.7) | collective-permute-done | bytes 245792 | tf_op jit(solution)/shard_map/ppermute | solution.py:238
  125.1 2.7 %shard_map.92 = (f32[128,128]{1,0:T(8,128)}, bf16[32,16,1024]{2,1,0:T(8,128)(2,1)S(1)}) custom-call(s32[3]{0:T(128)S(1)} %pad_add_fusion.place_ref, bf16[8,120,128]{2,1,0:T(8,128)(2,1)S(1)} %bitcast.83, bf16[8,120,128]{2,1,0:T(8,128)(2,1)} %collective-permute-done.5.in1_ref, bf16[8,120,128]{2,1,0:T(8,128)(2,1)S(1)} %collective-permute-done.6.in2_ref, ...), custom_call_target="tpu_custom_call" | custom-call | flops 536870912 | bytes 4194304 | tf_op jit(solution)/shard_map/pallas_call | solution.py:306
  128.7 15.1 %all-to-all-start.2 = ((f32[16,8,128]{2,1,0:T(8,128)}), f32[16,8,128]{2,1,0:T(8,128)S(1)}, u32[]{:S(2)}, u32[]{:S(2)}) async-start(f32[16,8,128]{2,1,0:T(8,128)} %bitcast.40), calls=%async_computation.2 | async-start | bytes 131072 | tf_op jit(solution)/shard_map/all_to_all | solution.py:228
  144.9 3.8 %collective-permute-start.10 = (f32[32,512]{1,0:T(8,128)S(1)}, f32[32,512]{1,0:T(8,128)S(1)}, u32[]{:S(2)}, u32[]{:S(2)}) collective-permute-start(f32[32,512]{1,0:T(8,128)S(1)} %constant_dynamic-slice_fusion), channel_id=1, source_target_pairs={{0,1},{1,0},{2,3},{3,2},{4,5},{5,4},{6,7},{7,6},{8,9},{9,8},{10,11... | collective-permute-start | bytes 196616 | tf_op jit(solution)/shard_map/ppermute | solution.py:254
  148.8 1.5 copy-done.5
  150.3 1.2 copy-done.10
  151.5 3.5 %shard_map.93 = (bf16[960,512]{1,0:T(8,128)(2,1)}, bf16[960,512]{1,0:T(8,128)(2,1)}) custom-call(bf16[32,16,1024]{2,1,0:T(8,128)(2,1)S(1)} %copy-done.10, bf16[512,512]{1,0:T(8,128)(2,1)S(1)} %shard_map.91.wide_ref, bf16[960,512]{1,0:T(8,128)(2,1)S(1)} %bitcast.77, bf16[960,512]{1,0:T(8,128)(2,1)S(1)} %bitcast.81, f32[960,512]{1,0:T(8,128)S(1)} %copy-done.5, ...), custom_call_target="tpu_custom_call" | custom-call | flops 536870912 | bytes 4194304 | tf_op jit(solution)/shard_map/pallas_call | solution.py:312
  (81 shorter events, 19.6 us)
Async XLA Ops:
  0.6 1.2 copy-start
  1.8 2.3 %copy-start.2 = (bf16[10,96,512]{2,1,0:T(8,128)(2,1)S(1)}, bf16[10,96,512]{2,1,0:T(8,128)(2,1)}, u32[]{:S(2)}) copy-start(bf16[10,96,512]{2,1,0:T(8,128)(2,1)} %param.9) | copy-start | bytes 2949124
  1.8 2.3 %copy-start.19 = (bf16[16,32,32]{2,1,0:T(8,128)(2,1)S(1)}, bf16[16,32,32]{2,1,0:T(8,128)(2,1)}, u32[]{:S(2)}) copy-start(bf16[16,32,32]{2,1,0:T(8,128)(2,1)} %param.8) | copy-start | bytes 98308
  2.0 13.8 %collective-permute-start = (bf16[16,960]{1,0:T(8,128)(2,1)S(1)}, bf16[16,960]{1,0:T(8,128)(2,1)S(1)}, u32[]{:S(2)}, u32[]{:S(2)}) collective-permute-start(bf16[16,960]{1,0:T(8,128)(2,1)S(1)} %shard_map.85), channel_id=1, source_target_pairs={{0,16},{16,32},{32,48},{48,64},{64,80},{80,96},{96,112},{112,128},... | collective-permute-start | bytes 92168 | tf_op jit(solution)/shard_map/ppermute | solution.py:233
  4.1 26.2 %copy-start.26 = (f32[4,96]{1,0:T(4,128)S(1)}, f32[4,96]{1,0:T(4,128)}, u32[]{:S(2)}) copy-start(f32[4,96]{1,0:T(4,128)} %param.6) | copy-start | bytes 4612
  4.1 26.3 %copy-start.1 = (bf16[10,96,512]{2,1,0:T(8,128)(2,1)S(1)}, bf16[10,96,512]{2,1,0:T(8,128)(2,1)}, u32[]{:S(2)}) copy-start(bf16[10,96,512]{2,1,0:T(8,128)(2,1)} %param.5) | copy-start | bytes 2949124
  4.1 26.3 %copy-start.11 = (bf16[1,512,512]{2,1,0:T(8,128)(2,1)S(1)}, bf16[1,512,512]{2,1,0:T(8,128)(2,1)}, u32[]{:S(2)}) copy-start(bf16[1,512,512]{2,1,0:T(8,128)(2,1)} %param.7) | copy-start | bytes 1572868
  16.4 72.1 %all-to-all-start = ((bf16[32,120,128]{2,1,0:T(8,128)(2,1)}), bf16[32,120,128]{2,1,0:T(8,128)(2,1)S(1)}, u32[]{:S(2)}, u32[]{:S(2)}) async-start(bf16[32,120,128]{2,1,0:T(8,128)(2,1)} %copy-done.3), calls=%async_computation | async-start | bytes 1966080 | tf_op jit(solution)/shard_map/all_to_all | solution.py:228
  38.3 4.0 %collective-permute-start.1 = (bf16[16,120,128]{2,1,0:T(8,128)(2,1)}, bf16[16,120,128]{2,1,0:T(8,128)(2,1)S(1)}, u32[]{:S(2)}, u32[]{:S(2)}) collective-permute-start(bf16[16,120,128]{2,1,0:T(8,128)(2,1)} %get-tuple-element.32), channel_id=1, source_target_pairs={{0,16},{16,0},{1,17},{17,1},{2,18},{18,2},{3,19},{19,3},{4,20},{20... | collective-permute-start | bytes 1474568 | tf_op jit(solution)/shard_map/ppermute | solution.py:238
  42.3 13.8 %collective-permute-start.2 = (bf16[2,4,120,128]{3,2,0,1:T(8,128)(2,1)S(1)}, bf16[2,4,120,128]{3,2,0,1:T(8,128)(2,1)S(1)}, u32[]{:S(2)}, u32[]{:S(2)}) collective-permute-start(bf16[2,4,120,128]{3,2,0,1:T(8,128)(2,1)S(1)} %pad_maximum_fusion), channel_id=1, source_target_pairs={{0,128},{128,256},{256,384},{384,0},{1,129},{129,257},{257,385},{3... | collective-permute-start | bytes 737288 | tf_op jit(solution)/shard_map/ppermute | solution.py:238
  45.8 15.3 %collective-permute-start.3 = (bf16[2,4,120,128]{3,2,0,1:T(8,128)(2,1)S(1)}, bf16[2,4,120,128]{3,2,0,1:T(8,128)(2,1)S(1)}, u32[]{:S(2)}, u32[]{:S(2)}) collective-permute-start(bf16[2,4,120,128]{3,2,0,1:T(8,128)(2,1)S(1)} %pad_maximum_fusion.1), channel_id=1, source_target_pairs={{0,256},{128,384},{256,0},{384,128},{1,257},{129,385},{257,1},{385... | collective-permute-start | bytes 737288 | tf_op jit(solution)/shard_map/ppermute | solution.py:238
  48.5 17.2 %collective-permute-start.4 = (bf16[2,4,120,128]{3,2,1,0:T(8,128)(2,1)S(1)}, bf16[2,4,120,128]{3,2,1,0:T(8,128)(2,1)S(1)}, u32[]{:S(2)}, u32[]{:S(2)}) collective-permute-start(bf16[2,4,120,128]{3,2,1,0:T(8,128)(2,1)S(1)} %pad_maximum_fusion.2), channel_id=1, source_target_pairs={{0,384},{128,0},{256,128},{384,256},{1,385},{129,1},{257,129},{385... | collective-permute-start | bytes 737288 | tf_op jit(solution)/shard_map/ppermute | solution.py:238
  66.5 52.1 %collective-permute-start.6 = (bf16[8,120,128]{2,1,0:T(8,128)(2,1)}, bf16[8,120,128]{2,1,0:T(8,128)(2,1)S(1)}, u32[]{:S(2)}, u32[]{:S(2)}) collective-permute-start(bf16[8,120,128]{2,1,0:T(8,128)(2,1)} %bitcast.30), channel_id=1, source_target_pairs={{0,64},{32,96},{64,0},{96,32},{1,65},{33,97},{65,1},{97,33},{2,66}... | collective-permute-start | bytes 737288 | tf_op jit(solution)/shard_map/ppermute | solution.py:238
  78.0 41.5 %collective-permute-start.5 = (bf16[8,120,128]{2,1,0:T(8,128)(2,1)}, bf16[8,120,128]{2,1,0:T(8,128)(2,1)}, u32[]{:S(2)}, u32[]{:S(2)}) collective-permute-start(bf16[8,120,128]{2,1,0:T(8,128)(2,1)} %bitcast.25), channel_id=1, source_target_pairs={{0,32},{32,64},{64,96},{96,0},{1,33},{33,65},{65,97},{97,1},{2,34}... | collective-permute-start | bytes 737288 | tf_op jit(solution)/shard_map/ppermute | solution.py:238
  82.1 43.0 %collective-permute-start.7 = (bf16[8,120,128]{2,1,0:T(8,128)(2,1)}, bf16[8,120,128]{2,1,0:T(8,128)(2,1)}, u32[]{:S(2)}, u32[]{:S(2)}) collective-permute-start(bf16[8,120,128]{2,1,0:T(8,128)(2,1)} %bitcast.35), channel_id=1, source_target_pairs={{0,96},{32,0},{64,32},{96,64},{1,97},{33,1},{65,33},{97,65},{2,98}... | collective-permute-start | bytes 737288 | tf_op jit(solution)/shard_map/ppermute | solution.py:238
  88.5 1.2 copy-start.7
  89.8 1.0 copy-start.12
  93.8 6.3 %copy-start.13 = (bf16[1,512,512]{2,1,0:T(8,128)(2,1)S(1)}, bf16[1,512,512]{2,1,0:T(8,128)(2,1)}, u32[]{:S(2)}) copy-start(bf16[1,512,512]{2,1,0:T(8,128)(2,1)} %param.7) | copy-start | bytes 1572868
  93.8 19.2 %all-to-all-start.1 = ((f32[4,128,512]{2,1,0:T(8,128)}), f32[4,128,512]{2,1,0:T(8,128)}, u32[]{:S(2)}, u32[]{:S(2)}) async-start(f32[4,128,512]{2,1,0:T(8,128)} %bitcast.82), calls=%async_computation.1 | async-start | bytes 2097152 | tf_op jit(solution)/shard_map/all_to_all | solution.py:228
  98.2 26.8 %collective-permute-start.8 = (f32[8,1024]{1,0:T(8,128)S(1)}, f32[8,1024]{1,0:T(8,128)S(1)}, u32[]{:S(2)}, u32[]{:S(2)}) collective-permute-start(f32[8,1024]{1,0:T(8,128)S(1)} %get-tuple-element.35), channel_id=1, source_target_pairs={{16,0},{32,16},{48,32},{64,48},{80,64},{96,80},{112,96},{128,112},... | collective-permute-start | bytes 98312 | tf_op jit(solution)/shard_map/ppermute | solution.py:233
  100.1 1.2 copy-start.22
  104.4 1.3 copy-start.4
  106.5 11.4 %copy-start.20 = (bf16[16,32,32]{2,1,0:T(8,128)(2,1)S(1)}, bf16[16,32,32]{2,1,0:T(8,128)(2,1)}, u32[]{:S(2)}) copy-start(bf16[16,32,32]{2,1,0:T(8,128)(2,1)} %param.8) | copy-start | bytes 98308
  106.7 7.6 %copy-start.16 = (bf16[512,512]{1,0:T(8,128)(2,1)}, bf16[512,512]{1,0:T(8,128)(2,1)S(1)}, u32[]{:S(2)}) copy-start(bf16[512,512]{1,0:T(8,128)(2,1)S(1)} %shard_map.89.front_ref) | copy-start | bytes 1572868
  114.3 4.3 %copy-start.25 = (f32[128,512]{1,0:T(8,128)}, f32[128,512]{1,0:T(8,128)S(1)}, u32[]{:S(2)}) copy-start(f32[128,512]{1,0:T(8,128)S(1)} %reduce_sum.9) | copy-start | bytes 786436
  115.0 10.0 %copy-start.15 = (bf16[512,512]{1,0:T(8,128)(2,1)S(1)}, bf16[512,512]{1,0:T(8,128)(2,1)}, u32[]{:S(2)}) copy-start(bf16[512,512]{1,0:T(8,128)(2,1)} %copy-done.14) | copy-start | bytes 1572868
  115.0 10.0 %copy-start.17 = (bf16[512,512]{1,0:T(8,128)(2,1)S(1)}, bf16[512,512]{1,0:T(8,128)(2,1)}, u32[]{:S(2)}) copy-start(bf16[512,512]{1,0:T(8,128)(2,1)} %copy-done.16) | copy-start | bytes 1572868
  115.0 28.9 %collective-permute-start.9 = (f32[64,512]{1,0:T(8,128)}, f32[64,512]{1,0:T(8,128)}, u32[]{:S(2)}, u32[]{:S(2)}) collective-permute-start(f32[64,512]{1,0:T(8,128)} %constant_dynamic-slice_fusion.1), channel_id=1, source_target_pairs={{0,2},{1,3},{2,0},{3,1},{4,6},{5,7},{6,4},{7,5},{8,10},{9,11},{10,... | collective-permute-start | bytes 393224 | tf_op jit(solution)/shard_map/ppermute | solution.py:254
  128.7 26.3 %all-to-all-start.2 = ((f32[16,8,128]{2,1,0:T(8,128)}), f32[16,8,128]{2,1,0:T(8,128)S(1)}, u32[]{:S(2)}, u32[]{:S(2)}) async-start(f32[16,8,128]{2,1,0:T(8,128)} %bitcast.40), calls=%async_computation.2 | async-start | bytes 131072 | tf_op jit(solution)/shard_map/all_to_all | solution.py:228
  144.9 10.8 %collective-permute-start.10 = (f32[32,512]{1,0:T(8,128)S(1)}, f32[32,512]{1,0:T(8,128)S(1)}, u32[]{:S(2)}, u32[]{:S(2)}) collective-permute-start(f32[32,512]{1,0:T(8,128)S(1)} %constant_dynamic-slice_fusion), channel_id=1, source_target_pairs={{0,1},{1,0},{2,3},{3,2},{4,5},{5,4},{6,7},{7,6},{8,9},{9,8},{10,11... | collective-permute-start | bytes 196616 | tf_op jit(solution)/shard_map/ppermute | solution.py:254
  148.7 1.5 copy-start.5
  150.3 1.2 copy-start.10
  (9 other events, 7.9 us)

commit v4 on v3

--- a/solution.py
+++ b/solution.py
@@ -183,8 +183,8 @@
         back_ref[pl.ds(clip * 96, 96), :] = total
 
 
-def right_kernel(place_ref, in0_ref, in1_ref, in2_ref, in3_ref, front_ref, rear_ref, part_ref, first_ref):
-    for zh, in_ref in enumerate((in0_ref, in1_ref, in2_ref, in3_ref)):
+def get_columns(place_ref, in_refs, first_ref):
+    for zh, in_ref in enumerate(in_refs):
         rest = in_ref[:, pl.ds(112, 8), :].astype(F32)
         begin = iota(rest.shape, 2) < 64
         low = jnp.where(begin, rest, 0.0)
@@ -195,6 +195,10 @@
             for tile in range(7):
                 first_ref[source, :, tile * LANES : (tile + 1) * LANES] = in_ref[block, pl.ds(tile * 16, 16), :]
             first_ref[source, :, 7 * LANES :] = last[block]
+
+
+def right_kernel(place_ref, in0_ref, in1_ref, in2_ref, in3_ref, front_ref, rear_ref, part_ref, first_ref):
+    get_columns(place_ref, (in0_ref, in1_ref, in2_ref, in3_ref), first_ref)
     for at in range(0, 512, 128):
         rows = first_ref[pl.ds(at // 16, 8)].reshape(128, 1024)
         full = dot(rows[:, :512], front_ref[...], (1, 0)) + dot(rows[:, 512:], rear_ref[...], (1, 0))
@@ -204,7 +208,8 @@
             part_ref[pl.ds(at // 4 + tile, 8, stride=4), :] = total[:, tile * LANES : (tile + 1) * LANES]
 
 
-def end_kernel(first_ref, wide_ref, frames_ref, grad_ref, back_ref, after_ref, taps_ref, mixed_ref, out_ref):
+def end_kernel(place_ref, in0_ref, in1_ref, in2_ref, in3_ref, wide_ref, frames_ref, grad_ref, back_ref, after_ref, taps_ref, mixed_ref, out_ref, first_ref):
+    get_columns(place_ref, (in0_ref, in1_ref, in2_ref, in3_ref), first_ref)
     place = (iota((8, LANES), 1) == iota((8, LANES), 0)).astype(F32)
     lane = iota((96, LANES), 1)
     second = dot(first_ref[...].reshape(512, 1024), wide_ref[...], (0, 0))
@@ -303,15 +308,16 @@
         (columns, after, conv_back, front, rear, wide)
     )
 
-    right_part, first = call(right_kernel, [((128, LANES), F32), ((32, 16, 1024), BF16)], scalars=1, arrays=6)(
+    scratch = [pltpu.VMEM((32, 16, 1024), BF16)]
+    (right_part,) = call(right_kernel, [((128, LANES), F32)], scratch=scratch, scalars=1, arrays=6)(
         place, *columns, front, rear
     )
     right_all = exchange(right_part.reshape(16, 8, LANES), CHAN)
     met = lax.optimization_barrier((met, right_part))[0]
     left_grad = sum(halves_met(kept + met, "zl", 1))
-    mixed, frames_grad = call(end_kernel, [((960, 512), BF16), ((960, 512), BF16)])(
-        first, wide, x, cot, conv_back, after, taps
-    )
+    mixed, frames_grad = call(
+        end_kernel, [((960, 512), BF16), ((960, 512), BF16)], scratch=scratch, scalars=1, arrays=10
+    )(place, *columns, wide, x, cot, conv_back, after, taps)
     (right_grad,) = call(total_kernel, [((16, 2, 32), F32)])(right_all)
     return (
         mixed.reshape(frames.shape),

time: 157 us -> 152 us (0.968)
  the two profiles are of different devices: /device:TPU:8 before, /device:TPU:1 now
where the time goes in v4:
time: 152 us; the launch traced here: 151 us
  starting transfers between devices  92.1 us (61%)
  Pallas kernels  20 us (13%)
  waiting for transfers between devices  16.2 us (11%)
  local copies, waits for them, and re-layouts  16.1 us (11%)
  other arithmetic  5.38 us (4%)
    all_to_all x3, starting transfers between devices, exchange(): return lax.all_to_all(value, axes, split_axis=0, concat_axis=0, tiled=True)  39.9 us
    ppermute x7, starting transfers between devices, ahead(): lax.ppermute(value, axis, [(s, (s + step) % count) for s in range(count)])  32.7 us
    ppermute x2, starting transfers between devices, along_seq(): return lax.ppermute(value, SEQ, pairs)  14 us
    unnamed x55, local copies, waits for them, and re-layouts  13.5 us
    ppermute x7, waiting for transfers between devices, ahead(): lax.ppermute(value, axis, [(s, (s + step) % count) for s in range(count)])  11.9 us
    ppermute x2, starting transfers between devices, halves_met(): lax.ppermute(other, axis, [(s, s ^ apart) for s in range(lax.axis_size(ax...  5.48 us
    pallas_call x1, Pallas kernels, shards(): call(conv_kernel, [((1024, 512), BF16), part, part], scratch=[pltpu.VMEM(...  5.28 us
    pallas_call x1, Pallas kernels, shards(): call(end_kernel, [((960, 512), BF16), ((960, 512), BF16)], scratch=scratc...  4.49 us
  transfers between devices with their start and end apart: 14, of which 6 were waited for; matrix products, arithmetic and copies ran while one was open for 5% of the time, Pallas kernels for 13%

profile of v4, /device:TPU:1, one launch (start us, length us, event | category | flops | bytes accessed | tf_op | source)
XLA Modules:
  0.0 150.9 jit_solution(6031949014549198465)
XLA Ops:
  0.6 1.2 copy-done
  2.0 10.4 %collective-permute-start = (bf16[16,960]{1,0:T(8,128)(2,1)S(1)}, bf16[16,960]{1,0:T(8,128)(2,1)S(1)}, u32[]{:S(2)}, u32[]{:S(2)}) collective-permute-start(bf16[16,960]{1,0:T(8,128)(2,1)S(1)} %shard_map.85), channel_id=1, source_target_pairs={{0,16},{16,32},{32,48},{48,64},{64,80},{80,96},{96,112},{112,128},... | collective-permute-start | bytes 92168 | tf_op jit(solution)/shard_map/ppermute | solution.py:238
  12.4 1.6 %shard_map.84 = bf16[32,120,128]{2,1,0:T(8,128)(2,1)S(1)} custom-call(bf16[960,512]{1,0:T(8,128)(2,1)S(1)} %bitcast.73, bf16[960,512]{1,0:T(8,128)(2,1)S(1)} %bitcast.78, bf16[512,32]{1,0:T(8,128)(2,1)S(1)} %bitcast.91), custom_call_target="tpu_custom_call" | custom-call | flops 536870912 | bytes 4194304 | tf_op jit(solution)/shard_map/pallas_call | solution.py:280
  15.6 15.7 %all-to-all-start = ((bf16[32,120,128]{2,1,0:T(8,128)(2,1)}), bf16[32,120,128]{2,1,0:T(8,128)(2,1)S(1)}, u32[]{:S(2)}, u32[]{:S(2)}) async-start(bf16[32,120,128]{2,1,0:T(8,128)(2,1)} %copy-done.3), calls=%async_computation | async-start | bytes 1966080 | tf_op jit(solution)/shard_map/all_to_all | solution.py:233
  32.3 5.3 %shard_map.86 = (bf16[1024,512]{1,0:T(8,128)(2,1)S(1)}, bf16[16,120,128]{2,1,0:T(8,128)(2,1)S(1)}, bf16[16,120,128]{2,1,0:T(8,128)(2,1)}) custom-call(s32[3]{0:T(128)S(1)} %pad_add_fusion.place_ref, bf16[960,512]{1,0:T(8,128)(2,1)S(1)} %bitcast.74, bf16[16,960]{1,0:T(8,128)(2,1)S(1)} %copy-done.22, f32[96,4]{1,0:T(8,128)S(1)} %bitcast.88, ...), custom_call_target="tpu_custom_call" | custom-call | flops 536870912 | bytes 4194304 | tf_op jit(solution)/shard_map/pallas_call | solution.py:285
  39.4 2.1 %collective-permute-start.1 = (bf16[16,120,128]{2,1,0:T(8,128)(2,1)}, bf16[16,120,128]{2,1,0:T(8,128)(2,1)S(1)}, u32[]{:S(2)}, u32[]{:S(2)}) collective-permute-start(bf16[16,120,128]{2,1,0:T(8,128)(2,1)} %get-tuple-element.30), channel_id=1, source_target_pairs={{0,16},{16,0},{1,17},{17,1},{2,18},{18,2},{3,19},{19,3},{4,20},{20... | collective-permute-start | bytes 1474568 | tf_op jit(solution)/shard_map/ppermute | solution.py:243
  41.6 1.1 slice_bitcast_fusion.7
  43.4 3.3 %collective-permute-start.2 = (bf16[2,4,120,128]{3,2,0,1:T(8,128)(2,1)S(1)}, bf16[2,4,120,128]{3,2,0,1:T(8,128)(2,1)S(1)}, u32[]{:S(2)}, u32[]{:S(2)}) collective-permute-start(bf16[2,4,120,128]{3,2,0,1:T(8,128)(2,1)S(1)} %pad_maximum_fusion), channel_id=1, source_target_pairs={{0,128},{128,256},{256,384},{384,0},{1,129},{129,257},{257,385},{3... | collective-permute-start | bytes 737288 | tf_op jit(solution)/shard_map/ppermute | solution.py:243
  46.7 4.3 %collective-permute-start.3 = (bf16[2,4,120,128]{3,2,0,1:T(8,128)(2,1)S(1)}, bf16[2,4,120,128]{3,2,0,1:T(8,128)(2,1)S(1)}, u32[]{:S(2)}, u32[]{:S(2)}) collective-permute-start(bf16[2,4,120,128]{3,2,0,1:T(8,128)(2,1)S(1)} %pad_maximum_fusion.1), channel_id=1, source_target_pairs={{0,256},{128,384},{256,0},{384,128},{1,257},{129,385},{257,1},{385... | collective-permute-start | bytes 737288 | tf_op jit(solution)/shard_map/ppermute | solution.py:243
  51.1 3.1 %collective-permute-start.4 = (bf16[2,4,120,128]{3,2,1,0:T(8,128)(2,1)S(1)}, bf16[2,4,120,128]{3,2,1,0:T(8,128)(2,1)S(1)}, u32[]{:S(2)}, u32[]{:S(2)}) collective-permute-start(bf16[2,4,120,128]{3,2,1,0:T(8,128)(2,1)S(1)} %pad_maximum_fusion.2), channel_id=1, source_target_pairs={{0,384},{128,0},{256,128},{384,256},{1,385},{129,1},{257,129},{385... | collective-permute-start | bytes 737288 | tf_op jit(solution)/shard_map/ppermute | solution.py:243
  54.2 3.2 %collective-permute-done.2 = bf16[2,4,120,128]{3,2,0,1:T(8,128)(2,1)S(1)} collective-permute-done((bf16[2,4,120,128]{3,2,0,1:T(8,128)(2,1)S(1)}, bf16[2,4,120,128]{3,2,0,1:T(8,128)(2,1)S(1)}, u32[]{:S(2)}, u32[]{:S(2)}) %collective-permute-start.2) | collective-permute-done | bytes 245792 | tf_op jit(solution)/shard_map/ppermute | solution.py:243
  57.4 7.3 %collective-permute-done.3 = bf16[2,4,120,128]{3,2,0,1:T(8,128)(2,1)S(1)} collective-permute-done((bf16[2,4,120,128]{3,2,0,1:T(8,128)(2,1)S(1)}, bf16[2,4,120,128]{3,2,0,1:T(8,128)(2,1)S(1)}, u32[]{:S(2)}, u32[]{:S(2)}) %collective-permute-start.3) | collective-permute-done | bytes 245792 | tf_op jit(solution)/shard_map/ppermute | solution.py:243
  66.2 6.6 %collective-permute-start.7 = (bf16[8,120,128]{2,1,0:T(8,128)(2,1)}, bf16[8,120,128]{2,1,0:T(8,128)(2,1)S(1)}, u32[]{:S(2)}, u32[]{:S(2)}) collective-permute-start(bf16[8,120,128]{2,1,0:T(8,128)(2,1)} %bitcast.35), channel_id=1, source_target_pairs={{0,96},{32,0},{64,32},{96,64},{1,97},{33,1},{65,33},{97,65},{2,98}... | collective-permute-start | bytes 737288 | tf_op jit(solution)/shard_map/ppermute | solution.py:243
  73.5 6.0 %collective-permute-start.6 = (bf16[8,120,128]{2,1,0:T(8,128)(2,1)}, bf16[8,120,128]{2,1,0:T(8,128)(2,1)}, u32[]{:S(2)}, u32[]{:S(2)}) collective-permute-start(bf16[8,120,128]{2,1,0:T(8,128)(2,1)} %bitcast.30), channel_id=1, source_target_pairs={{0,64},{32,96},{64,0},{96,32},{1,65},{33,97},{65,1},{97,33},{2,66}... | collective-permute-start | bytes 737288 | tf_op jit(solution)/shard_map/ppermute | solution.py:243
  80.3 7.3 %collective-permute-start.5 = (bf16[8,120,128]{2,1,0:T(8,128)(2,1)}, bf16[8,120,128]{2,1,0:T(8,128)(2,1)}, u32[]{:S(2)}, u32[]{:S(2)}) collective-permute-start(bf16[8,120,128]{2,1,0:T(8,128)(2,1)} %bitcast.25), channel_id=1, source_target_pairs={{0,32},{32,64},{64,96},{96,0},{1,33},{33,65},{65,97},{97,1},{2,34}... | collective-permute-start | bytes 737288 | tf_op jit(solution)/shard_map/ppermute | solution.py:243
  87.6 1.2 copy-done.7
  88.8 1.0 copy-done.10
  89.9 1.0 shard_map.87
  90.9 1.0 copy-done.8
  92.9 4.4 %all-to-all-start.1 = ((f32[4,128,512]{2,1,0:T(8,128)}), f32[4,128,512]{2,1,0:T(8,128)}, u32[]{:S(2)}, u32[]{:S(2)}) async-start(f32[4,128,512]{2,1,0:T(8,128)} %bitcast.84), calls=%async_computation.1 | async-start | bytes 2097152 | tf_op jit(solution)/shard_map/all_to_all | solution.py:233
  97.3 1.2 copy-done.20
  98.5 3.0 %shard_map.88.back_ref = f32[960,512]{1,0:T(8,128)S(1)} custom-call(bf16[512,1024]{1,0:T(8,128)(2,1)S(1)} %copy-done.20, f32[96,4]{1,0:T(8,128)S(1)} %bitcast.89, bf16[512,512]{1,0:T(8,128)(2,1)S(1)} %bitcast.87), custom_call_target="tpu_custom_call" | custom-call | flops 34359738368 | bytes 4194304 | tf_op jit(solution)/shard_map/pallas_call | solution.py:299
  101.6 3.7 %collective-permute-start.8 = (f32[8,1024]{1,0:T(8,128)S(1)}, f32[8,1024]{1,0:T(8,128)S(1)}, u32[]{:S(2)}, u32[]{:S(2)}) collective-permute-start(f32[8,1024]{1,0:T(8,128)S(1)} %get-tuple-element.33), channel_id=1, source_target_pairs={{16,0},{32,16},{48,32},{64,48},{80,64},{96,80},{112,96},{128,112},... | collective-permute-start | bytes 98312 | tf_op jit(solution)/shard_map/ppermute | solution.py:238
  106.5 4.2 %all-to-all-done.1 = f32[4,128,512]{2,1,0:T(8,128)} async-done(((f32[4,128,512]{2,1,0:T(8,128)}), f32[4,128,512]{2,1,0:T(8,128)}, u32[]{:S(2)}, u32[]{:S(2)}) %all-to-all-start.1) | async-done | bytes 1048608 | tf_op jit(solution)/shard_map/all_to_all | solution.py:233
  110.7 1.3 reduce_sum.9
  112.7 2.2 %collective-permute-start.9 = (f32[64,512]{1,0:T(8,128)}, f32[64,512]{1,0:T(8,128)}, u32[]{:S(2)}, u32[]{:S(2)}) collective-permute-start(f32[64,512]{1,0:T(8,128)} %constant_dynamic-slice_fusion.1), channel_id=1, source_target_pairs={{0,2},{1,3},{2,0},{3,1},{4,6},{5,7},{6,4},{7,5},{8,10},{9,11},{10,... | collective-permute-start | bytes 393224 | tf_op jit(solution)/shard_map/ppermute | solution.py:259
  115.9 2.7 %shard_map.93 = f32[128,128]{1,0:T(8,128)} custom-call(s32[3]{0:T(128)S(1)} %pad_add_fusion.place_ref, bf16[8,120,128]{2,1,0:T(8,128)(2,1)S(1)} %bitcast.82, bf16[8,120,128]{2,1,0:T(8,128)(2,1)} %collective-permute-done.5.in1_ref, bf16[8,120,128]{2,1,0:T(8,128)(2,1)} %collective-permute-done.6.in2_ref, ...), custom_call_target="tpu_custom_call" | custom-call | flops 536870912 | bytes 4194304 | tf_op jit(solution)/shard_map/pallas_call | solution.py:312
  118.5 19.8 %all-to-all-start.2 = ((f32[16,8,128]{2,1,0:T(8,128)}), f32[16,8,128]{2,1,0:T(8,128)S(1)}, u32[]{:S(2)}, u32[]{:S(2)}) async-start(f32[16,8,128]{2,1,0:T(8,128)} %bitcast.40), calls=%async_computation.2 | async-start | bytes 131072 | tf_op jit(solution)/shard_map/all_to_all | solution.py:233
  138.4 1.0 dynamic-slice_add_fusion
  140.0 3.3 %collective-permute-start.10 = (f32[32,512]{1,0:T(8,128)}, f32[32,512]{1,0:T(8,128)S(1)}, u32[]{:S(2)}, u32[]{:S(2)}) collective-permute-start(f32[32,512]{1,0:T(8,128)} %constant_dynamic-slice_fusion), channel_id=1, source_target_pairs={{0,1},{1,0},{2,3},{3,2},{4,5},{5,4},{6,7},{7,6},{8,9},{9,8},{10,11... | collective-permute-start | bytes 196616 | tf_op jit(solution)/shard_map/ppermute | solution.py:259
  143.3 1.5 %copy-done.5 = f32[960,512]{1,0:T(8,128)S(1)} copy-done((f32[960,512]{1,0:T(8,128)S(1)}, f32[960,512]{1,0:T(8,128)}, u32[]{:S(2)}) %copy-start.5) | copy-done | bytes 1966104
  144.8 4.5 %shard_map.92 = (bf16[960,512]{1,0:T(8,128)(2,1)}, bf16[960,512]{1,0:T(8,128)(2,1)}) custom-call(s32[3]{0:T(128)S(1)} %pad_add_fusion.place_ref, bf16[8,120,128]{2,1,0:T(8,128)(2,1)S(1)} %bitcast.83, bf16[8,120,128]{2,1,0:T(8,128)(2,1)} %collective-permute-done.5.in1_ref, bf16[8,120,128]{2,1,0:T(8,128)(2,1)} %collective-permute-done.6.in2_ref, ...), custom_call_target="tpu_custom_call" | custom-call | flops 536870912 | bytes 4194304 | tf_op jit(solution)/shard_map/pallas_call | solution.py:318
  (81 shorter events, 14.3 us)
Async XLA Ops:
  0.6 1.2 copy-start
  1.8 10.5 %copy-start.2 = (bf16[10,96,512]{2,1,0:T(8,128)(2,1)S(1)}, bf16[10,96,512]{2,1,0:T(8,128)(2,1)}, u32[]{:S(2)}) copy-start(bf16[10,96,512]{2,1,0:T(8,128)(2,1)} %param.9) | copy-start | bytes 2949124
  1.8 10.6 %copy-start.17 = (bf16[16,32,32]{2,1,0:T(8,128)(2,1)S(1)}, bf16[16,32,32]{2,1,0:T(8,128)(2,1)}, u32[]{:S(2)}) copy-start(bf16[16,32,32]{2,1,0:T(8,128)(2,1)} %param.8) | copy-start | bytes 98308
  2.0 12.9 %collective-permute-start = (bf16[16,960]{1,0:T(8,128)(2,1)S(1)}, bf16[16,960]{1,0:T(8,128)(2,1)S(1)}, u32[]{:S(2)}, u32[]{:S(2)}) collective-permute-start(bf16[16,960]{1,0:T(8,128)(2,1)S(1)} %shard_map.85), channel_id=1, source_target_pairs={{0,16},{16,32},{32,48},{48,64},{64,80},{80,96},{96,112},{112,128},... | collective-permute-start | bytes 92168 | tf_op jit(solution)/shard_map/ppermute | solution.py:238
  12.4 18.9 %copy-start.26 = (f32[4,96]{1,0:T(4,128)S(1)}, f32[4,96]{1,0:T(4,128)}, u32[]{:S(2)}) copy-start(f32[4,96]{1,0:T(4,128)} %param.6) | copy-start | bytes 4612
  12.4 19.1 %copy-start.1 = (bf16[10,96,512]{2,1,0:T(8,128)(2,1)S(1)}, bf16[10,96,512]{2,1,0:T(8,128)(2,1)}, u32[]{:S(2)}) copy-start(bf16[10,96,512]{2,1,0:T(8,128)(2,1)} %param.5) | copy-start | bytes 2949124
  12.4 19.1 %copy-start.9 = (bf16[1,512,512]{2,1,0:T(8,128)(2,1)S(1)}, bf16[1,512,512]{2,1,0:T(8,128)(2,1)}, u32[]{:S(2)}) copy-start(bf16[1,512,512]{2,1,0:T(8,128)(2,1)} %param.7) | copy-start | bytes 1572868
  15.6 72.0 %all-to-all-start = ((bf16[32,120,128]{2,1,0:T(8,128)(2,1)}), bf16[32,120,128]{2,1,0:T(8,128)(2,1)S(1)}, u32[]{:S(2)}, u32[]{:S(2)}) async-start(bf16[32,120,128]{2,1,0:T(8,128)(2,1)} %copy-done.3), calls=%async_computation | async-start | bytes 1966080 | tf_op jit(solution)/shard_map/all_to_all | solution.py:233
  39.4 4.0 %collective-permute-start.1 = (bf16[16,120,128]{2,1,0:T(8,128)(2,1)}, bf16[16,120,128]{2,1,0:T(8,128)(2,1)S(1)}, u32[]{:S(2)}, u32[]{:S(2)}) collective-permute-start(bf16[16,120,128]{2,1,0:T(8,128)(2,1)} %get-tuple-element.30), channel_id=1, source_target_pairs={{0,16},{16,0},{1,17},{17,1},{2,18},{18,2},{3,19},{19,3},{4,20},{20... | collective-permute-start | bytes 1474568 | tf_op jit(solution)/shard_map/ppermute | solution.py:243
  43.4 14.0 %collective-permute-start.2 = (bf16[2,4,120,128]{3,2,0,1:T(8,128)(2,1)S(1)}, bf16[2,4,120,128]{3,2,0,1:T(8,128)(2,1)S(1)}, u32[]{:S(2)}, u32[]{:S(2)}) collective-permute-start(bf16[2,4,120,128]{3,2,0,1:T(8,128)(2,1)S(1)} %pad_maximum_fusion), channel_id=1, source_target_pairs={{0,128},{128,256},{256,384},{384,0},{1,129},{129,257},{257,385},{3... | collective-permute-start | bytes 737288 | tf_op jit(solution)/shard_map/ppermute | solution.py:243
  46.7 18.0 %collective-permute-start.3 = (bf16[2,4,120,128]{3,2,0,1:T(8,128)(2,1)S(1)}, bf16[2,4,120,128]{3,2,0,1:T(8,128)(2,1)S(1)}, u32[]{:S(2)}, u32[]{:S(2)}) collective-permute-start(bf16[2,4,120,128]{3,2,0,1:T(8,128)(2,1)S(1)} %pad_maximum_fusion.1), channel_id=1, source_target_pairs={{0,256},{128,384},{256,0},{384,128},{1,257},{129,385},{257,1},{385... | collective-permute-start | bytes 737288 | tf_op jit(solution)/shard_map/ppermute | solution.py:243
  51.1 14.4 %collective-permute-start.4 = (bf16[2,4,120,128]{3,2,1,0:T(8,128)(2,1)S(1)}, bf16[2,4,120,128]{3,2,1,0:T(8,128)(2,1)S(1)}, u32[]{:S(2)}, u32[]{:S(2)}) collective-permute-start(bf16[2,4,120,128]{3,2,1,0:T(8,128)(2,1)S(1)} %pad_maximum_fusion.2), channel_id=1, source_target_pairs={{0,384},{128,0},{256,128},{384,256},{1,385},{129,1},{257,129},{385... | collective-permute-start | bytes 737288 | tf_op jit(solution)/shard_map/ppermute | solution.py:243
  66.2 49.4 %collective-permute-start.7 = (bf16[8,120,128]{2,1,0:T(8,128)(2,1)}, bf16[8,120,128]{2,1,0:T(8,128)(2,1)S(1)}, u32[]{:S(2)}, u32[]{:S(2)}) collective-permute-start(bf16[8,120,128]{2,1,0:T(8,128)(2,1)} %bitcast.35), channel_id=1, source_target_pairs={{0,96},{32,0},{64,32},{96,64},{1,97},{33,1},{65,33},{97,65},{2,98}... | collective-permute-start | bytes 737288 | tf_op jit(solution)/shard_map/ppermute | solution.py:243
  73.5 42.1 %collective-permute-start.6 = (bf16[8,120,128]{2,1,0:T(8,128)(2,1)}, bf16[8,120,128]{2,1,0:T(8,128)(2,1)}, u32[]{:S(2)}, u32[]{:S(2)}) collective-permute-start(bf16[8,120,128]{2,1,0:T(8,128)(2,1)} %bitcast.30), channel_id=1, source_target_pairs={{0,64},{32,96},{64,0},{96,32},{1,65},{33,97},{65,1},{97,33},{2,66}... | collective-permute-start | bytes 737288 | tf_op jit(solution)/shard_map/ppermute | solution.py:243
  80.3 35.4 %collective-permute-start.5 = (bf16[8,120,128]{2,1,0:T(8,128)(2,1)}, bf16[8,120,128]{2,1,0:T(8,128)(2,1)}, u32[]{:S(2)}, u32[]{:S(2)}) collective-permute-start(bf16[8,120,128]{2,1,0:T(8,128)(2,1)} %bitcast.25), channel_id=1, source_target_pairs={{0,32},{32,64},{64,96},{96,0},{1,33},{33,65},{65,97},{97,1},{2,34}... | collective-permute-start | bytes 737288 | tf_op jit(solution)/shard_map/ppermute | solution.py:243
  87.6 1.2 copy-start.7
  88.8 1.0 copy-start.10
  90.9 1.0 copy-start.8
  92.9 4.4 %copy-start.11 = (bf16[1,512,512]{2,1,0:T(8,128)(2,1)S(1)}, bf16[1,512,512]{2,1,0:T(8,128)(2,1)}, u32[]{:S(2)}) copy-start(bf16[1,512,512]{2,1,0:T(8,128)(2,1)} %param.7) | copy-start | bytes 1572868
  92.9 17.8 %all-to-all-start.1 = ((f32[4,128,512]{2,1,0:T(8,128)}), f32[4,128,512]{2,1,0:T(8,128)}, u32[]{:S(2)}, u32[]{:S(2)}) async-start(f32[4,128,512]{2,1,0:T(8,128)} %bitcast.84), calls=%async_computation.1 | async-start | bytes 2097152 | tf_op jit(solution)/shard_map/all_to_all | solution.py:233
  97.3 1.2 copy-start.20
  101.5 3.9 %copy-start.4 = (f32[960,512]{1,0:T(8,128)}, f32[960,512]{1,0:T(8,128)S(1)}, u32[]{:S(2)}) copy-start(f32[960,512]{1,0:T(8,128)S(1)} %shard_map.88.back_ref) | copy-start | bytes 5898244
  101.6 14.3 %collective-permute-start.8 = (f32[8,1024]{1,0:T(8,128)S(1)}, f32[8,1024]{1,0:T(8,128)S(1)}, u32[]{:S(2)}, u32[]{:S(2)}) collective-permute-start(f32[8,1024]{1,0:T(8,128)S(1)} %get-tuple-element.33), channel_id=1, source_target_pairs={{16,0},{32,16},{48,32},{64,48},{80,64},{96,80},{112,96},{128,112},... | collective-permute-start | bytes 98312 | tf_op jit(solution)/shard_map/ppermute | solution.py:238
  106.3 8.7 %copy-start.18 = (bf16[16,32,32]{2,1,0:T(8,128)(2,1)S(1)}, bf16[16,32,32]{2,1,0:T(8,128)(2,1)}, u32[]{:S(2)}) copy-start(bf16[16,32,32]{2,1,0:T(8,128)(2,1)} %param.8) | copy-start | bytes 98308
  106.5 5.5 %copy-start.14 = (bf16[512,512]{1,0:T(8,128)(2,1)}, bf16[512,512]{1,0:T(8,128)(2,1)S(1)}, u32[]{:S(2)}) copy-start(bf16[512,512]{1,0:T(8,128)(2,1)S(1)} %shard_map.90.rear_ref) | copy-start | bytes 1572868
  112.0 3.7 %copy-start.23 = (f32[128,512]{1,0:T(8,128)}, f32[128,512]{1,0:T(8,128)S(1)}, u32[]{:S(2)}) copy-start(f32[128,512]{1,0:T(8,128)S(1)} %reduce_sum.9) | copy-start | bytes 786436
  112.7 3.1 %copy-start.13 = (bf16[512,512]{1,0:T(8,128)(2,1)S(1)}, bf16[512,512]{1,0:T(8,128)(2,1)}, u32[]{:S(2)}) copy-start(bf16[512,512]{1,0:T(8,128)(2,1)} %copy-done.12) | copy-start | bytes 1572868
  112.7 3.1 %copy-start.15 = (bf16[512,512]{1,0:T(8,128)(2,1)S(1)}, bf16[512,512]{1,0:T(8,128)(2,1)}, u32[]{:S(2)}) copy-start(bf16[512,512]{1,0:T(8,128)(2,1)} %copy-done.14) | copy-start | bytes 1572868
  112.7 25.6 %collective-permute-start.9 = (f32[64,512]{1,0:T(8,128)}, f32[64,512]{1,0:T(8,128)}, u32[]{:S(2)}, u32[]{:S(2)}) collective-permute-start(f32[64,512]{1,0:T(8,128)} %constant_dynamic-slice_fusion.1), channel_id=1, source_target_pairs={{0,2},{1,3},{2,0},{3,1},{4,6},{5,7},{6,4},{7,5},{8,10},{9,11},{10,... | collective-permute-start | bytes 393224 | tf_op jit(solution)/shard_map/ppermute | solution.py:259
  118.5 30.8 %all-to-all-start.2 = ((f32[16,8,128]{2,1,0:T(8,128)}), f32[16,8,128]{2,1,0:T(8,128)S(1)}, u32[]{:S(2)}, u32[]{:S(2)}) async-start(f32[16,8,128]{2,1,0:T(8,128)} %bitcast.40), calls=%async_computation.2 | async-start | bytes 131072 | tf_op jit(solution)/shard_map/all_to_all | solution.py:233
  140.0 10.0 %collective-permute-start.10 = (f32[32,512]{1,0:T(8,128)}, f32[32,512]{1,0:T(8,128)S(1)}, u32[]{:S(2)}, u32[]{:S(2)}) collective-permute-start(f32[32,512]{1,0:T(8,128)} %constant_dynamic-slice_fusion), channel_id=1, source_target_pairs={{0,1},{1,0},{2,3},{3,2},{4,5},{5,4},{6,7},{7,6},{8,9},{9,8},{10,11... | collective-permute-start | bytes 196616 | tf_op jit(solution)/shard_map/ppermute | solution.py:259
  143.3 1.5 %copy-start.5 = (f32[960,512]{1,0:T(8,128)S(1)}, f32[960,512]{1,0:T(8,128)}, u32[]{:S(2)}) copy-start(f32[960,512]{1,0:T(8,128)} %copy-done.4) | copy-start | bytes 5898244
  (9 other events, 7.5 us)

commit v5 on v4

--- a/solution.py
+++ b/solution.py
@@ -251,11 +251,11 @@
     return [jnp.stack([part[:, step] for part in both]).reshape(8, 120, LANES) for step in range(4)]
 
 
-def halves_met(part, axis, apart):
-    rows = part.shape[0] // 2
+def halves_met(part, axis, apart, along):
+    size = part.shape[along] // 2
     upper = lax.axis_index(axis) // apart % 2
-    mine = lax.dynamic_slice_in_dim(part, upper * rows, rows, 0)
-    other = lax.dynamic_slice_in_dim(part, (1 - upper) * rows, rows, 0)
+    mine = lax.dynamic_slice_in_dim(part, upper * size, size, along)
+    other = lax.dynamic_slice_in_dim(part, (1 - upper) * size, size, along)
     return mine, lax.ppermute(other, axis, [(s, s ^ apart) for s in range(lax.axis_size(axis))])
 
 
@@ -299,7 +299,7 @@
     (conv_back,) = call(dconv_kernel, [((960, 512), F32)], flops=1 << 35)(dfirst, taps, left)
     left_sum = jnp.sum(exchange(left_part.reshape(4, 128, 512), "x"), 0)
     left_sum = lax.optimization_barrier((left_sum, conv_back))[0]
-    kept, met = halves_met(left_sum, "zl", 2)
+    kept, met = halves_met(left_sum.reshape(2, 2, 32, 512), "zl", 1, 1)
     late = lax.optimization_barrier((x, cot, right, dedge))
     (wide,) = call(wide_kernel, [((512, 512), BF16)], flops=1 << 31)(late[2])
     (front,) = call(front_gate_kernel, [((512, 512), BF16)], flops=1 << 31)(*late[:2])
@@ -314,7 +314,7 @@
     )
     right_all = exchange(right_part.reshape(16, 8, LANES), CHAN)
     met = lax.optimization_barrier((met, right_part))[0]
-    left_grad = sum(halves_met(kept + met, "zl", 1))
+    left_grad = sum(halves_met(kept + met, "zl", 2, 0))
     mixed, frames_grad = call(
         end_kernel, [((960, 512), BF16), ((960, 512), BF16)], scratch=scratch, scalars=1, arrays=10
     )(place, *columns, wide, x, cot, conv_back, after, taps)

time: 152 us -> 149 us (0.980)
  starting transfers between devices: 92.1 us -> 89.3 us
    all_to_all x3, starting transfers between devices: 39.9 us -> 33.2 us  [exchange(): return lax.all_to_all(value, axes, split_axis=0, concat_axis=0, tiled=True)]
    ppermute x2, starting transfers between devices: 5.48 us -> 9.39 us  [halves_met(): lax.ppermute(other, axis, [(s, s ^ apart) for s in range(lax.axis_size(ax...]
  transfers between devices with their start and end apart: 14 -> 14, of which waited for: 6 -> 5; matrix products, arithmetic and copies ran while one was open for 5% -> 5% of each run, Pallas kernels for 13% -> 13%
where the time goes in v5:
time: 149 us; the launch traced here: 148 us
  starting transfers between devices  89.3 us (60%)
  Pallas kernels  20 us (13%)
  local copies, waits for them, and re-layouts  16.1 us (11%)
  waiting for transfers between devices  16 us (11%)
  other arithmetic  5.38 us (4%)
    all_to_all x3, starting transfers between devices, exchange(): return lax.all_to_all(value, axes, split_axis=0, concat_axis=0, tiled=True)  33.2 us
    ppermute x7, starting transfers between devices, ahead(): lax.ppermute(value, axis, [(s, (s + step) % count) for s in range(count)])  32.7 us
    ppermute x2, starting transfers between devices, along_seq(): return lax.ppermute(value, SEQ, pairs)  14 us
    unnamed x55, local copies, waits for them, and re-layouts  13.5 us
    ppermute x7, waiting for transfers between devices, ahead(): lax.ppermute(value, axis, [(s, (s + step) % count) for s in range(count)])  11.9 us
    ppermute x2, starting transfers between devices, halves_met(): lax.ppermute(other, axis, [(s, s ^ apart) for s in range(lax.axis_size(ax...  9.39 us
    pallas_call x1, Pallas kernels, shards(): call(conv_kernel, [((1024, 512), BF16), part, part], scratch=[pltpu.VMEM(...  5.28 us
    pallas_call x1, Pallas kernels, shards(): call(end_kernel, [((960, 512), BF16), ((960, 512), BF16)], scratch=scratc...  4.5 us
  transfers between devices with their start and end apart: 14, of which 5 were waited for; matrix products, arithmetic and copies ran while one was open for 5% of the time, Pallas kernels for 13%

profile of v5, /device:TPU:1, one launch (start us, length us, event | category | flops | bytes accessed | tf_op | source)
XLA Modules:
  0.0 148.0 jit_solution(2462571308474972982)
XLA Ops:
  0.6 1.2 copy-done
  2.0 10.4 %collective-permute-start = (bf16[16,960]{1,0:T(8,128)(2,1)S(1)}, bf16[16,960]{1,0:T(8,128)(2,1)S(1)}, u32[]{:S(2)}, u32[]{:S(2)}) collective-permute-start(bf16[16,960]{1,0:T(8,128)(2,1)S(1)} %shard_map.85), channel_id=1, source_target_pairs={{0,16},{16,32},{32,48},{48,64},{64,80},{80,96},{96,112},{112,128},... | collective-permute-start | bytes 92168 | tf_op jit(solution)/shard_map/ppermute | solution.py:238
  12.4 1.6 %shard_map.84 = bf16[32,120,128]{2,1,0:T(8,128)(2,1)S(1)} custom-call(bf16[960,512]{1,0:T(8,128)(2,1)S(1)} %bitcast.74, bf16[960,512]{1,0:T(8,128)(2,1)S(1)} %bitcast.79, bf16[512,32]{1,0:T(8,128)(2,1)S(1)} %bitcast.92), custom_call_target="tpu_custom_call" | custom-call | flops 536870912 | bytes 4194304 | tf_op jit(solution)/shard_map/pallas_call | solution.py:280
  15.6 15.7 %all-to-all-start = ((bf16[32,120,128]{2,1,0:T(8,128)(2,1)}), bf16[32,120,128]{2,1,0:T(8,128)(2,1)S(1)}, u32[]{:S(2)}, u32[]{:S(2)}) async-start(bf16[32,120,128]{2,1,0:T(8,128)(2,1)} %copy-done.3), calls=%async_computation | async-start | bytes 1966080 | tf_op jit(solution)/shard_map/all_to_all | solution.py:233
  32.3 5.3 %shard_map.86 = (bf16[1024,512]{1,0:T(8,128)(2,1)S(1)}, bf16[16,120,128]{2,1,0:T(8,128)(2,1)S(1)}, bf16[16,120,128]{2,1,0:T(8,128)(2,1)}) custom-call(s32[3]{0:T(128)S(1)} %pad_add_fusion.place_ref, bf16[960,512]{1,0:T(8,128)(2,1)S(1)} %bitcast.75, bf16[16,960]{1,0:T(8,128)(2,1)S(1)} %copy-done.22, f32[96,4]{1,0:T(8,128)S(1)} %bitcast.89, ...), custom_call_target="tpu_custom_call" | custom-call | flops 536870912 | bytes 4194304 | tf_op jit(solution)/shard_map/pallas_call | solution.py:285
  39.4 2.1 %collective-permute-start.1 = (bf16[16,120,128]{2,1,0:T(8,128)(2,1)}, bf16[16,120,128]{2,1,0:T(8,128)(2,1)S(1)}, u32[]{:S(2)}, u32[]{:S(2)}) collective-permute-start(bf16[16,120,128]{2,1,0:T(8,128)(2,1)} %get-tuple-element.30), channel_id=1, source_target_pairs={{0,16},{16,0},{1,17},{17,1},{2,18},{18,2},{3,19},{19,3},{4,20},{20... | collective-permute-start | bytes 1474568 | tf_op jit(solution)/shard_map/ppermute | solution.py:243
  41.6 1.1 slice_bitcast_fusion.7
  43.4 3.3 %collective-permute-start.2 = (bf16[2,4,120,128]{3,2,0,1:T(8,128)(2,1)S(1)}, bf16[2,4,120,128]{3,2,0,1:T(8,128)(2,1)S(1)}, u32[]{:S(2)}, u32[]{:S(2)}) collective-permute-start(bf16[2,4,120,128]{3,2,0,1:T(8,128)(2,1)S(1)} %pad_maximum_fusion), channel_id=1, source_target_pairs={{0,128},{128,256},{256,384},{384,0},{1,129},{129,257},{257,385},{3... | collective-permute-start | bytes 737288 | tf_op jit(solution)/shard_map/ppermute | solution.py:243
  46.7 4.3 %collective-permute-start.3 = (bf16[2,4,120,128]{3,2,0,1:T(8,128)(2,1)S(1)}, bf16[2,4,120,128]{3,2,0,1:T(8,128)(2,1)S(1)}, u32[]{:S(2)}, u32[]{:S(2)}) collective-permute-start(bf16[2,4,120,128]{3,2,0,1:T(8,128)(2,1)S(1)} %pad_maximum_fusion.1), channel_id=1, source_target_pairs={{0,256},{128,384},{256,0},{384,128},{1,257},{129,385},{257,1},{385... | collective-permute-start | bytes 737288 | tf_op jit(solution)/shard_map/ppermute | solution.py:243
  51.1 3.1 %collective-permute-start.4 = (bf16[2,4,120,128]{3,2,1,0:T(8,128)(2,1)S(1)}, bf16[2,4,120,128]{3,2,1,0:T(8,128)(2,1)S(1)}, u32[]{:S(2)}, u32[]{:S(2)}) collective-permute-start(bf16[2,4,120,128]{3,2,1,0:T(8,128)(2,1)S(1)} %pad_maximum_fusion.2), channel_id=1, source_target_pairs={{0,384},{128,0},{256,128},{384,256},{1,385},{129,1},{257,129},{385... | collective-permute-start | bytes 737288 | tf_op jit(solution)/shard_map/ppermute | solution.py:243
  54.2 3.2 %collective-permute-done.2 = bf16[2,4,120,128]{3,2,0,1:T(8,128)(2,1)S(1)} collective-permute-done((bf16[2,4,120,128]{3,2,0,1:T(8,128)(2,1)S(1)}, bf16[2,4,120,128]{3,2,0,1:T(8,128)(2,1)S(1)}, u32[]{:S(2)}, u32[]{:S(2)}) %collective-permute-start.2) | collective-permute-done | bytes 245792 | tf_op jit(solution)/shard_map/ppermute | solution.py:243
  57.4 7.3 %collective-permute-done.3 = bf16[2,4,120,128]{3,2,0,1:T(8,128)(2,1)S(1)} collective-permute-done((bf16[2,4,120,128]{3,2,0,1:T(8,128)(2,1)S(1)}, bf16[2,4,120,128]{3,2,0,1:T(8,128)(2,1)S(1)}, u32[]{:S(2)}, u32[]{:S(2)}) %collective-permute-start.3) | collective-permute-done | bytes 245792 | tf_op jit(solution)/shard_map/ppermute | solution.py:243
  66.2 6.6 %collective-permute-start.7 = (bf16[8,120,128]{2,1,0:T(8,128)(2,1)}, bf16[8,120,128]{2,1,0:T(8,128)(2,1)S(1)}, u32[]{:S(2)}, u32[]{:S(2)}) collective-permute-start(bf16[8,120,128]{2,1,0:T(8,128)(2,1)} %bitcast.35), channel_id=1, source_target_pairs={{0,96},{32,0},{64,32},{96,64},{1,97},{33,1},{65,33},{97,65},{2,98}... | collective-permute-start | bytes 737288 | tf_op jit(solution)/shard_map/ppermute | solution.py:243
  73.5 6.0 %collective-permute-start.6 = (bf16[8,120,128]{2,1,0:T(8,128)(2,1)}, bf16[8,120,128]{2,1,0:T(8,128)(2,1)}, u32[]{:S(2)}, u32[]{:S(2)}) collective-permute-start(bf16[8,120,128]{2,1,0:T(8,128)(2,1)} %bitcast.30), channel_id=1, source_target_pairs={{0,64},{32,96},{64,0},{96,32},{1,65},{33,97},{65,1},{97,33},{2,66}... | collective-permute-start | bytes 737288 | tf_op jit(solution)/shard_map/ppermute | solution.py:243
  80.3 7.3 %collective-permute-start.5 = (bf16[8,120,128]{2,1,0:T(8,128)(2,1)}, bf16[8,120,128]{2,1,0:T(8,128)(2,1)}, u32[]{:S(2)}, u32[]{:S(2)}) collective-permute-start(bf16[8,120,128]{2,1,0:T(8,128)(2,1)} %bitcast.25), channel_id=1, source_target_pairs={{0,32},{32,64},{64,96},{96,0},{1,33},{33,65},{65,97},{97,1},{2,34}... | collective-permute-start | bytes 737288 | tf_op jit(solution)/shard_map/ppermute | solution.py:243
  87.6 1.2 copy-done.7
  88.8 1.0 copy-done.10
  89.9 1.0 shard_map.87
  90.9 1.0 copy-done.8
  92.9 4.4 %all-to-all-start.1 = ((f32[4,128,512]{2,1,0:T(8,128)}), f32[4,128,512]{2,1,0:T(8,128)}, u32[]{:S(2)}, u32[]{:S(2)}) async-start(f32[4,128,512]{2,1,0:T(8,128)} %bitcast.85), calls=%async_computation.1 | async-start | bytes 2097152 | tf_op jit(solution)/shard_map/all_to_all | solution.py:233
  97.3 1.2 copy-done.20
  98.5 3.0 %shard_map.88.back_ref = f32[960,512]{1,0:T(8,128)S(1)} custom-call(bf16[512,1024]{1,0:T(8,128)(2,1)S(1)} %copy-done.20, f32[96,4]{1,0:T(8,128)S(1)} %bitcast.90, bf16[512,512]{1,0:T(8,128)(2,1)S(1)} %bitcast.88), custom_call_target="tpu_custom_call" | custom-call | flops 34359738368 | bytes 4194304 | tf_op jit(solution)/shard_map/pallas_call | solution.py:299
  101.6 3.7 %collective-permute-start.8 = (f32[8,1024]{1,0:T(8,128)S(1)}, f32[8,1024]{1,0:T(8,128)S(1)}, u32[]{:S(2)}, u32[]{:S(2)}) collective-permute-start(f32[8,1024]{1,0:T(8,128)S(1)} %get-tuple-element.33), channel_id=1, source_target_pairs={{16,0},{32,16},{48,32},{64,48},{80,64},{96,80},{112,96},{128,112},... | collective-permute-start | bytes 98312 | tf_op jit(solution)/shard_map/ppermute | solution.py:238
  106.5 4.2 %all-to-all-done.1 = f32[4,128,512]{2,1,0:T(8,128)} async-done(((f32[4,128,512]{2,1,0:T(8,128)}), f32[4,128,512]{2,1,0:T(8,128)}, u32[]{:S(2)}, u32[]{:S(2)}) %all-to-all-start.1) | async-done | bytes 1048608 | tf_op jit(solution)/shard_map/all_to_all | solution.py:233
  110.7 1.3 reduce_sum.9
  112.7 5.2 %collective-permute-start.9 = (f32[2,1,32,512]{3,2,1,0:T(8,128)}, f32[2,1,32,512]{3,2,1,0:T(8,128)}, u32[]{:S(2)}, u32[]{:S(2)}) collective-permute-start(f32[2,1,32,512]{3,2,1,0:T(8,128)} %constant_dynamic-slice_fusion.1), channel_id=1, source_target_pairs={{0,1},{1,0},{2,3},{3,2},{4,5},{5,4},{6,7},{7,6},{8,9},{9,8},{10,11... | collective-permute-start | bytes 393224 | tf_op jit(solution)/shard_map/ppermute | solution.py:259
  118.8 2.7 %shard_map.93 = f32[128,128]{1,0:T(8,128)} custom-call(s32[3]{0:T(128)S(1)} %pad_add_fusion.place_ref, bf16[8,120,128]{2,1,0:T(8,128)(2,1)S(1)} %bitcast.83, bf16[8,120,128]{2,1,0:T(8,128)(2,1)} %collective-permute-done.5.in1_ref, bf16[8,120,128]{2,1,0:T(8,128)(2,1)} %collective-permute-done.6.in2_ref, ...), custom_call_target="tpu_custom_call" | custom-call | flops 536870912 | bytes 4194304 | tf_op jit(solution)/shard_map/pallas_call | solution.py:312
  121.5 13.1 %all-to-all-start.2 = ((f32[16,8,128]{2,1,0:T(8,128)}), f32[16,8,128]{2,1,0:T(8,128)S(1)}, u32[]{:S(2)}, u32[]{:S(2)}) async-start(f32[16,8,128]{2,1,0:T(8,128)} %bitcast.41), calls=%async_computation.2 | async-start | bytes 131072 | tf_op jit(solution)/shard_map/all_to_all | solution.py:233
  134.6 1.0 dynamic-slice_add_fusion
  136.3 4.2 %collective-permute-start.10 = (f32[1,1,32,512]{3,2,1,0:T(8,128)}, f32[1,1,32,512]{3,2,1,0:T(8,128)S(1)}, u32[]{:S(2)}, u32[]{:S(2)}) collective-permute-start(f32[1,1,32,512]{3,2,1,0:T(8,128)} %constant_dynamic-slice_fusion), channel_id=1, source_target_pairs={{0,2},{1,3},{2,0},{3,1},{4,6},{5,7},{6,4},{7,5},{8,10},{9,11},{10,... | collective-permute-start | bytes 196616 | tf_op jit(solution)/shard_map/ppermute | solution.py:259
  140.4 1.5 %copy-done.5 = f32[960,512]{1,0:T(8,128)S(1)} copy-done((f32[960,512]{1,0:T(8,128)S(1)}, f32[960,512]{1,0:T(8,128)}, u32[]{:S(2)}) %copy-start.5) | copy-done | bytes 1966104
  142.0 4.5 %shard_map.92 = (bf16[960,512]{1,0:T(8,128)(2,1)}, bf16[960,512]{1,0:T(8,128)(2,1)}) custom-call(s32[3]{0:T(128)S(1)} %pad_add_fusion.place_ref, bf16[8,120,128]{2,1,0:T(8,128)(2,1)S(1)} %bitcast.84, bf16[8,120,128]{2,1,0:T(8,128)(2,1)} %collective-permute-done.5.in1_ref, bf16[8,120,128]{2,1,0:T(8,128)(2,1)} %collective-permute-done.6.in2_ref, ...), custom_call_target="tpu_custom_call" | custom-call | flops 536870912 | bytes 4194304 | tf_op jit(solution)/shard_map/pallas_call | solution.py:318
  (81 shorter events, 14.2 us)
Async XLA Ops:
  0.6 1.2 copy-start
  1.8 10.5 %copy-start.2 = (bf16[10,96,512]{2,1,0:T(8,128)(2,1)S(1)}, bf16[10,96,512]{2,1,0:T(8,128)(2,1)}, u32[]{:S(2)}) copy-start(bf16[10,96,512]{2,1,0:T(8,128)(2,1)} %param.9) | copy-start | bytes 2949124
  1.8 10.6 %copy-start.17 = (bf16[16,32,32]{2,1,0:T(8,128)(2,1)S(1)}, bf16[16,32,32]{2,1,0:T(8,128)(2,1)}, u32[]{:S(2)}) copy-start(bf16[16,32,32]{2,1,0:T(8,128)(2,1)} %param.8) | copy-start | bytes 98308
  2.0 12.9 %collective-permute-start = (bf16[16,960]{1,0:T(8,128)(2,1)S(1)}, bf16[16,960]{1,0:T(8,128)(2,1)S(1)}, u32[]{:S(2)}, u32[]{:S(2)}) collective-permute-start(bf16[16,960]{1,0:T(8,128)(2,1)S(1)} %shard_map.85), channel_id=1, source_target_pairs={{0,16},{16,32},{32,48},{48,64},{64,80},{80,96},{96,112},{112,128},... | collective-permute-start | bytes 92168 | tf_op jit(solution)/shard_map/ppermute | solution.py:238
  12.4 18.9 %copy-start.26 = (f32[4,96]{1,0:T(4,128)S(1)}, f32[4,96]{1,0:T(4,128)}, u32[]{:S(2)}) copy-start(f32[4,96]{1,0:T(4,128)} %param.6) | copy-start | bytes 4612
  12.4 19.1 %copy-start.1 = (bf16[10,96,512]{2,1,0:T(8,128)(2,1)S(1)}, bf16[10,96,512]{2,1,0:T(8,128)(2,1)}, u32[]{:S(2)}) copy-start(bf16[10,96,512]{2,1,0:T(8,128)(2,1)} %param.5) | copy-start | bytes 2949124
  12.4 19.1 %copy-start.9 = (bf16[1,512,512]{2,1,0:T(8,128)(2,1)S(1)}, bf16[1,512,512]{2,1,0:T(8,128)(2,1)}, u32[]{:S(2)}) copy-start(bf16[1,512,512]{2,1,0:T(8,128)(2,1)} %param.7) | copy-start | bytes 1572868
  15.6 72.0 %all-to-all-start = ((bf16[32,120,128]{2,1,0:T(8,128)(2,1)}), bf16[32,120,128]{2,1,0:T(8,128)(2,1)S(1)}, u32[]{:S(2)}, u32[]{:S(2)}) async-start(bf16[32,120,128]{2,1,0:T(8,128)(2,1)} %copy-done.3), calls=%async_computation | async-start | bytes 1966080 | tf_op jit(solution)/shard_map/all_to_all | solution.py:233
  39.4 4.0 %collective-permute-start.1 = (bf16[16,120,128]{2,1,0:T(8,128)(2,1)}, bf16[16,120,128]{2,1,0:T(8,128)(2,1)S(1)}, u32[]{:S(2)}, u32[]{:S(2)}) collective-permute-start(bf16[16,120,128]{2,1,0:T(8,128)(2,1)} %get-tuple-element.30), channel_id=1, source_target_pairs={{0,16},{16,0},{1,17},{17,1},{2,18},{18,2},{3,19},{19,3},{4,20},{20... | collective-permute-start | bytes 1474568 | tf_op jit(solution)/shard_map/ppermute | solution.py:243
  43.4 14.0 %collective-permute-start.2 = (bf16[2,4,120,128]{3,2,0,1:T(8,128)(2,1)S(1)}, bf16[2,4,120,128]{3,2,0,1:T(8,128)(2,1)S(1)}, u32[]{:S(2)}, u32[]{:S(2)}) collective-permute-start(bf16[2,4,120,128]{3,2,0,1:T(8,128)(2,1)S(1)} %pad_maximum_fusion), channel_id=1, source_target_pairs={{0,128},{128,256},{256,384},{384,0},{1,129},{129,257},{257,385},{3... | collective-permute-start | bytes 737288 | tf_op jit(solution)/shard_map/ppermute | solution.py:243
  46.7 18.0 %collective-permute-start.3 = (bf16[2,4,120,128]{3,2,0,1:T(8,128)(2,1)S(1)}, bf16[2,4,120,128]{3,2,0,1:T(8,128)(2,1)S(1)}, u32[]{:S(2)}, u32[]{:S(2)}) collective-permute-start(bf16[2,4,120,128]{3,2,0,1:T(8,128)(2,1)S(1)} %pad_maximum_fusion.1), channel_id=1, source_target_pairs={{0,256},{128,384},{256,0},{384,128},{1,257},{129,385},{257,1},{385... | collective-permute-start | bytes 737288 | tf_op jit(solution)/shard_map/ppermute | solution.py:243
  51.1 14.4 %collective-permute-start.4 = (bf16[2,4,120,128]{3,2,1,0:T(8,128)(2,1)S(1)}, bf16[2,4,120,128]{3,2,1,0:T(8,128)(2,1)S(1)}, u32[]{:S(2)}, u32[]{:S(2)}) collective-permute-start(bf16[2,4,120,128]{3,2,1,0:T(8,128)(2,1)S(1)} %pad_maximum_fusion.2), channel_id=1, source_target_pairs={{0,384},{128,0},{256,128},{384,256},{1,385},{129,1},{257,129},{385... | collective-permute-start | bytes 737288 | tf_op jit(solution)/shard_map/ppermute | solution.py:243
  66.2 52.5 %collective-permute-start.7 = (bf16[8,120,128]{2,1,0:T(8,128)(2,1)}, bf16[8,120,128]{2,1,0:T(8,128)(2,1)S(1)}, u32[]{:S(2)}, u32[]{:S(2)}) collective-permute-start(bf16[8,120,128]{2,1,0:T(8,128)(2,1)} %bitcast.35), channel_id=1, source_target_pairs={{0,96},{32,0},{64,32},{96,64},{1,97},{33,1},{65,33},{97,65},{2,98}... | collective-permute-start | bytes 737288 | tf_op jit(solution)/shard_map/ppermute | solution.py:243
  73.5 45.2 %collective-permute-start.6 = (bf16[8,120,128]{2,1,0:T(8,128)(2,1)}, bf16[8,120,128]{2,1,0:T(8,128)(2,1)}, u32[]{:S(2)}, u32[]{:S(2)}) collective-permute-start(bf16[8,120,128]{2,1,0:T(8,128)(2,1)} %bitcast.30), channel_id=1, source_target_pairs={{0,64},{32,96},{64,0},{96,32},{1,65},{33,97},{65,1},{97,33},{2,66}... | collective-permute-start | bytes 737288 | tf_op jit(solution)/shard_map/ppermute | solution.py:243
  80.3 38.4 %collective-permute-start.5 = (bf16[8,120,128]{2,1,0:T(8,128)(2,1)}, bf16[8,120,128]{2,1,0:T(8,128)(2,1)}, u32[]{:S(2)}, u32[]{:S(2)}) collective-permute-start(bf16[8,120,128]{2,1,0:T(8,128)(2,1)} %bitcast.25), channel_id=1, source_target_pairs={{0,32},{32,64},{64,96},{96,0},{1,33},{33,65},{65,97},{97,1},{2,34}... | collective-permute-start | bytes 737288 | tf_op jit(solution)/shard_map/ppermute | solution.py:243
  87.6 1.2 copy-start.7
  88.8 1.0 copy-start.10
  90.9 1.0 copy-start.8
  92.9 4.4 %copy-start.11 = (bf16[1,512,512]{2,1,0:T(8,128)(2,1)S(1)}, bf16[1,512,512]{2,1,0:T(8,128)(2,1)}, u32[]{:S(2)}) copy-start(bf16[1,512,512]{2,1,0:T(8,128)(2,1)} %param.7) | copy-start | bytes 1572868
  92.9 17.8 %all-to-all-start.1 = ((f32[4,128,512]{2,1,0:T(8,128)}), f32[4,128,512]{2,1,0:T(8,128)}, u32[]{:S(2)}, u32[]{:S(2)}) async-start(f32[4,128,512]{2,1,0:T(8,128)} %bitcast.85), calls=%async_computation.1 | async-start | bytes 2097152 | tf_op jit(solution)/shard_map/all_to_all | solution.py:233
  97.3 1.2 copy-start.20
  101.5 3.9 %copy-start.4 = (f32[960,512]{1,0:T(8,128)}, f32[960,512]{1,0:T(8,128)S(1)}, u32[]{:S(2)}) copy-start(f32[960,512]{1,0:T(8,128)S(1)} %shard_map.88.back_ref) | copy-start | bytes 5898244
  101.6 17.2 %collective-permute-start.8 = (f32[8,1024]{1,0:T(8,128)S(1)}, f32[8,1024]{1,0:T(8,128)S(1)}, u32[]{:S(2)}, u32[]{:S(2)}) collective-permute-start(f32[8,1024]{1,0:T(8,128)S(1)} %get-tuple-element.33), channel_id=1, source_target_pairs={{16,0},{32,16},{48,32},{64,48},{80,64},{96,80},{112,96},{128,112},... | collective-permute-start | bytes 98312 | tf_op jit(solution)/shard_map/ppermute | solution.py:238
  106.3 11.7 %copy-start.18 = (bf16[16,32,32]{2,1,0:T(8,128)(2,1)S(1)}, bf16[16,32,32]{2,1,0:T(8,128)(2,1)}, u32[]{:S(2)}) copy-start(bf16[16,32,32]{2,1,0:T(8,128)(2,1)} %param.8) | copy-start | bytes 98308
  106.5 5.5 %copy-start.14 = (bf16[512,512]{1,0:T(8,128)(2,1)}, bf16[512,512]{1,0:T(8,128)(2,1)S(1)}, u32[]{:S(2)}) copy-start(bf16[512,512]{1,0:T(8,128)(2,1)S(1)} %shard_map.90.rear_ref) | copy-start | bytes 1572868
  112.0 6.7 %copy-start.23 = (f32[128,512]{1,0:T(8,128)}, f32[128,512]{1,0:T(8,128)S(1)}, u32[]{:S(2)}) copy-start(f32[128,512]{1,0:T(8,128)S(1)} %reduce_sum.9) | copy-start | bytes 786436
  112.7 6.0 %copy-start.13 = (bf16[512,512]{1,0:T(8,128)(2,1)S(1)}, bf16[512,512]{1,0:T(8,128)(2,1)}, u32[]{:S(2)}) copy-start(bf16[512,512]{1,0:T(8,128)(2,1)} %copy-done.12) | copy-start | bytes 1572868
  112.7 6.0 %copy-start.15 = (bf16[512,512]{1,0:T(8,128)(2,1)S(1)}, bf16[512,512]{1,0:T(8,128)(2,1)}, u32[]{:S(2)}) copy-start(bf16[512,512]{1,0:T(8,128)(2,1)} %copy-done.14) | copy-start | bytes 1572868
  112.7 21.8 %collective-permute-start.9 = (f32[2,1,32,512]{3,2,1,0:T(8,128)}, f32[2,1,32,512]{3,2,1,0:T(8,128)}, u32[]{:S(2)}, u32[]{:S(2)}) collective-permute-start(f32[2,1,32,512]{3,2,1,0:T(8,128)} %constant_dynamic-slice_fusion.1), channel_id=1, source_target_pairs={{0,1},{1,0},{2,3},{3,2},{4,5},{5,4},{6,7},{7,6},{8,9},{9,8},{10,11... | collective-permute-start | bytes 393224 | tf_op jit(solution)/shard_map/ppermute | solution.py:259
  121.5 25.0 %all-to-all-start.2 = ((f32[16,8,128]{2,1,0:T(8,128)}), f32[16,8,128]{2,1,0:T(8,128)S(1)}, u32[]{:S(2)}, u32[]{:S(2)}) async-start(f32[16,8,128]{2,1,0:T(8,128)} %bitcast.41), calls=%async_computation.2 | async-start | bytes 131072 | tf_op jit(solution)/shard_map/all_to_all | solution.py:233
  136.3 10.9 %collective-permute-start.10 = (f32[1,1,32,512]{3,2,1,0:T(8,128)}, f32[1,1,32,512]{3,2,1,0:T(8,128)S(1)}, u32[]{:S(2)}, u32[]{:S(2)}) collective-permute-start(f32[1,1,32,512]{3,2,1,0:T(8,128)} %constant_dynamic-slice_fusion), channel_id=1, source_target_pairs={{0,2},{1,3},{2,0},{3,1},{4,6},{5,7},{6,4},{7,5},{8,10},{9,11},{10,... | collective-permute-start | bytes 196616 | tf_op jit(solution)/shard_map/ppermute | solution.py:259
  140.4 1.5 %copy-start.5 = (f32[960,512]{1,0:T(8,128)S(1)}, f32[960,512]{1,0:T(8,128)}, u32[]{:S(2)}) copy-start(f32[960,512]{1,0:T(8,128)} %copy-done.4) | copy-start | bytes 5898244
  (9 other events, 7.5 us)

commit v6 on v5

--- a/solution.py
+++ b/solution.py
@@ -251,12 +251,12 @@
     return [jnp.stack([part[:, step] for part in both]).reshape(8, 120, LANES) for step in range(4)]
 
 
-def halves_met(part, axis, apart, along):
+def halves_met(part, axis, apart, along, sent=F32):
     size = part.shape[along] // 2
     upper = lax.axis_index(axis) // apart % 2
     mine = lax.dynamic_slice_in_dim(part, upper * size, size, along)
     other = lax.dynamic_slice_in_dim(part, (1 - upper) * size, size, along)
-    return mine, lax.ppermute(other, axis, [(s, s ^ apart) for s in range(lax.axis_size(axis))])
+    return mine, lax.ppermute(other.astype(sent), axis, [(s, s ^ apart) for s in range(lax.axis_size(axis))])
 
 
 def total_kernel(in_ref, out_ref):
@@ -299,7 +299,7 @@
     (conv_back,) = call(dconv_kernel, [((960, 512), F32)], flops=1 << 35)(dfirst, taps, left)
     left_sum = jnp.sum(exchange(left_part.reshape(4, 128, 512), "x"), 0)
     left_sum = lax.optimization_barrier((left_sum, conv_back))[0]
-    kept, met = halves_met(left_sum.reshape(2, 2, 32, 512), "zl", 1, 1)
+    kept, met = halves_met(left_sum.reshape(2, 2, 32, 512), "zl", 1, 1, BF16)
     late = lax.optimization_barrier((x, cot, right, dedge))
     (wide,) = call(wide_kernel, [((512, 512), BF16)], flops=1 << 31)(late[2])
     (front,) = call(front_gate_kernel, [((512, 512), BF16)], flops=1 << 31)(*late[:2])

time: 149 us -> 149 us (level)
  no operation moved by 1% of the time
where the time goes in v6:
time: 149 us; the launch traced here: 148 us
  starting transfers between devices  89.4 us (60%)
  Pallas kernels  20 us (13%)
  local copies, waits for them, and re-layouts  16 us (11%)
  waiting for transfers between devices  16 us (11%)
  other arithmetic  5.35 us (4%)
    all_to_all x3, starting transfers between devices, exchange(): return lax.all_to_all(value, axes, split_axis=0, concat_axis=0, tiled=True)  33.3 us
    ppermute x7, starting transfers between devices, ahead(): lax.ppermute(value, axis, [(s, (s + step) % count) for s in range(count)])  32.7 us
    ppermute x2, starting transfers between devices, along_seq(): return lax.ppermute(value, SEQ, pairs)  14 us
    unnamed x55, local copies, waits for them, and re-layouts  13.5 us
    ppermute x7, waiting for transfers between devices, ahead(): lax.ppermute(value, axis, [(s, (s + step) % count) for s in range(count)])  11.9 us
    ppermute x2, starting transfers between devices, halves_met(): lax.ppermute(other.astype(sent), axis, [(s, s ^ apart) for s in range(lax...  9.39 us
    pallas_call x1, Pallas kernels, shards(): call(conv_kernel, [((1024, 512), BF16), part, part], scratch=[pltpu.VMEM(...  5.28 us
    pallas_call x1, Pallas kernels, shards(): call(end_kernel, [((960, 512), BF16), ((960, 512), BF16)], scratch=scratc...  4.49 us
  transfers between devices with their start and end apart: 14, of which 5 were waited for; matrix products, arithmetic and copies ran while one was open for 5% of the time, Pallas kernels for 13%

profile of v6, /device:TPU:1, one launch (start us, length us, event | category | flops | bytes accessed | tf_op | source)
XLA Modules:
  0.0 148.0 jit_solution(15000579254457166416)
XLA Ops:
  0.6 1.2 copy-done
  2.0 10.4 %collective-permute-start = (bf16[16,960]{1,0:T(8,128)(2,1)S(1)}, bf16[16,960]{1,0:T(8,128)(2,1)S(1)}, u32[]{:S(2)}, u32[]{:S(2)}) collective-permute-start(bf16[16,960]{1,0:T(8,128)(2,1)S(1)} %shard_map.85), channel_id=1, source_target_pairs={{0,16},{16,32},{32,48},{48,64},{64,80},{80,96},{96,112},{112,128},... | collective-permute-start | bytes 92168 | tf_op jit(solution)/shard_map/ppermute | solution.py:238
  12.4 1.6 %shard_map.84 = bf16[32,120,128]{2,1,0:T(8,128)(2,1)S(1)} custom-call(bf16[960,512]{1,0:T(8,128)(2,1)S(1)} %bitcast.74, bf16[960,512]{1,0:T(8,128)(2,1)S(1)} %bitcast.79, bf16[512,32]{1,0:T(8,128)(2,1)S(1)} %bitcast.92), custom_call_target="tpu_custom_call" | custom-call | flops 536870912 | bytes 4194304 | tf_op jit(solution)/shard_map/pallas_call | solution.py:280
  15.6 15.7 %all-to-all-start = ((bf16[32,120,128]{2,1,0:T(8,128)(2,1)}), bf16[32,120,128]{2,1,0:T(8,128)(2,1)S(1)}, u32[]{:S(2)}, u32[]{:S(2)}) async-start(bf16[32,120,128]{2,1,0:T(8,128)(2,1)} %copy-done.3), calls=%async_computation | async-start | bytes 1966080 | tf_op jit(solution)/shard_map/all_to_all | solution.py:233
  32.3 5.3 %shard_map.86 = (bf16[1024,512]{1,0:T(8,128)(2,1)S(1)}, bf16[16,120,128]{2,1,0:T(8,128)(2,1)S(1)}, bf16[16,120,128]{2,1,0:T(8,128)(2,1)}) custom-call(s32[3]{0:T(128)S(1)} %pad_add_fusion.place_ref, bf16[960,512]{1,0:T(8,128)(2,1)S(1)} %bitcast.75, bf16[16,960]{1,0:T(8,128)(2,1)S(1)} %copy-done.22, f32[96,4]{1,0:T(8,128)S(1)} %bitcast.89, ...), custom_call_target="tpu_custom_call" | custom-call | flops 536870912 | bytes 4194304 | tf_op jit(solution)/shard_map/pallas_call | solution.py:285
  37.6 1.0 copy-done.6
  39.4 2.1 %collective-permute-start.1 = (bf16[16,120,128]{2,1,0:T(8,128)(2,1)}, bf16[16,120,128]{2,1,0:T(8,128)(2,1)S(1)}, u32[]{:S(2)}, u32[]{:S(2)}) collective-permute-start(bf16[16,120,128]{2,1,0:T(8,128)(2,1)} %get-tuple-element.30), channel_id=1, source_target_pairs={{0,16},{16,0},{1,17},{17,1},{2,18},{18,2},{3,19},{19,3},{4,20},{20... | collective-permute-start | bytes 1474568 | tf_op jit(solution)/shard_map/ppermute | solution.py:243
  41.6 1.1 slice_bitcast_fusion.7
  43.4 3.3 %collective-permute-start.2 = (bf16[2,4,120,128]{3,2,0,1:T(8,128)(2,1)S(1)}, bf16[2,4,120,128]{3,2,0,1:T(8,128)(2,1)S(1)}, u32[]{:S(2)}, u32[]{:S(2)}) collective-permute-start(bf16[2,4,120,128]{3,2,0,1:T(8,128)(2,1)S(1)} %pad_maximum_fusion), channel_id=1, source_target_pairs={{0,128},{128,256},{256,384},{384,0},{1,129},{129,257},{257,385},{3... | collective-permute-start | bytes 737288 | tf_op jit(solution)/shard_map/ppermute | solution.py:243
  46.7 4.3 %collective-permute-start.3 = (bf16[2,4,120,128]{3,2,0,1:T(8,128)(2,1)S(1)}, bf16[2,4,120,128]{3,2,0,1:T(8,128)(2,1)S(1)}, u32[]{:S(2)}, u32[]{:S(2)}) collective-permute-start(bf16[2,4,120,128]{3,2,0,1:T(8,128)(2,1)S(1)} %pad_maximum_fusion.1), channel_id=1, source_target_pairs={{0,256},{128,384},{256,0},{384,128},{1,257},{129,385},{257,1},{385... | collective-permute-start | bytes 737288 | tf_op jit(solution)/shard_map/ppermute | solution.py:243
  51.1 3.1 %collective-permute-start.4 = (bf16[2,4,120,128]{3,2,1,0:T(8,128)(2,1)S(1)}, bf16[2,4,120,128]{3,2,1,0:T(8,128)(2,1)S(1)}, u32[]{:S(2)}, u32[]{:S(2)}) collective-permute-start(bf16[2,4,120,128]{3,2,1,0:T(8,128)(2,1)S(1)} %pad_maximum_fusion.2), channel_id=1, source_target_pairs={{0,384},{128,0},{256,128},{384,256},{1,385},{129,1},{257,129},{385... | collective-permute-start | bytes 737288 | tf_op jit(solution)/shard_map/ppermute | solution.py:243
  54.2 3.2 %collective-permute-done.2 = bf16[2,4,120,128]{3,2,0,1:T(8,128)(2,1)S(1)} collective-permute-done((bf16[2,4,120,128]{3,2,0,1:T(8,128)(2,1)S(1)}, bf16[2,4,120,128]{3,2,0,1:T(8,128)(2,1)S(1)}, u32[]{:S(2)}, u32[]{:S(2)}) %collective-permute-start.2) | collective-permute-done | bytes 245792 | tf_op jit(solution)/shard_map/ppermute | solution.py:243
  57.4 7.3 %collective-permute-done.3 = bf16[2,4,120,128]{3,2,0,1:T(8,128)(2,1)S(1)} collective-permute-done((bf16[2,4,120,128]{3,2,0,1:T(8,128)(2,1)S(1)}, bf16[2,4,120,128]{3,2,0,1:T(8,128)(2,1)S(1)}, u32[]{:S(2)}, u32[]{:S(2)}) %collective-permute-start.3) | collective-permute-done | bytes 245792 | tf_op jit(solution)/shard_map/ppermute | solution.py:243
  66.2 6.6 %collective-permute-start.7 = (bf16[8,120,128]{2,1,0:T(8,128)(2,1)}, bf16[8,120,128]{2,1,0:T(8,128)(2,1)S(1)}, u32[]{:S(2)}, u32[]{:S(2)}) collective-permute-start(bf16[8,120,128]{2,1,0:T(8,128)(2,1)} %bitcast.35), channel_id=1, source_target_pairs={{0,96},{32,0},{64,32},{96,64},{1,97},{33,1},{65,33},{97,65},{2,98}... | collective-permute-start | bytes 737288 | tf_op jit(solution)/shard_map/ppermute | solution.py:243
  73.5 6.0 %collective-permute-start.6 = (bf16[8,120,128]{2,1,0:T(8,128)(2,1)}, bf16[8,120,128]{2,1,0:T(8,128)(2,1)}, u32[]{:S(2)}, u32[]{:S(2)}) collective-permute-start(bf16[8,120,128]{2,1,0:T(8,128)(2,1)} %bitcast.30), channel_id=1, source_target_pairs={{0,64},{32,96},{64,0},{96,32},{1,65},{33,97},{65,1},{97,33},{2,66}... | collective-permute-start | bytes 737288 | tf_op jit(solution)/shard_map/ppermute | solution.py:243
  80.3 7.3 %collective-permute-start.5 = (bf16[8,120,128]{2,1,0:T(8,128)(2,1)}, bf16[8,120,128]{2,1,0:T(8,128)(2,1)}, u32[]{:S(2)}, u32[]{:S(2)}) collective-permute-start(bf16[8,120,128]{2,1,0:T(8,128)(2,1)} %bitcast.25), channel_id=1, source_target_pairs={{0,32},{32,64},{64,96},{96,0},{1,33},{33,65},{65,97},{97,1},{2,34}... | collective-permute-start | bytes 737288 | tf_op jit(solution)/shard_map/ppermute | solution.py:243
  87.6 1.2 copy-done.7
  88.8 1.0 copy-done.10
  89.9 1.0 shard_map.87
  90.9 1.0 copy-done.8
  92.9 4.4 %all-to-all-start.1 = ((f32[4,128,512]{2,1,0:T(8,128)}), f32[4,128,512]{2,1,0:T(8,128)}, u32[]{:S(2)}, u32[]{:S(2)}) async-start(f32[4,128,512]{2,1,0:T(8,128)} %bitcast.85), calls=%async_computation.1 | async-start | bytes 2097152 | tf_op jit(solution)/shard_map/all_to_all | solution.py:233
  97.3 1.2 copy-done.20
  98.5 3.0 %shard_map.88.back_ref = f32[960,512]{1,0:T(8,128)S(1)} custom-call(bf16[512,1024]{1,0:T(8,128)(2,1)S(1)} %copy-done.20, f32[96,4]{1,0:T(8,128)S(1)} %bitcast.90, bf16[512,512]{1,0:T(8,128)(2,1)S(1)} %bitcast.88), custom_call_target="tpu_custom_call" | custom-call | flops 34359738368 | bytes 4194304 | tf_op jit(solution)/shard_map/pallas_call | solution.py:299
  101.6 3.7 %collective-permute-start.8 = (f32[8,1024]{1,0:T(8,128)S(1)}, f32[8,1024]{1,0:T(8,128)S(1)}, u32[]{:S(2)}, u32[]{:S(2)}) collective-permute-start(f32[8,1024]{1,0:T(8,128)S(1)} %get-tuple-element.33), channel_id=1, source_target_pairs={{16,0},{32,16},{48,32},{64,48},{80,64},{96,80},{112,96},{128,112},... | collective-permute-start | bytes 98312 | tf_op jit(solution)/shard_map/ppermute | solution.py:238
  106.5 4.2 %all-to-all-done.1 = f32[4,128,512]{2,1,0:T(8,128)} async-done(((f32[4,128,512]{2,1,0:T(8,128)}), f32[4,128,512]{2,1,0:T(8,128)}, u32[]{:S(2)}, u32[]{:S(2)}) %all-to-all-start.1) | async-done | bytes 1048608 | tf_op jit(solution)/shard_map/all_to_all | solution.py:233
  110.7 1.3 reduce_sum.9
  112.7 5.2 %collective-permute-start.9 = (bf16[2,1,32,512]{3,2,1,0:T(8,128)(2,1)}, bf16[2,1,32,512]{3,2,1,0:T(8,128)(2,1)}, u32[]{:S(2)}, u32[]{:S(2)}) collective-permute-start(bf16[2,1,32,512]{3,2,1,0:T(8,128)(2,1)} %dynamic-slice_convert_fusion), channel_id=1, source_target_pairs={{0,1},{1,0},{2,3},{3,2},{4,5},{5,4},{6,7},{7,6},{8,9},{9,8},{10,11... | collective-permute-start | bytes 196616 | tf_op jit(solution)/shard_map/ppermute | solution.py:259
  118.7 2.7 %shard_map.93 = f32[128,128]{1,0:T(8,128)} custom-call(s32[3]{0:T(128)S(1)} %pad_add_fusion.place_ref, bf16[8,120,128]{2,1,0:T(8,128)(2,1)S(1)} %bitcast.83, bf16[8,120,128]{2,1,0:T(8,128)(2,1)} %collective-permute-done.5.in1_ref, bf16[8,120,128]{2,1,0:T(8,128)(2,1)} %collective-permute-done.6.in2_ref, ...), custom_call_target="tpu_custom_call" | custom-call | flops 536870912 | bytes 4194304 | tf_op jit(solution)/shard_map/pallas_call | solution.py:312
  121.4 13.2 %all-to-all-start.2 = ((f32[16,8,128]{2,1,0:T(8,128)}), f32[16,8,128]{2,1,0:T(8,128)S(1)}, u32[]{:S(2)}, u32[]{:S(2)}) async-start(f32[16,8,128]{2,1,0:T(8,128)} %bitcast.41), calls=%async_computation.2 | async-start | bytes 131072 | tf_op jit(solution)/shard_map/all_to_all | solution.py:233
  136.3 4.2 %collective-permute-start.10 = (f32[1,1,32,512]{3,2,1,0:T(8,128)}, f32[1,1,32,512]{3,2,1,0:T(8,128)S(1)}, u32[]{:S(2)}, u32[]{:S(2)}) collective-permute-start(f32[1,1,32,512]{3,2,1,0:T(8,128)} %constant_dynamic-slice_fusion), channel_id=1, source_target_pairs={{0,2},{1,3},{2,0},{3,1},{4,6},{5,7},{6,4},{7,5},{8,10},{9,11},{10,... | collective-permute-start | bytes 196616 | tf_op jit(solution)/shard_map/ppermute | solution.py:259
  140.4 1.5 %copy-done.5 = f32[960,512]{1,0:T(8,128)S(1)} copy-done((f32[960,512]{1,0:T(8,128)S(1)}, f32[960,512]{1,0:T(8,128)}, u32[]{:S(2)}) %copy-start.5) | copy-done | bytes 1966104
  142.0 4.5 %shard_map.92 = (bf16[960,512]{1,0:T(8,128)(2,1)}, bf16[960,512]{1,0:T(8,128)(2,1)}) custom-call(s32[3]{0:T(128)S(1)} %pad_add_fusion.place_ref, bf16[8,120,128]{2,1,0:T(8,128)(2,1)S(1)} %bitcast.84, bf16[8,120,128]{2,1,0:T(8,128)(2,1)} %collective-permute-done.5.in1_ref, bf16[8,120,128]{2,1,0:T(8,128)(2,1)} %collective-permute-done.6.in2_ref, ...), custom_call_target="tpu_custom_call" | custom-call | flops 536870912 | bytes 4194304 | tf_op jit(solution)/shard_map/pallas_call | solution.py:318
  (81 shorter events, 14.1 us)
Async XLA Ops:
  0.6 1.2 copy-start
  1.8 10.5 %copy-start.2 = (bf16[10,96,512]{2,1,0:T(8,128)(2,1)S(1)}, bf16[10,96,512]{2,1,0:T(8,128)(2,1)}, u32[]{:S(2)}) copy-start(bf16[10,96,512]{2,1,0:T(8,128)(2,1)} %param.9) | copy-start | bytes 2949124
  1.8 10.6 %copy-start.17 = (bf16[16,32,32]{2,1,0:T(8,128)(2,1)S(1)}, bf16[16,32,32]{2,1,0:T(8,128)(2,1)}, u32[]{:S(2)}) copy-start(bf16[16,32,32]{2,1,0:T(8,128)(2,1)} %param.8) | copy-start | bytes 98308
  2.0 12.9 %collective-permute-start = (bf16[16,960]{1,0:T(8,128)(2,1)S(1)}, bf16[16,960]{1,0:T(8,128)(2,1)S(1)}, u32[]{:S(2)}, u32[]{:S(2)}) collective-permute-start(bf16[16,960]{1,0:T(8,128)(2,1)S(1)} %shard_map.85), channel_id=1, source_target_pairs={{0,16},{16,32},{32,48},{48,64},{64,80},{80,96},{96,112},{112,128},... | collective-permute-start | bytes 92168 | tf_op jit(solution)/shard_map/ppermute | solution.py:238
  12.4 18.9 %copy-start.26 = (f32[4,96]{1,0:T(4,128)S(1)}, f32[4,96]{1,0:T(4,128)}, u32[]{:S(2)}) copy-start(f32[4,96]{1,0:T(4,128)} %param.6) | copy-start | bytes 4612
  12.4 19.1 %copy-start.1 = (bf16[10,96,512]{2,1,0:T(8,128)(2,1)S(1)}, bf16[10,96,512]{2,1,0:T(8,128)(2,1)}, u32[]{:S(2)}) copy-start(bf16[10,96,512]{2,1,0:T(8,128)(2,1)} %param.5) | copy-start | bytes 2949124
  12.4 19.1 %copy-start.9 = (bf16[1,512,512]{2,1,0:T(8,128)(2,1)S(1)}, bf16[1,512,512]{2,1,0:T(8,128)(2,1)}, u32[]{:S(2)}) copy-start(bf16[1,512,512]{2,1,0:T(8,128)(2,1)} %param.7) | copy-start | bytes 1572868
  15.6 72.0 %all-to-all-start = ((bf16[32,120,128]{2,1,0:T(8,128)(2,1)}), bf16[32,120,128]{2,1,0:T(8,128)(2,1)S(1)}, u32[]{:S(2)}, u32[]{:S(2)}) async-start(bf16[32,120,128]{2,1,0:T(8,128)(2,1)} %copy-done.3), calls=%async_computation | async-start | bytes 1966080 | tf_op jit(solution)/shard_map/all_to_all | solution.py:233
  39.4 4.0 %collective-permute-start.1 = (bf16[16,120,128]{2,1,0:T(8,128)(2,1)}, bf16[16,120,128]{2,1,0:T(8,128)(2,1)S(1)}, u32[]{:S(2)}, u32[]{:S(2)}) collective-permute-start(bf16[16,120,128]{2,1,0:T(8,128)(2,1)} %get-tuple-element.30), channel_id=1, source_target_pairs={{0,16},{16,0},{1,17},{17,1},{2,18},{18,2},{3,19},{19,3},{4,20},{20... | collective-permute-start | bytes 1474568 | tf_op jit(solution)/shard_map/ppermute | solution.py:243
  43.4 14.0 %collective-permute-start.2 = (bf16[2,4,120,128]{3,2,0,1:T(8,128)(2,1)S(1)}, bf16[2,4,120,128]{3,2,0,1:T(8,128)(2,1)S(1)}, u32[]{:S(2)}, u32[]{:S(2)}) collective-permute-start(bf16[2,4,120,128]{3,2,0,1:T(8,128)(2,1)S(1)} %pad_maximum_fusion), channel_id=1, source_target_pairs={{0,128},{128,256},{256,384},{384,0},{1,129},{129,257},{257,385},{3... | collective-permute-start | bytes 737288 | tf_op jit(solution)/shard_map/ppermute | solution.py:243
  46.7 18.0 %collective-permute-start.3 = (bf16[2,4,120,128]{3,2,0,1:T(8,128)(2,1)S(1)}, bf16[2,4,120,128]{3,2,0,1:T(8,128)(2,1)S(1)}, u32[]{:S(2)}, u32[]{:S(2)}) collective-permute-start(bf16[2,4,120,128]{3,2,0,1:T(8,128)(2,1)S(1)} %pad_maximum_fusion.1), channel_id=1, source_target_pairs={{0,256},{128,384},{256,0},{384,128},{1,257},{129,385},{257,1},{385... | collective-permute-start | bytes 737288 | tf_op jit(solution)/shard_map/ppermute | solution.py:243
  51.1 14.4 %collective-permute-start.4 = (bf16[2,4,120,128]{3,2,1,0:T(8,128)(2,1)S(1)}, bf16[2,4,120,128]{3,2,1,0:T(8,128)(2,1)S(1)}, u32[]{:S(2)}, u32[]{:S(2)}) collective-permute-start(bf16[2,4,120,128]{3,2,1,0:T(8,128)(2,1)S(1)} %pad_maximum_fusion.2), channel_id=1, source_target_pairs={{0,384},{128,0},{256,128},{384,256},{1,385},{129,1},{257,129},{385... | collective-permute-start | bytes 737288 | tf_op jit(solution)/shard_map/ppermute | solution.py:243
  66.2 52.4 %collective-permute-start.7 = (bf16[8,120,128]{2,1,0:T(8,128)(2,1)}, bf16[8,120,128]{2,1,0:T(8,128)(2,1)S(1)}, u32[]{:S(2)}, u32[]{:S(2)}) collective-permute-start(bf16[8,120,128]{2,1,0:T(8,128)(2,1)} %bitcast.35), channel_id=1, source_target_pairs={{0,96},{32,0},{64,32},{96,64},{1,97},{33,1},{65,33},{97,65},{2,98}... | collective-permute-start | bytes 737288 | tf_op jit(solution)/shard_map/ppermute | solution.py:243
  73.5 45.1 %collective-permute-start.6 = (bf16[8,120,128]{2,1,0:T(8,128)(2,1)}, bf16[8,120,128]{2,1,0:T(8,128)(2,1)}, u32[]{:S(2)}, u32[]{:S(2)}) collective-permute-start(bf16[8,120,128]{2,1,0:T(8,128)(2,1)} %bitcast.30), channel_id=1, source_target_pairs={{0,64},{32,96},{64,0},{96,32},{1,65},{33,97},{65,1},{97,33},{2,66}... | collective-permute-start | bytes 737288 | tf_op jit(solution)/shard_map/ppermute | solution.py:243
  80.3 38.4 %collective-permute-start.5 = (bf16[8,120,128]{2,1,0:T(8,128)(2,1)}, bf16[8,120,128]{2,1,0:T(8,128)(2,1)}, u32[]{:S(2)}, u32[]{:S(2)}) collective-permute-start(bf16[8,120,128]{2,1,0:T(8,128)(2,1)} %bitcast.25), channel_id=1, source_target_pairs={{0,32},{32,64},{64,96},{96,0},{1,33},{33,65},{65,97},{97,1},{2,34}... | collective-permute-start | bytes 737288 | tf_op jit(solution)/shard_map/ppermute | solution.py:243
  87.6 1.2 copy-start.7
  88.8 1.0 copy-start.10
  90.9 1.0 copy-start.8
  92.9 4.4 %copy-start.11 = (bf16[1,512,512]{2,1,0:T(8,128)(2,1)S(1)}, bf16[1,512,512]{2,1,0:T(8,128)(2,1)}, u32[]{:S(2)}) copy-start(bf16[1,512,512]{2,1,0:T(8,128)(2,1)} %param.7) | copy-start | bytes 1572868
  92.9 17.8 %all-to-all-start.1 = ((f32[4,128,512]{2,1,0:T(8,128)}), f32[4,128,512]{2,1,0:T(8,128)}, u32[]{:S(2)}, u32[]{:S(2)}) async-start(f32[4,128,512]{2,1,0:T(8,128)} %bitcast.85), calls=%async_computation.1 | async-start | bytes 2097152 | tf_op jit(solution)/shard_map/all_to_all | solution.py:233
  97.3 1.2 copy-start.20
  101.5 3.9 %copy-start.4 = (f32[960,512]{1,0:T(8,128)}, f32[960,512]{1,0:T(8,128)S(1)}, u32[]{:S(2)}) copy-start(f32[960,512]{1,0:T(8,128)S(1)} %shard_map.88.back_ref) | copy-start | bytes 5898244
  101.6 17.1 %collective-permute-start.8 = (f32[8,1024]{1,0:T(8,128)S(1)}, f32[8,1024]{1,0:T(8,128)S(1)}, u32[]{:S(2)}, u32[]{:S(2)}) collective-permute-start(f32[8,1024]{1,0:T(8,128)S(1)} %get-tuple-element.33), channel_id=1, source_target_pairs={{16,0},{32,16},{48,32},{64,48},{80,64},{96,80},{112,96},{128,112},... | collective-permute-start | bytes 98312 | tf_op jit(solution)/shard_map/ppermute | solution.py:238
  106.3 11.7 %copy-start.18 = (bf16[16,32,32]{2,1,0:T(8,128)(2,1)S(1)}, bf16[16,32,32]{2,1,0:T(8,128)(2,1)}, u32[]{:S(2)}) copy-start(bf16[16,32,32]{2,1,0:T(8,128)(2,1)} %param.8) | copy-start | bytes 98308
  106.5 5.5 %copy-start.14 = (bf16[512,512]{1,0:T(8,128)(2,1)}, bf16[512,512]{1,0:T(8,128)(2,1)S(1)}, u32[]{:S(2)}) copy-start(bf16[512,512]{1,0:T(8,128)(2,1)S(1)} %shard_map.90.rear_ref) | copy-start | bytes 1572868
  112.0 6.7 %copy-start.23 = (f32[128,512]{1,0:T(8,128)}, f32[128,512]{1,0:T(8,128)S(1)}, u32[]{:S(2)}) copy-start(f32[128,512]{1,0:T(8,128)S(1)} %reduce_sum.9) | copy-start | bytes 786436
  112.7 6.0 %copy-start.13 = (bf16[512,512]{1,0:T(8,128)(2,1)S(1)}, bf16[512,512]{1,0:T(8,128)(2,1)}, u32[]{:S(2)}) copy-start(bf16[512,512]{1,0:T(8,128)(2,1)} %copy-done.12) | copy-start | bytes 1572868
  112.7 6.0 %copy-start.15 = (bf16[512,512]{1,0:T(8,128)(2,1)S(1)}, bf16[512,512]{1,0:T(8,128)(2,1)}, u32[]{:S(2)}) copy-start(bf16[512,512]{1,0:T(8,128)(2,1)} %copy-done.14) | copy-start | bytes 1572868
  112.7 21.9 %collective-permute-start.9 = (bf16[2,1,32,512]{3,2,1,0:T(8,128)(2,1)}, bf16[2,1,32,512]{3,2,1,0:T(8,128)(2,1)}, u32[]{:S(2)}, u32[]{:S(2)}) collective-permute-start(bf16[2,1,32,512]{3,2,1,0:T(8,128)(2,1)} %dynamic-slice_convert_fusion), channel_id=1, source_target_pairs={{0,1},{1,0},{2,3},{3,2},{4,5},{5,4},{6,7},{7,6},{8,9},{9,8},{10,11... | collective-permute-start | bytes 196616 | tf_op jit(solution)/shard_map/ppermute | solution.py:259
  121.4 25.0 %all-to-all-start.2 = ((f32[16,8,128]{2,1,0:T(8,128)}), f32[16,8,128]{2,1,0:T(8,128)S(1)}, u32[]{:S(2)}, u32[]{:S(2)}) async-start(f32[16,8,128]{2,1,0:T(8,128)} %bitcast.41), calls=%async_computation.2 | async-start | bytes 131072 | tf_op jit(solution)/shard_map/all_to_all | solution.py:233
  136.3 10.9 %collective-permute-start.10 = (f32[1,1,32,512]{3,2,1,0:T(8,128)}, f32[1,1,32,512]{3,2,1,0:T(8,128)S(1)}, u32[]{:S(2)}, u32[]{:S(2)}) collective-permute-start(f32[1,1,32,512]{3,2,1,0:T(8,128)} %constant_dynamic-slice_fusion), channel_id=1, source_target_pairs={{0,2},{1,3},{2,0},{3,1},{4,6},{5,7},{6,4},{7,5},{8,10},{9,11},{10,... | collective-permute-start | bytes 196616 | tf_op jit(solution)/shard_map/ppermute | solution.py:259
  140.4 1.5 %copy-start.5 = (f32[960,512]{1,0:T(8,128)S(1)}, f32[960,512]{1,0:T(8,128)}, u32[]{:S(2)}) copy-start(f32[960,512]{1,0:T(8,128)} %copy-done.4) | copy-start | bytes 5898244
  (9 other events, 7.5 us)
